TPU v7x, 256 devices: a whole 4x4x8 slice. The times are simulated.
256 devices in a mesh: slab: 8 (over x, y_hi), pencil: 32 (over z, y_lo, core).
Axes of the slice: x: 4, y: 4 (y_hi: 2, y_lo: 2; y = y_hi * 2 + y_lo), z: 8, core: 2. Of those that a mesh axis runs over, the one named last changes fastest.
Arguments:
- thermal_deviation: float32 [96, 512, 1024], P('slab', 'pencil'), may hold values from -6 to 6
- downstream_speed: bfloat16 [96, 512, 1024], P('slab', 'pencil'), may hold values from -4 to 4
- crossflow_speed: bfloat16 [96, 512, 1024], P('slab', 'pencil'), may hold values from -4 to 4
- wallward_speed: bfloat16 [96, 512, 1024], P('slab', 'pencil'), may hold values from -4 to 4
- downstream_solver_matrix: float32 [1024, 1024], replicated, may hold values from 0 to 1
- wallward_solver_matrices: float32 [2, 512, 512], replicated, may hold values from 0 to 1
- wall_segments: int32 [16], replicated, may hold values from 1 to 128, 1024 in all
Outputs:
- updated: float32 [96, 512, 1024], P('slab', 'pencil')
Inputs may be any that keep to these rules, and one draw needn't show every extreme that they name: `wall_segments`: the 16 patches alternate between conducting and insulating, the first conducting; their lengths sum to 1024 and the longest is exactly 128.
All inputs are finite; a program needn't handle non-finite values.
Results may differ from a plain program's by a relative error of at most 0.0003.
Values sent between devices are 32-bit elements; how exact they have to be, the bound alone decides.
No kernel may reach another device: no remote copies, remote signals or barrier semaphores. Data moves between devices by JAX's collectives and lax.ppermute only.
A program may use at most 128 MiB of HBM per device.

v0:
```python
import jax
import jax.numpy as jnp
from jax import lax
from jax.experimental import pallas as pl
from jax.experimental.pallas import tpu as pltpu
from jax.sharding import PartitionSpec as P

TRANSPORT_PART = 0.25
CONDUCTION_PART = 0.2
LANES = 128
VMEM = pl.BlockSpec(memory_space=pltpu.VMEM)
SMEM = pl.BlockSpec(memory_space=pltpu.SMEM)


def metric_of(levels, extent):
    return 0.5 / (1.0 + jnp.sin(jnp.pi * (levels + 0.5) / extent))


def halves(wide):
    high = wide.astype(jnp.bfloat16)
    return high, (wide - high.astype(jnp.float32)).astype(jnp.bfloat16)


def split_kernel(a_ref, w_ref, ah_ref, al_ref, wh_ref, wl_ref):
    ah_ref[...], al_ref[...] = halves(a_ref[...])
    wh_ref[...], wl_ref[...] = halves(w_ref[...])


def split_matrices(a, w):
    steps = 8
    n, k = a.shape[0], w.shape[1]
    a_spec = pl.BlockSpec((n // steps, n), lambda i: (i, 0))
    w_spec = pl.BlockSpec((2, k // steps, k), lambda i: (0, i, 0))
    a16 = jax.ShapeDtypeStruct(a.shape, jnp.bfloat16)
    w16 = jax.ShapeDtypeStruct(w.shape, jnp.bfloat16)
    return pl.pallas_call(
        split_kernel,
        grid=(steps,),
        in_specs=[a_spec, w_spec],
        out_specs=[a_spec, a_spec, w_spec, w_spec],
        out_shape=[a16, a16, w16, w16],
        compiler_params=pltpu.CompilerParams(vmem_limit_bytes=16 * 2**20),
        cost_estimate=pl.CostEstimate(
            flops=4 * (a.size + w.size), bytes_accessed=8 * (a.size + w.size), transcendentals=0
        ),
        name="split_matrices",
    )(a, w)


def row_kernel(t_ref, u_ref, v_ref, w_ref, yb_ref, ya_ref, zb_ref, za_ref, g_ref, ah_ref, al_ref, out_ref, rh, rl):
    planes, rows, nx = t_ref.shape
    metric = jnp.concatenate([g_ref[...]] * (nx // LANES), axis=1)
    level = lax.broadcasted_iota(jnp.int32, (rows, nx), 0)
    for y in range(planes):
        t = t_ref[y]
        ahead = t_ref[y + 1] if y + 1 < planes else ya_ref[...]
        behind = t_ref[y - 1] if y else yb_ref[...]
        east = pltpu.roll(t, nx - 1, 1)
        west = pltpu.roll(t, 1, 1)
        above = jnp.where(level == rows - 1, za_ref[y : y + 1, :], pltpu.roll(t, rows - 1, 0))
        below = jnp.where(level == 0, zb_ref[y : y + 1, :], pltpu.roll(t, 1, 0))
        u = u_ref[y].astype(jnp.float32)
        v = v_ref[y].astype(jnp.float32)
        w = w_ref[y].astype(jnp.float32)
        carried = 0.5 * u * (east - west) + 0.5 * v * (ahead - behind) + w * metric * (above - below)
        conducted = (
            (ahead - 2.0 * t + behind)
            + 0.5 * (east - 2.0 * t + west)
            + 0.5 * metric * (above - 2.0 * t + below)
        )
        side = t - TRANSPORT_PART * carried + CONDUCTION_PART * conducted
        rh[y * rows : (y + 1) * rows, :], rl[y * rows : (y + 1) * rows, :] = halves(side)
    wide = 2 * LANES
    unit_rows = 3 * rows
    blocks = nx // LANES
    for c in range(nx // wide):
        ah = ah_ref[c * wide : (c + 1) * wide, :]
        al = al_ref[c * wide : (c + 1) * wide, :]

        def dot(x, m):
            return lax.dot_general(x, m, (((1,), (1,)), ((), ())), preferred_element_type=jnp.float32)

        solved = dot(rh[...], ah) + (dot(rh[...], al) + dot(rl[...], ah))
        for q in range(planes // 3):
            for h in range(2):
                piece = solved[q * unit_rows : (q + 1) * unit_rows, h * LANES : (h + 1) * LANES]
                out_ref[q * blocks + 2 * c + h] = piece.reshape(3, rows, LANES)


def row_solve(t, u, v, w, halos, metric, ah, al, groups):
    planes, rows, nx = t.shape
    return pl.pallas_call(
        row_kernel,
        in_specs=[VMEM] * 11,
        out_specs=VMEM,
        out_shape=jax.ShapeDtypeStruct((groups, 3, rows, LANES), jnp.float32),
        scratch_shapes=[pltpu.VMEM((planes * rows, nx), jnp.bfloat16)] * 2,
        compiler_params=pltpu.CompilerParams(vmem_limit_bytes=32 * 2**20),
        cost_estimate=pl.CostEstimate(
            flops=6 * planes * rows * nx * nx, bytes_accessed=8 * 2**20, transcendentals=0
        ),
        name="row_solve",
    )(t, u, v, w, *halos, metric, ah, al)


def column_kernel(first_ref, seg_ref, x_ref, wh_ref, wl_ref, out_ref):
    groups, units, rows, lanes = x_ref.shape
    column = lax.broadcasted_iota(jnp.int32, (1, lanes), 1) + first_ref[0]
    crossed = jnp.zeros((1, lanes), jnp.int32)
    end = jnp.int32(0)
    for s in range(seg_ref.shape[0]):
        end = end + seg_ref[s]
        crossed = crossed + jnp.where(column >= end, 1, 0)
    insulated = jnp.concatenate([crossed % 2] * units, axis=1) == 1
    extent = groups * rows
    lines = jnp.concatenate([x_ref[:, i].reshape(extent, lanes) for i in range(units)], axis=1)
    xh, xl = halves(lines)
    both = jnp.concatenate([xh, xl], axis=1)
    width = units * lanes

    def solve(c, lo, hi):
        d = jnp.dot(wh_ref[c, lo:hi, :], both, preferred_element_type=jnp.float32)
        e = jnp.dot(wl_ref[c, lo:hi, :], xh, preferred_element_type=jnp.float32)
        return d[:, :width] + (d[:, width:] + e)

    step = 128
    for k in range(0, extent, step):
        solved = jnp.where(insulated, solve(1, k, k + step), solve(0, k, k + step))
        for i in range(units):
            out_ref[k // rows : (k + step) // rows, i] = solved[:, i * lanes : (i + 1) * lanes].reshape(
                step // rows, rows, lanes
            )


def column_solve(first, segments, x, wh, wl):
    return pl.pallas_call(
        column_kernel,
        in_specs=[SMEM, SMEM, VMEM, VMEM, VMEM],
        out_specs=VMEM,
        out_shape=jax.ShapeDtypeStruct(x.shape, jnp.float32),
        compiler_params=pltpu.CompilerParams(vmem_limit_bytes=32 * 2**20),
        cost_estimate=pl.CostEstimate(
            flops=12 * wh.shape[1] * x.size, bytes_accessed=4 * 2**20, transcendentals=0
        ),
        name="column_solve",
    )(first, segments, x, wh, wl)


def place_kernel(x_ref, out_ref):
    groups = x_ref.shape[0]
    blocks = out_ref.shape[2] // LANES
    for p in range(groups):
        q, b = p // blocks, p % blocks
        out_ref[3 * q : 3 * q + 3, :, b * LANES : (b + 1) * LANES] = x_ref[p]


def place(x, shape):
    return pl.pallas_call(
        place_kernel,
        in_specs=[VMEM],
        out_specs=VMEM,
        out_shape=jax.ShapeDtypeStruct(shape, jnp.float32),
        compiler_params=pltpu.CompilerParams(vmem_limit_bytes=16 * 2**20),
        name="place",
    )(x)


def swapped(x):
    return lax.all_to_all(x, "pencil", split_axis=0, concat_axis=0, tiled=True)


def on_device(t, u, v, w, downstream_solver_matrix, wallward_solver_matrices, wall_segments):
    planes, rows, nx = t.shape
    slabs, groups = lax.axis_size("slab"), lax.axis_size("pencil")
    here = lax.axis_index("pencil")
    up = [(i, i + 1) for i in range(groups - 1)]
    down = [(i + 1, i) for i in range(groups - 1)]
    halos = (
        lax.ppermute(t[-1], "slab", [(i, (i + 1) % slabs) for i in range(slabs)]),
        lax.ppermute(t[0], "slab", [((i + 1) % slabs, i) for i in range(slabs)]),
        lax.ppermute(t[:, -1], "pencil", up),
        lax.ppermute(t[:, 0], "pencil", down),
    )
    levels = (here * rows + jnp.arange(rows, dtype=jnp.int32)).astype(jnp.float32)
    metric = jnp.broadcast_to(metric_of(levels, groups * rows)[:, None], (rows, LANES))
    ah, al, wh, wl = split_matrices(downstream_solver_matrix, wallward_solver_matrices)
    x = swapped(row_solve(t, u, v, w, halos, metric, ah, al, groups))
    first = (here % (nx // LANES) * LANES).astype(jnp.int32).reshape(1)
    x = swapped(column_solve(first, wall_segments, x, wh, wl))
    return place(x, t.shape)


def solution(mesh):
    field = P("slab", "pencil", None)
    return jax.shard_map(
        on_device,
        mesh=mesh,
        in_specs=(field, field, field, field, P(), P(), P()),
        out_specs=field,
        check_vma=False,
    )
```

profile of v0, /device:TPU:1, one launch (start us, length us, event | category | flops | bytes accessed | tf_op | source)
XLA Modules:
  0.0 89.5 jit_solution(12516022409839847429)
XLA Ops:
  0.0 1.2 %fusion = (f32[12,1,1024]{2,1,0:T(1,128)S(1)}, f32[12,1,1024]{2,1,0:T(1,128)S(1)}) fusion(f32[12,16,1024]{2,1,0:T(8,128)} %t_ref.1), kind=kLoop, calls=%fused_computation.5 | loop fusion | bytes 196608 | tf_op jit(solution)/shard_map/slice | solution.py:182
  1.2 4.6 %collective-permute-start.2 = (f32[12,1024]{1,0:T(8,128)S(1)}, f32[12,1024]{1,0:T(8,128)S(1)}, u32[]{:S(2)}, u32[]{:S(2)}) collective-permute-start(f32[12,1024]{1,0:T(8,128)S(1)} %bitcast.11), channel_id=1, source_target_pairs={{0,1},{1,2},{2,3},{3,4},{4,5},{5,6},{6,7},{7,8},{8,9},{9,10},{10,1... | collective-permute-start | bytes 147464 | tf_op jit(solution)/shard_map/ppermute | solution.py:181
  5.8 1.9 %collective-permute-start.3 = (f32[12,1024]{1,0:T(8,128)S(1)}, f32[12,1024]{1,0:T(8,128)S(1)}, u32[]{:S(2)}, u32[]{:S(2)}) collective-permute-start(f32[12,1024]{1,0:T(8,128)S(1)} %bitcast.12), channel_id=1, source_target_pairs={{1,0},{2,1},{3,2},{4,3},{5,4},{6,5},{7,6},{8,7},{9,8},{10,9},{11,1... | collective-permute-start | bytes 147464 | tf_op jit(solution)/shard_map/ppermute | solution.py:182
  7.8 0.9 slice_bitcast_fusion
  8.6 4.9 %collective-permute-start.1 = (f32[16,1024]{1,0:T(8,128)S(1)}, f32[16,1024]{1,0:T(8,128)S(1)}, u32[]{:S(2)}, u32[]{:S(2)}) collective-permute-start(f32[16,1024]{1,0:T(8,128)S(1)} %get-tuple-element.15), channel_id=1, source_target_pairs={{32,0},{64,32},{96,64},{128,96},{160,128},{192,160},{224,192},{0,2... | collective-permute-start | bytes 196616 | tf_op jit(solution)/shard_map/ppermute | solution.py:180
  13.5 0.0 collective-permute-start
  13.6 0.0 copy-start
  13.6 2.2 %copy-done = f32[1024,1024]{1,0:T(8,128)S(1)} copy-done((f32[1024,1024]{1,0:T(8,128)S(1)}, f32[1024,1024]{1,0:T(8,128)}, u32[]{:S(2)}) %copy-start) | copy-done | bytes 4194328
  15.8 1.6 %copy-done.1 = f32[2,512,512]{2,1,0:T(8,128)S(1)} copy-done((f32[2,512,512]{2,1,0:T(8,128)S(1)}, f32[2,512,512]{2,1,0:T(8,128)}, u32[]{:S(2)}) %copy-start.1) | copy-done | bytes 2097176
  17.4 1.5 %split_matrices.1 = (bf16[1024,1024]{1,0:T(8,128)(2,1)S(1)}, bf16[1024,1024]{1,0:T(8,128)(2,1)S(1)}, bf16[2,512,512]{2,1,0:T(8,128)(2,1)S(1)}, bf16[2,512,512]{2,1,0:T(8,128)(2,1)S(1)}) custom-call(f32[1024,1024]{1,0:T(8,128)S(1)} %copy-done, f32[2,512,512]{2,1,0:T(8,128)S(1)} %copy-done.1), custom_call_target="tpu_custom_call" | custom-call | flops 6291456 | bytes 12582912 | tf_op jit(solution)/shard_map/split_matrices/pallas_call | solution.py:36
  18.9 0.0 collective-permute-done.2.zb_ref
  18.9 0.0 collective-permute-done.3.za_ref
  18.9 0.0 collective-permute-done.1.ya_ref
  18.9 1.4 %collective-permute-done.yb_ref = f32[16,1024]{1,0:T(8,128)S(1)} collective-permute-done((f32[16,1024]{1,0:T(8,128)S(1)}, f32[16,1024]{1,0:T(8,128)S(1)}, u32[]{:S(2)}, u32[]{:S(2)}) %collective-permute-start) | collective-permute-done | bytes 65568 | tf_op jit(solution)/shard_map/ppermute | solution.py:179
  20.3 0.1 broadcast_in_dim.2.g_ref
  20.3 0.0 copy-done.2
  20.3 0.0 copy-done.3
  20.4 0.0 copy-start.6
  20.4 3.9 %row_solve.1 = f32[32,3,16,128]{3,2,1,0:T(8,128)} custom-call(f32[12,16,1024]{2,1,0:T(8,128)S(1)} %copy-done.2, bf16[12,16,1024]{2,1,0:T(8,128)(2,1)S(1)} %copy-done.3, bf16[12,16,1024]{2,1,0:T(8,128)(2,1)S(1)} %copy-done.4, bf16[12,16,1024]{2,1,0:T(8,128)(2,1)S(1)} %copy-done.5, f32[16,1024]{1,0:T(8,128)S(1)} %collective-permute-done.yb_ref, ...), custom_call_target="tpu_custom_call" | custom-call | flops 1207959552 | bytes 8388608 | tf_op jit(solution)/shard_map/row_solve/pallas_call | solution.py:92
  24.2 13.0 %all-to-all-start = ((f32[32,3,16,128]{3,2,1,0:T(8,128)}), f32[32,3,16,128]{3,2,1,0:T(8,128)S(1)}, u32[]{:S(2)}, u32[]{:S(2)}) async-start(f32[32,3,16,128]{3,2,1,0:T(8,128)} %row_solve.1), calls=%async_computation | async-start | bytes 1572864 | tf_op jit(solution)/shard_map/all_to_all | solution.py:169
  37.3 22.6 %all-to-all-done.x_ref = f32[32,3,16,128]{3,2,1,0:T(8,128)S(1)} async-done(((f32[32,3,16,128]{3,2,1,0:T(8,128)}), f32[32,3,16,128]{3,2,1,0:T(8,128)S(1)}, u32[]{:S(2)}, u32[]{:S(2)}) %all-to-all-start) | async-done | bytes 786464 | tf_op jit(solution)/shard_map/all_to_all | solution.py:169
  59.9 2.1 %column_solve.1 = f32[32,3,16,128]{3,2,1,0:T(8,128)S(1)} custom-call(s32[1]{0:T(128)} %bitcast.first_ref, s32[16]{0:T(128)S(1)} %copy-done.6, f32[32,3,16,128]{3,2,1,0:T(8,128)S(1)} %all-to-all-done.x_ref, bf16[2,512,512]{2,1,0:T(8,128)(2,1)S(1)} %get-tuple-element.11.wh_ref, bf16[2,512,512]{2,1,0:T(8,128)(2,1)S(1)} %get-tuple-element.12.wl_ref), custom_call_target="tpu_custom_call" | custom-call | flops 1207959552 | bytes 4194304 | tf_op jit(solution)/shard_map/column_solve/pallas_call | solution.py:136
  62.0 26.6 %all_to_all.10.x_ref = f32[32,3,16,128]{3,2,1,0:T(8,128)S(1)} all-to-all(f32[32,3,16,128]{3,2,1,0:T(8,128)S(1)} %column_solve.1), channel_id=1, replica_groups=mesh['slab'=8,'pencil'=32] {'pencil'}, dimensions={0} | all-to-all | bytes 1572864 | tf_op jit(solution)/shard_map/all_to_all | solution.py:169
  88.5 0.9 %place.1 = f32[12,16,1024]{2,1,0:T(8,128)} custom-call(f32[32,3,16,128]{3,2,1,0:T(8,128)S(1)} %all_to_all.10.x_ref), custom_call_target="tpu_custom_call" | custom-call | tf_op jit(solution)/shard_map/place/pallas_call | solution.py:158
  (11 shorter events, 0.1 us)
Async XLA Ops:
  1.2 17.7 %collective-permute-start.2 = (f32[12,1024]{1,0:T(8,128)S(1)}, f32[12,1024]{1,0:T(8,128)S(1)}, u32[]{:S(2)}, u32[]{:S(2)}) collective-permute-start(f32[12,1024]{1,0:T(8,128)S(1)} %bitcast.11), channel_id=1, source_target_pairs={{0,1},{1,2},{2,3},{3,4},{4,5},{5,6},{6,7},{7,8},{8,9},{9,10},{10,1... | collective-permute-start | bytes 147464 | tf_op jit(solution)/shard_map/ppermute | solution.py:181
  5.8 13.0 %collective-permute-start.3 = (f32[12,1024]{1,0:T(8,128)S(1)}, f32[12,1024]{1,0:T(8,128)S(1)}, u32[]{:S(2)}, u32[]{:S(2)}) collective-permute-start(f32[12,1024]{1,0:T(8,128)S(1)} %bitcast.12), channel_id=1, source_target_pairs={{1,0},{2,1},{3,2},{4,3},{5,4},{6,5},{7,6},{8,7},{9,8},{10,9},{11,1... | collective-permute-start | bytes 147464 | tf_op jit(solution)/shard_map/ppermute | solution.py:182
  8.6 10.2 %collective-permute-start.1 = (f32[16,1024]{1,0:T(8,128)S(1)}, f32[16,1024]{1,0:T(8,128)S(1)}, u32[]{:S(2)}, u32[]{:S(2)}) collective-permute-start(f32[16,1024]{1,0:T(8,128)S(1)} %get-tuple-element.15), channel_id=1, source_target_pairs={{32,0},{64,32},{96,64},{128,96},{160,128},{192,160},{224,192},{0,2... | collective-permute-start | bytes 196616 | tf_op jit(solution)/shard_map/ppermute | solution.py:180
  13.5 6.7 %collective-permute-start = (f32[16,1024]{1,0:T(8,128)S(1)}, f32[16,1024]{1,0:T(8,128)S(1)}, u32[]{:S(2)}, u32[]{:S(2)}) collective-permute-start(f32[16,1024]{1,0:T(8,128)S(1)} %get-tuple-element.16), channel_id=1, source_target_pairs={{0,32},{32,64},{64,96},{96,128},{128,160},{160,192},{192,224},{224... | collective-permute-start | bytes 196616 | tf_op jit(solution)/shard_map/ppermute | solution.py:179
  13.6 2.2 %copy-start = (f32[1024,1024]{1,0:T(8,128)S(1)}, f32[1024,1024]{1,0:T(8,128)}, u32[]{:S(2)}) copy-start(f32[1024,1024]{1,0:T(8,128)} %a_ref.1) | copy-start | bytes 12582916
  15.8 1.6 %copy-start.1 = (f32[2,512,512]{2,1,0:T(8,128)S(1)}, f32[2,512,512]{2,1,0:T(8,128)}, u32[]{:S(2)}) copy-start(f32[2,512,512]{2,1,0:T(8,128)} %w_ref.2) | copy-start | bytes 6291460
  17.4 3.0 %copy-start.2 = (f32[12,16,1024]{2,1,0:T(8,128)S(1)}, f32[12,16,1024]{2,1,0:T(8,128)}, u32[]{:S(2)}) copy-start(f32[12,16,1024]{2,1,0:T(8,128)} %t_ref.1) | copy-start | bytes 2359300
  17.4 3.0 %copy-start.3 = (bf16[12,16,1024]{2,1,0:T(8,128)(2,1)S(1)}, bf16[12,16,1024]{2,1,0:T(8,128)(2,1)}, u32[]{:S(2)}) copy-start(bf16[12,16,1024]{2,1,0:T(8,128)(2,1)} %u_ref.1) | copy-start | bytes 1179652
  17.4 3.0 %copy-start.4 = (bf16[12,16,1024]{2,1,0:T(8,128)(2,1)S(1)}, bf16[12,16,1024]{2,1,0:T(8,128)(2,1)}, u32[]{:S(2)}) copy-start(bf16[12,16,1024]{2,1,0:T(8,128)(2,1)} %v_ref.1) | copy-start | bytes 1179652
  17.4 3.0 %copy-start.5 = (bf16[12,16,1024]{2,1,0:T(8,128)(2,1)S(1)}, bf16[12,16,1024]{2,1,0:T(8,128)(2,1)}, u32[]{:S(2)}) copy-start(bf16[12,16,1024]{2,1,0:T(8,128)(2,1)} %w_ref.3) | copy-start | bytes 1179652
  20.4 39.5 %copy-start.6 = (s32[16]{0:T(128)S(1)}, s32[16]{0:T(128)}, u32[]{:S(2)}) copy-start(s32[16]{0:T(128)} %seg_ref.1) | copy-start | bytes 196
  24.2 35.6 %all-to-all-start = ((f32[32,3,16,128]{3,2,1,0:T(8,128)}), f32[32,3,16,128]{3,2,1,0:T(8,128)S(1)}, u32[]{:S(2)}, u32[]{:S(2)}) async-start(f32[32,3,16,128]{3,2,1,0:T(8,128)} %row_solve.1), calls=%async_computation | async-start | bytes 1572864 | tf_op jit(solution)/shard_map/all_to_all | solution.py:169
where the time goes:
time: 89.9 us; the launch traced here: 89.5 us
  blocking collectives  26.6 us (30%)
  starting transfers between devices  24.4 us (27%)
  waiting for transfers between devices  24 us (27%)
  Pallas kernels  8.35 us (9%)
  local copies, waits for them, and re-layouts  5.96 us (7%)
    all_to_all x1, blocking collectives, swapped(): return lax.all_to_all(x, 'pencil', split_axis=0, concat_axis=0, tiled=True)  26.6 us
    all_to_all x1, waiting for transfers between devices, swapped(): return lax.all_to_all(x, 'pencil', split_axis=0, concat_axis=0, tiled=True)  22.6 us
    all_to_all x1, starting transfers between devices, swapped(): return lax.all_to_all(x, 'pencil', split_axis=0, concat_axis=0, tiled=True)  13 us
    ppermute x1, starting transfers between devices, on_device(): lax.ppermute(t[0], 'slab', [((i + 1) % slabs, i) for i in range(slabs)])  4.89 us
    ppermute x1, starting transfers between devices, on_device(): lax.ppermute(t[:, -1], 'pencil', up)  4.59 us
    pallas_call x1, Pallas kernels, row_solve(): pl.pallas_call(row_kernel, in_specs=[VMEM] * 11, out_specs=VMEM, out_shap...  3.87 us
    unnamed x16, local copies, waits for them, and re-layouts  3.82 us
    pallas_call x1, Pallas kernels, column_solve(): pl.pallas_call(column_kernel, in_specs=[SMEM, SMEM, VMEM, VMEM, VMEM], ou...  2.09 us
  transfers between devices with their start and end apart: 5, of which 2 were waited for; matrix products, arithmetic and copies ran while one was open for 1% of the time, Pallas kernels for 2%

commit v1 on v0

--- a/solution.py
+++ b/solution.py
@@ -8,7 +8,10 @@
 TRANSPORT_PART = 0.25
 CONDUCTION_PART = 0.2
 LANES = 128
+EDGE = 53
+PREP = 46
 VMEM = pl.BlockSpec(memory_space=pltpu.VMEM)
+HBM = pl.BlockSpec(memory_space=pltpu.HBM)
 SMEM = pl.BlockSpec(memory_space=pltpu.SMEM)
 
 
@@ -21,30 +24,104 @@
     return high, (wide - high.astype(jnp.float32)).astype(jnp.bfloat16)
 
 
-def split_kernel(a_ref, w_ref, ah_ref, al_ref, wh_ref, wl_ref):
-    ah_ref[...], al_ref[...] = halves(a_ref[...])
-    wh_ref[...], wl_ref[...] = halves(w_ref[...])
-
-
-def split_matrices(a, w):
-    steps = 8
-    n, k = a.shape[0], w.shape[1]
-    a_spec = pl.BlockSpec((n // steps, n), lambda i: (i, 0))
-    w_spec = pl.BlockSpec((2, k // steps, k), lambda i: (0, i, 0))
+def edge_kernel(t_hbm, yf_ref, yl_ref, zl_ref, zh_ref, buf, sems):
+    planes, rows, _ = t_hbm.shape
+    half = buf.shape[2]
+    copies = [
+        pltpu.make_async_copy(t_hbm.at[:, pl.ds(0, half)], buf.at[0], sems.at[0]),
+        pltpu.make_async_copy(t_hbm.at[:, pl.ds(rows - half, half)], buf.at[1], sems.at[1]),
+        pltpu.make_async_copy(t_hbm.at[0], yf_ref, sems.at[2]),
+        pltpu.make_async_copy(t_hbm.at[planes - 1], yl_ref, sems.at[3]),
+    ]
+    for copy in copies:
+        copy.start()
+    copies[0].wait()
+    for y in range(planes):
+        zl_ref[y : y + 1, :] = buf[0, y, :1, :]
+    copies[1].wait()
+    for y in range(planes):
+        zh_ref[y : y + 1, :] = buf[1, y, half - 1 :, :]
+    copies[2].wait()
+    copies[3].wait()
+
+
+def edges(t):
+    planes, rows, nx = t.shape
+    half = 8
+    plane = jax.ShapeDtypeStruct((rows, nx), t.dtype)
+    level = jax.ShapeDtypeStruct((planes, nx), t.dtype)
+    return pl.pallas_call(
+        edge_kernel,
+        in_specs=[HBM],
+        out_specs=[VMEM] * 4,
+        out_shape=[plane, plane, level, level],
+        scratch_shapes=[pltpu.VMEM((2, planes, half, nx), t.dtype), pltpu.SemaphoreType.DMA((4,))],
+        compiler_params=pltpu.CompilerParams(vmem_limit_bytes=EDGE * 2**20),
+        name="edges",
+    )(t)
+
+
+def prepare_kernel(here_ref, seg_ref, a_hbm, w_hbm, ah_ref, al_ref, wh_ref, wl_ref, mask_ref, g_ref, a_buf, w_buf, sems):
+    parts = sems.shape[0] // 2
+    a_rows, w_rows = a_buf.shape[0] // parts, w_buf.shape[1] // parts
+    copies = []
+    for i in range(parts):
+        cut = slice(i * a_rows, (i + 1) * a_rows)
+        copies.append(pltpu.make_async_copy(a_hbm.at[cut], a_buf.at[cut], sems.at[i]))
+    for i in range(parts):
+        cut = slice(i * w_rows, (i + 1) * w_rows)
+        copies.append(pltpu.make_async_copy(w_hbm.at[:, cut], w_buf.at[:, cut], sems.at[parts + i]))
+    for copy in copies:
+        copy.start()
+    here = here_ref[0]
+    rows, lanes = g_ref.shape
+    blocks = a_buf.shape[0] // lanes
+    column = lax.broadcasted_iota(jnp.int32, mask_ref.shape, 1) + here % blocks * lanes
+    crossed = jnp.zeros(mask_ref.shape, jnp.int32)
+    end = jnp.int32(0)
+    for s in range(seg_ref.shape[0]):
+        end = end + seg_ref[s]
+        crossed = crossed + jnp.where(column >= end, 1, 0)
+    mask_ref[...] = crossed % 2
+    levels = (lax.broadcasted_iota(jnp.int32, (rows, lanes), 0) + here * rows).astype(jnp.float32)
+    g_ref[...] = metric_of(levels, w_buf.shape[1])
+    for i in range(parts):
+        cut = slice(i * a_rows, (i + 1) * a_rows)
+        copies[i].wait()
+        ah_ref[cut], al_ref[cut] = halves(a_buf[cut])
+    for i in range(parts):
+        cut = slice(i * w_rows, (i + 1) * w_rows)
+        copies[parts + i].wait()
+        wh_ref[:, cut], wl_ref[:, cut] = halves(w_buf[:, cut])
+
+
+def prepare(here, segments, a, w, rows):
     a16 = jax.ShapeDtypeStruct(a.shape, jnp.bfloat16)
     w16 = jax.ShapeDtypeStruct(w.shape, jnp.bfloat16)
-    return pl.pallas_call(
-        split_kernel,
-        grid=(steps,),
-        in_specs=[a_spec, w_spec],
-        out_specs=[a_spec, a_spec, w_spec, w_spec],
-        out_shape=[a16, a16, w16, w16],
-        compiler_params=pltpu.CompilerParams(vmem_limit_bytes=16 * 2**20),
+    parts = 4
+    return pl.pallas_call(
+        prepare_kernel,
+        in_specs=[SMEM, SMEM, HBM, HBM],
+        out_specs=[VMEM] * 6,
+        out_shape=[
+            a16,
+            a16,
+            w16,
+            w16,
+            jax.ShapeDtypeStruct((8, LANES), jnp.int32),
+            jax.ShapeDtypeStruct((rows, LANES), jnp.float32),
+        ],
+        scratch_shapes=[
+            pltpu.VMEM(a.shape, a.dtype),
+            pltpu.VMEM(w.shape, w.dtype),
+            pltpu.SemaphoreType.DMA((2 * parts,)),
+        ],
+        compiler_params=pltpu.CompilerParams(vmem_limit_bytes=PREP * 2**20),
         cost_estimate=pl.CostEstimate(
             flops=4 * (a.size + w.size), bytes_accessed=8 * (a.size + w.size), transcendentals=0
         ),
-        name="split_matrices",
-    )(a, w)
+        name="prepare",
+    )(here, segments, a, w)
 
 
 def row_kernel(t_ref, u_ref, v_ref, w_ref, yb_ref, ya_ref, zb_ref, za_ref, g_ref, ah_ref, al_ref, out_ref, rh, rl):
@@ -103,15 +180,9 @@
     )(t, u, v, w, *halos, metric, ah, al)
 
 
-def column_kernel(first_ref, seg_ref, x_ref, wh_ref, wl_ref, out_ref):
+def column_kernel(mask_ref, x_ref, wh_ref, wl_ref, out_ref):
     groups, units, rows, lanes = x_ref.shape
-    column = lax.broadcasted_iota(jnp.int32, (1, lanes), 1) + first_ref[0]
-    crossed = jnp.zeros((1, lanes), jnp.int32)
-    end = jnp.int32(0)
-    for s in range(seg_ref.shape[0]):
-        end = end + seg_ref[s]
-        crossed = crossed + jnp.where(column >= end, 1, 0)
-    insulated = jnp.concatenate([crossed % 2] * units, axis=1) == 1
+    insulated = jnp.concatenate([mask_ref[:1, :]] * units, axis=1) == 1
     extent = groups * rows
     lines = jnp.concatenate([x_ref[:, i].reshape(extent, lanes) for i in range(units)], axis=1)
     xh, xl = halves(lines)
@@ -132,10 +203,10 @@
             )
 
 
-def column_solve(first, segments, x, wh, wl):
+def column_solve(mask, x, wh, wl):
     return pl.pallas_call(
         column_kernel,
-        in_specs=[SMEM, SMEM, VMEM, VMEM, VMEM],
+        in_specs=[VMEM] * 4,
         out_specs=VMEM,
         out_shape=jax.ShapeDtypeStruct(x.shape, jnp.float32),
         compiler_params=pltpu.CompilerParams(vmem_limit_bytes=32 * 2**20),
@@ -143,7 +214,7 @@
             flops=12 * wh.shape[1] * x.size, bytes_accessed=4 * 2**20, transcendentals=0
         ),
         name="column_solve",
-    )(first, segments, x, wh, wl)
+    )(mask, x, wh, wl)
 
 
 def place_kernel(x_ref, out_ref):
@@ -175,18 +246,18 @@
     here = lax.axis_index("pencil")
     up = [(i, i + 1) for i in range(groups - 1)]
     down = [(i + 1, i) for i in range(groups - 1)]
+    y_first, y_last, z_low, z_high = edges(t)
     halos = (
-        lax.ppermute(t[-1], "slab", [(i, (i + 1) % slabs) for i in range(slabs)]),
-        lax.ppermute(t[0], "slab", [((i + 1) % slabs, i) for i in range(slabs)]),
-        lax.ppermute(t[:, -1], "pencil", up),
-        lax.ppermute(t[:, 0], "pencil", down),
+        lax.ppermute(y_last, "slab", [(i, (i + 1) % slabs) for i in range(slabs)]),
+        lax.ppermute(y_first, "slab", [((i + 1) % slabs, i) for i in range(slabs)]),
+        lax.ppermute(z_high, "pencil", up),
+        lax.ppermute(z_low, "pencil", down),
     )
-    levels = (here * rows + jnp.arange(rows, dtype=jnp.int32)).astype(jnp.float32)
-    metric = jnp.broadcast_to(metric_of(levels, groups * rows)[:, None], (rows, LANES))
-    ah, al, wh, wl = split_matrices(downstream_solver_matrix, wallward_solver_matrices)
+    ah, al, wh, wl, mask, metric = prepare(
+        here.astype(jnp.int32).reshape(1), wall_segments, downstream_solver_matrix, wallward_solver_matrices, rows
+    )
     x = swapped(row_solve(t, u, v, w, halos, metric, ah, al, groups))
-    first = (here % (nx // LANES) * LANES).astype(jnp.int32).reshape(1)
-    x = swapped(column_solve(first, wall_segments, x, wh, wl))
+    x = swapped(column_solve(mask, x, wh, wl))
     return place(x, t.shape)
 
 

time: 89.9 us -> 83.8 us (0.932)
  blocking collectives: 26.6 us -> 60.3 us
  waiting for transfers between devices: 24 us -> 0.01 us
  starting transfers between devices: 24.4 us -> 12.2 us
  local copies, waits for them, and re-layouts: 5.96 us -> 0.67 us
  Pallas kernels: 8.35 us -> 10.2 us
    all_to_all x1 -> x2, blocking collectives: 26.6 us -> 60.3 us  [swapped(): return lax.all_to_all(x, 'pencil', split_axis=0, concat_axis=0, tiled=True)]
    all_to_all x1 -> x0, waiting for transfers between devices: 22.6 us -> none  [swapped(): return lax.all_to_all(x, 'pencil', split_axis=0, concat_axis=0, tiled=True)]
    all_to_all x1 -> x0, starting transfers between devices: 13 us -> none  [swapped(): return lax.all_to_all(x, 'pencil', split_axis=0, concat_axis=0, tiled=True)]
    unnamed x16 -> x10, local copies, waits for them, and re-layouts: 3.82 us -> 0.67 us
    pallas_call x2 -> x3, Pallas kernels: 3.55 us -> 6.23 us  [the longest x1 3.51 us: prepare(): pl.pallas_call(prepare_kernel, in_specs=[SMEM, SMEM, HBM, HBM], out_specs...]
    ppermute x4, waiting for transfers between devices: 1.38 us -> 0.01 us  [the longest x1 0.01 us: on_device(): lax.ppermute(z_high, 'pencil', up)]
    slice x1 -> x0, local copies, waits for them, and re-layouts: 1.19 us -> none  [on_device(): t[:, 0]]
  transfers between devices with their start and end apart: 5 -> 4, of which waited for: 2 -> 0; matrix products, arithmetic and copies ran while one was open for 1% -> 0% of each run, Pallas kernels for 2% -> 4%
where the time goes in v1:
time: 83.8 us; the launch traced here: 83.6 us
  blocking collectives  60.3 us (72%)
  starting transfers between devices  12.2 us (15%)
  Pallas kernels  10.2 us (12%)
    all_to_all x2, blocking collectives, swapped(): return lax.all_to_all(x, 'pencil', split_axis=0, concat_axis=0, tiled=True)  60.3 us
    ppermute x1, starting transfers between devices, on_device(): lax.ppermute(z_high, 'pencil', up)  4.19 us
    ppermute x1, starting transfers between devices, on_device(): lax.ppermute(y_last, 'slab', [(i, (i + 1) % slabs) for i in range(slabs)])  3.82 us
    pallas_call x1, Pallas kernels, prepare(): pl.pallas_call(prepare_kernel, in_specs=[SMEM, SMEM, HBM, HBM], out_specs...  3.51 us
    pallas_call x1, Pallas kernels, row_solve(): pl.pallas_call(row_kernel, in_specs=[VMEM] * 11, out_specs=VMEM, out_shap...  3.08 us
    ppermute x1, starting transfers between devices, on_device(): lax.ppermute(y_first, 'slab', [((i + 1) % slabs, i) for i in range(slabs)])  2.28 us
    ppermute x1, starting transfers between devices, on_device(): lax.ppermute(z_low, 'pencil', down)  1.92 us
  transfers between devices with their start and end apart: 4, of which 0 were waited for; matrix products, arithmetic and copies ran while one was open for 0% of the time, Pallas kernels for 4%

profile of v1, /device:TPU:1, one launch (start us, length us, event | category | flops | bytes accessed | tf_op | source)
XLA Modules:
  0.0 83.6 jit_solution(17791924538792620274)
XLA Ops:
  0.0 1.2 %edges.1 = (f32[16,1024]{1,0:T(8,128)S(1)}, f32[16,1024]{1,0:T(8,128)S(1)}, f32[12,1024]{1,0:T(8,128)S(1)}, f32[12,1024]{1,0:T(8,128)S(1)}) custom-call(f32[12,16,1024]{2,1,0:T(8,128)} %t_ref.1), custom_call_target="tpu_custom_call" | custom-call | tf_op jit(solution)/shard_map/edges/pallas_call | solution.py:53
  1.2 3.8 %collective-permute-start = (f32[16,1024]{1,0:T(8,128)S(1)}, f32[16,1024]{1,0:T(8,128)S(1)}, u32[]{:S(2)}, u32[]{:S(2)}) collective-permute-start(f32[16,1024]{1,0:T(8,128)S(1)} %get-tuple-element.16), channel_id=1, source_target_pairs={{0,32},{32,64},{64,96},{96,128},{128,160},{160,192},{192,224},{224... | collective-permute-start | bytes 196616 | tf_op jit(solution)/shard_map/ppermute | solution.py:251
  5.0 2.3 %collective-permute-start.1 = (f32[16,1024]{1,0:T(8,128)S(1)}, f32[16,1024]{1,0:T(8,128)S(1)}, u32[]{:S(2)}, u32[]{:S(2)}) collective-permute-start(f32[16,1024]{1,0:T(8,128)S(1)} %get-tuple-element.17), channel_id=1, source_target_pairs={{32,0},{64,32},{96,64},{128,96},{160,128},{192,160},{224,192},{0,2... | collective-permute-start | bytes 196616 | tf_op jit(solution)/shard_map/ppermute | solution.py:252
  7.3 4.2 %collective-permute-start.2 = (f32[12,1024]{1,0:T(8,128)S(1)}, f32[12,1024]{1,0:T(8,128)S(1)}, u32[]{:S(2)}, u32[]{:S(2)}) collective-permute-start(f32[12,1024]{1,0:T(8,128)S(1)} %get-tuple-element.18), channel_id=1, source_target_pairs={{0,1},{1,2},{2,3},{3,4},{4,5},{5,6},{6,7},{7,8},{8,9},{9,10},{10,1... | collective-permute-start | bytes 147464 | tf_op jit(solution)/shard_map/ppermute | solution.py:253
  11.5 1.9 %collective-permute-start.3 = (f32[12,1024]{1,0:T(8,128)S(1)}, f32[12,1024]{1,0:T(8,128)S(1)}, u32[]{:S(2)}, u32[]{:S(2)}) collective-permute-start(f32[12,1024]{1,0:T(8,128)S(1)} %get-tuple-element.19), channel_id=1, source_target_pairs={{1,0},{2,1},{3,2},{4,3},{5,4},{6,5},{7,6},{8,7},{9,8},{10,9},{11,1... | collective-permute-start | bytes 147464 | tf_op jit(solution)/shard_map/ppermute | solution.py:254
  13.4 0.0 copy-start.4
  13.4 0.6 copy-done.4
  14.1 0.0 copy-start
  14.1 0.0 copy-start.1
  14.1 0.0 copy-start.2
  14.1 3.5 %prepare.1 = (bf16[1024,1024]{1,0:T(8,128)(2,1)S(1)}, bf16[1024,1024]{1,0:T(8,128)(2,1)S(1)}, bf16[2,512,512]{2,1,0:T(8,128)(2,1)S(1)}, bf16[2,512,512]{2,1,0:T(...) custom-call(s32[1]{0:T(128)} %bitcast.here_ref, s32[16]{0:T(128)S(1)} %copy-done.4, f32[1024,1024]{1,0:T(8,128)} %a_hbm.1, ...), custom_call_target="tpu_custom_call" | custom-call | flops 6291456 | bytes 12582912 | tf_op jit(solution)/shard_map/prepare/pallas_call | solution.py:102
  17.6 0.0 collective-permute-done.2.zb_ref
  17.6 0.0 collective-permute-done.3.za_ref
  17.6 0.0 collective-permute-done.yb_ref
  17.6 0.0 collective-permute-done.1.ya_ref
  17.6 0.0 copy-done
  17.7 0.0 copy-done.1
  17.7 0.0 copy-done.2
  17.7 0.0 copy-done.3
  17.7 3.1 %row_solve.1 = f32[32,3,16,128]{3,2,1,0:T(8,128)S(1)} custom-call(f32[12,16,1024]{2,1,0:T(8,128)S(1)} %copy-done, bf16[12,16,1024]{2,1,0:T(8,128)(2,1)S(1)} %copy-done.1, bf16[12,16,1024]{2,1,0:T(8,128)(2,1)S(1)} %copy-done.2, bf16[12,16,1024]{2,1,0:T(8,128)(2,1)S(1)} %copy-done.3, f32[16,1024]{1,0:T(8,128)S(1)} %collective-permute-done.yb_ref, ...), custom_call_target="tpu_custom_call" | custom-call | flops 1207959552 | bytes 8388608 | tf_op jit(solution)/shard_map/row_solve/pallas_call | solution.py:169
  20.8 33.7 %all_to_all.10.x_ref = f32[32,3,16,128]{3,2,1,0:T(8,128)S(1)} all-to-all(f32[32,3,16,128]{3,2,1,0:T(8,128)S(1)} %row_solve.1), channel_id=1, replica_groups=mesh['slab'=8,'pencil'=32] {'pencil'}, dimensions={0} | all-to-all | bytes 1572864 | tf_op jit(solution)/shard_map/all_to_all | solution.py:240
  54.5 1.6 %column_solve.1 = f32[32,3,16,128]{3,2,1,0:T(8,128)S(1)} custom-call(s32[8,128]{1,0:T(8,128)S(1)} %get-tuple-element.15.mask_ref, f32[32,3,16,128]{3,2,1,0:T(8,128)S(1)} %all_to_all.10.x_ref, bf16[2,512,512]{2,1,0:T(8,128)(2,1)S(1)} %get-tuple-element.23.wh_ref, bf16[2,512,512]{2,1,0:T(8,128)(2,1)S(1)} %get-tuple-element.24.wl_ref), custom_call_target="tpu_custom_call" | custom-call | flops 1207959552 | bytes 4194304 | tf_op jit(solution)/shard_map/column_solve/pallas_call | solution.py:207
  56.0 26.6 %all_to_all.11.x_ref = f32[32,3,16,128]{3,2,1,0:T(8,128)S(1)} all-to-all(f32[32,3,16,128]{3,2,1,0:T(8,128)S(1)} %column_solve.1), channel_id=1, replica_groups=mesh['slab'=8,'pencil'=32] {'pencil'}, dimensions={0} | all-to-all | bytes 1572864 | tf_op jit(solution)/shard_map/all_to_all | solution.py:240
  82.6 0.9 %place.1 = f32[12,16,1024]{2,1,0:T(8,128)} custom-call(f32[32,3,16,128]{3,2,1,0:T(8,128)S(1)} %all_to_all.11.x_ref), custom_call_target="tpu_custom_call" | custom-call | tf_op jit(solution)/shard_map/place/pallas_call | solution.py:229
  (1 shorter events, 0.0 us)
Async XLA Ops:
  1.2 16.5 %collective-permute-start = (f32[16,1024]{1,0:T(8,128)S(1)}, f32[16,1024]{1,0:T(8,128)S(1)}, u32[]{:S(2)}, u32[]{:S(2)}) collective-permute-start(f32[16,1024]{1,0:T(8,128)S(1)} %get-tuple-element.16), channel_id=1, source_target_pairs={{0,32},{32,64},{64,96},{96,128},{128,160},{160,192},{192,224},{224... | collective-permute-start | bytes 196616 | tf_op jit(solution)/shard_map/ppermute | solution.py:251
  5.0 12.6 %collective-permute-start.1 = (f32[16,1024]{1,0:T(8,128)S(1)}, f32[16,1024]{1,0:T(8,128)S(1)}, u32[]{:S(2)}, u32[]{:S(2)}) collective-permute-start(f32[16,1024]{1,0:T(8,128)S(1)} %get-tuple-element.17), channel_id=1, source_target_pairs={{32,0},{64,32},{96,64},{128,96},{160,128},{192,160},{224,192},{0,2... | collective-permute-start | bytes 196616 | tf_op jit(solution)/shard_map/ppermute | solution.py:252
  7.3 10.3 %collective-permute-start.2 = (f32[12,1024]{1,0:T(8,128)S(1)}, f32[12,1024]{1,0:T(8,128)S(1)}, u32[]{:S(2)}, u32[]{:S(2)}) collective-permute-start(f32[12,1024]{1,0:T(8,128)S(1)} %get-tuple-element.18), channel_id=1, source_target_pairs={{0,1},{1,2},{2,3},{3,4},{4,5},{5,6},{6,7},{7,8},{8,9},{9,10},{10,1... | collective-permute-start | bytes 147464 | tf_op jit(solution)/shard_map/ppermute | solution.py:253
  11.5 6.1 %collective-permute-start.3 = (f32[12,1024]{1,0:T(8,128)S(1)}, f32[12,1024]{1,0:T(8,128)S(1)}, u32[]{:S(2)}, u32[]{:S(2)}) collective-permute-start(f32[12,1024]{1,0:T(8,128)S(1)} %get-tuple-element.19), channel_id=1, source_target_pairs={{1,0},{2,1},{3,2},{4,3},{5,4},{6,5},{7,6},{8,7},{9,8},{10,9},{11,1... | collective-permute-start | bytes 147464 | tf_op jit(solution)/shard_map/ppermute | solution.py:254
  13.4 0.7 copy-start.4
  14.1 3.6 %copy-start = (f32[12,16,1024]{2,1,0:T(8,128)S(1)}, f32[12,16,1024]{2,1,0:T(8,128)}, u32[]{:S(2)}) copy-start(f32[12,16,1024]{2,1,0:T(8,128)} %t_ref.1) | copy-start | bytes 2359300
  14.1 3.6 %copy-start.1 = (bf16[12,16,1024]{2,1,0:T(8,128)(2,1)S(1)}, bf16[12,16,1024]{2,1,0:T(8,128)(2,1)}, u32[]{:S(2)}) copy-start(bf16[12,16,1024]{2,1,0:T(8,128)(2,1)} %u_ref.1) | copy-start | bytes 1179652
  14.1 3.6 %copy-start.2 = (bf16[12,16,1024]{2,1,0:T(8,128)(2,1)S(1)}, bf16[12,16,1024]{2,1,0:T(8,128)(2,1)}, u32[]{:S(2)}) copy-start(bf16[12,16,1024]{2,1,0:T(8,128)(2,1)} %v_ref.1) | copy-start | bytes 1179652
  14.1 3.6 %copy-start.3 = (bf16[12,16,1024]{2,1,0:T(8,128)(2,1)S(1)}, bf16[12,16,1024]{2,1,0:T(8,128)(2,1)}, u32[]{:S(2)}) copy-start(bf16[12,16,1024]{2,1,0:T(8,128)(2,1)} %w_ref.1) | copy-start | bytes 1179652

commit v2 on v1

v2 whole, which is shorter than its diff:
```python
import jax
import jax.numpy as jnp
from jax import lax
from jax.experimental import pallas as pl
from jax.experimental.pallas import tpu as pltpu
from jax.sharding import PartitionSpec as P

TRANSPORT_PART = 0.25
CONDUCTION_PART = 0.2
LANES = 128
LAYER = 4
BULK = 2
EDGE = 53
PREP = 46
VMEM = pl.BlockSpec(memory_space=pltpu.VMEM)
HBM = pl.BlockSpec(memory_space=pltpu.HBM)
SMEM = pl.BlockSpec(memory_space=pltpu.SMEM)


def metric_of(levels, extent):
    return 0.5 / (1.0 + jnp.sin(jnp.pi * (levels + 0.5) / extent))


def halves(wide):
    high = wide.astype(jnp.bfloat16)
    return high, (wide - high.astype(jnp.float32)).astype(jnp.bfloat16)


def edge_kernel(here_ref, seg_hbm, t_hbm, yf_ref, yl_ref, zl_ref, zh_ref, mask_ref, buf, seg_ref, sems):
    planes, rows, _ = t_hbm.shape
    half = buf.shape[2]
    copies = [
        pltpu.make_async_copy(t_hbm.at[:, pl.ds(0, half)], buf.at[0], sems.at[0]),
        pltpu.make_async_copy(t_hbm.at[:, pl.ds(rows - half, half)], buf.at[1], sems.at[1]),
        pltpu.make_async_copy(t_hbm.at[0], yf_ref, sems.at[2]),
        pltpu.make_async_copy(t_hbm.at[planes - 1], yl_ref, sems.at[3]),
        pltpu.make_async_copy(seg_hbm, seg_ref, sems.at[4]),
    ]
    for copy in copies:
        copy.start()
    copies[4].wait()
    column = lax.broadcasted_iota(jnp.int32, mask_ref.shape, 1) + here_ref[0] // LAYER * LANES
    crossed = jnp.zeros(mask_ref.shape, jnp.int32)
    end = jnp.int32(0)
    for s in range(seg_ref.shape[0]):
        end = end + seg_ref[s]
        crossed = crossed + jnp.where(column >= end, 1, 0)
    mask_ref[...] = crossed % 2
    copies[0].wait()
    for y in range(planes):
        zl_ref[y : y + 1, :] = buf[0, y, :1, :]
    copies[1].wait()
    for y in range(planes):
        zh_ref[y : y + 1, :] = buf[1, y, half - 1 :, :]
    copies[2].wait()
    copies[3].wait()


def edges(here, segments, t):
    planes, rows, nx = t.shape
    half = 8
    plane = jax.ShapeDtypeStruct((rows, nx), t.dtype)
    level = jax.ShapeDtypeStruct((planes, nx), t.dtype)
    return pl.pallas_call(
        edge_kernel,
        in_specs=[SMEM, HBM, HBM],
        out_specs=[VMEM] * 5,
        out_shape=[plane, plane, level, level, jax.ShapeDtypeStruct((8, LANES), jnp.int32)],
        scratch_shapes=[
            pltpu.VMEM((2, planes, half, nx), t.dtype),
            pltpu.SMEM(segments.shape, jnp.int32),
            pltpu.SemaphoreType.DMA((5,)),
        ],
        compiler_params=pltpu.CompilerParams(vmem_limit_bytes=EDGE * 2**20),
        name="edges",
    )(here, segments, t)


def prepare_kernel(here_ref, a_hbm, w_hbm, ah_ref, al_ref, wh_ref, wl_ref, g_ref, a_buf, w_buf, sems):
    parts = sems.shape[0] // 2
    a_rows, w_rows = a_buf.shape[0] // parts, w_buf.shape[1] // parts
    copies = []
    for i in range(parts):
        cut = slice(i * a_rows, (i + 1) * a_rows)
        copies.append(pltpu.make_async_copy(a_hbm.at[cut], a_buf.at[cut], sems.at[i]))
    for i in range(parts):
        cut = slice(i * w_rows, (i + 1) * w_rows)
        copies.append(pltpu.make_async_copy(w_hbm.at[:, cut], w_buf.at[:, cut], sems.at[parts + i]))
    for copy in copies:
        copy.start()
    rows, lanes = g_ref.shape
    levels = (lax.broadcasted_iota(jnp.int32, (rows, lanes), 0) + here_ref[0] * rows).astype(jnp.float32)
    g_ref[...] = metric_of(levels, w_buf.shape[1])
    for i in range(parts):
        cut = slice(i * a_rows, (i + 1) * a_rows)
        copies[i].wait()
        ah_ref[cut], al_ref[cut] = halves(a_buf[cut])
    for i in range(parts):
        cut = slice(i * w_rows, (i + 1) * w_rows)
        copies[parts + i].wait()
        wh_ref[:, cut], wl_ref[:, cut] = halves(w_buf[:, cut])


def prepare(here, a, w, rows):
    a16 = jax.ShapeDtypeStruct(a.shape, jnp.bfloat16)
    w16 = jax.ShapeDtypeStruct(w.shape, jnp.bfloat16)
    parts = 4
    return pl.pallas_call(
        prepare_kernel,
        in_specs=[SMEM, HBM, HBM],
        out_specs=[VMEM] * 5,
        out_shape=[a16, a16, w16, w16, jax.ShapeDtypeStruct((rows, LANES), jnp.float32)],
        scratch_shapes=[
            pltpu.VMEM(a.shape, a.dtype),
            pltpu.VMEM(w.shape, w.dtype),
            pltpu.SemaphoreType.DMA((2 * parts,)),
        ],
        compiler_params=pltpu.CompilerParams(vmem_limit_bytes=PREP * 2**20),
        cost_estimate=pl.CostEstimate(
            flops=4 * (a.size + w.size), bytes_accessed=8 * (a.size + w.size), transcendentals=0
        ),
        name="prepare",
    )(here, a, w)


def row_kernel(
    here_ref, t_ref, u_ref, v_ref, w_ref, yb_ref, ya_ref, zb_ref, za_ref, g_ref, ah_ref, al_ref, out_ref, *rest
):
    by_place, (rh, rl, kept) = rest[:LAYER], rest[LAYER:]
    planes, rows, nx = t_ref.shape
    metric = jnp.concatenate([g_ref[...]] * (nx // LANES), axis=1)
    level = lax.broadcasted_iota(jnp.int32, (rows, nx), 0)
    for y in range(planes):
        t = t_ref[y]
        ahead = t_ref[y + 1] if y + 1 < planes else ya_ref[...]
        behind = t_ref[y - 1] if y else yb_ref[...]
        east = pltpu.roll(t, nx - 1, 1)
        west = pltpu.roll(t, 1, 1)
        above = jnp.where(level == rows - 1, za_ref[y : y + 1, :], pltpu.roll(t, rows - 1, 0))
        below = jnp.where(level == 0, zb_ref[y : y + 1, :], pltpu.roll(t, 1, 0))
        u = u_ref[y].astype(jnp.float32)
        v = v_ref[y].astype(jnp.float32)
        w = w_ref[y].astype(jnp.float32)
        carried = 0.5 * u * (east - west) + 0.5 * v * (ahead - behind) + w * metric * (above - below)
        conducted = (
            (ahead - 2.0 * t + behind)
            + 0.5 * (east - 2.0 * t + west)
            + 0.5 * metric * (above - 2.0 * t + below)
        )
        side = t - TRANSPORT_PART * carried + CONDUCTION_PART * conducted
        rh[y * rows : (y + 1) * rows, :], rl[y * rows : (y + 1) * rows, :] = halves(side)
    wide = 2 * LANES
    unit_rows = 3 * rows
    blocks = nx // LANES
    for c in range(nx // wide):
        ah = ah_ref[c * wide : (c + 1) * wide, :]
        al = al_ref[c * wide : (c + 1) * wide, :]

        def dot(x, m):
            return lax.dot_general(x, m, (((1,), (1,)), ((), ())), preferred_element_type=jnp.float32)

        solved = dot(rh[...], ah) + (dot(rh[...], al) + dot(rl[...], ah))
        for q in range(planes // 3):
            for h in range(2):
                block = 2 * c + h
                piece = solved[q * unit_rows : (q + 1) * unit_rows, h * LANES : (h + 1) * LANES]
                piece = piece.reshape(3, rows, LANES)
                out_ref[LAYER * block + q] = piece[:BULK]
                kept[q, block] = piece[BULK]
    layer, place_ = here_ref[0] // LAYER, here_ref[0] % LAYER
    for s in range(LAYER):
        for d in range(blocks):
            by_place[s][d] = kept[place_ ^ s, (layer + d) % blocks]


def row_solve(here, t, u, v, w, halos, metric, ah, al, groups):
    planes, rows, nx = t.shape
    layers = groups // LAYER
    lines = jax.ShapeDtypeStruct((layers, rows, LANES), jnp.float32)
    return pl.pallas_call(
        row_kernel,
        in_specs=[SMEM] + [VMEM] * 11,
        out_specs=[VMEM] * (1 + LAYER),
        out_shape=[jax.ShapeDtypeStruct((groups, BULK, rows, LANES), jnp.float32)] + [lines] * LAYER,
        scratch_shapes=[pltpu.VMEM((planes * rows, nx), jnp.bfloat16)] * 2
        + [pltpu.VMEM((LAYER, layers, rows, LANES), jnp.float32)],
        compiler_params=pltpu.CompilerParams(vmem_limit_bytes=32 * 2**20),
        cost_estimate=pl.CostEstimate(
            flops=6 * planes * rows * nx * nx, bytes_accessed=8 * 2**20, transcendentals=0
        ),
        name="row_solve",
    )(here, t, u, v, w, *halos, metric, ah, al)


def solved_lines(lines, insulated, wh_ref, wl_ref, k, step):
    xh, both = lines
    width = xh.shape[1]

    def solve(c):
        d = jnp.dot(wh_ref[c, k : k + step, :], both, preferred_element_type=jnp.float32)
        e = jnp.dot(wl_ref[c, k : k + step, :], xh, preferred_element_type=jnp.float32)
        return d[:, :width] + (d[:, width:] + e)

    return jnp.where(insulated, solve(1), solve(0))


def column_kernel(mask_ref, x_ref, wh_ref, wl_ref, _, out_ref):
    groups, units, rows, lanes = x_ref.shape
    insulated = jnp.concatenate([mask_ref[:1, :]] * units, axis=1) == 1
    extent = groups * rows
    lines = jnp.concatenate([x_ref[:, i].reshape(extent, lanes) for i in range(units)], axis=1)
    xh, xl = halves(lines)
    lines = xh, jnp.concatenate([xh, xl], axis=1)
    step = 128
    for k in range(0, extent, step):
        solved = solved_lines(lines, insulated, wh_ref, wl_ref, k, step)
        for i in range(units):
            out_ref[k // rows : (k + step) // rows, i] = solved[:, i * lanes : (i + 1) * lanes].reshape(
                step // rows, rows, lanes
            )


def column_solve(mask, x, wh, wl, after):
    return pl.pallas_call(
        column_kernel,
        in_specs=[VMEM] * 4 + [pl.BlockSpec(memory_space=pl.ANY)],
        out_specs=VMEM,
        out_shape=jax.ShapeDtypeStruct(x.shape, jnp.float32),
        compiler_params=pltpu.CompilerParams(vmem_limit_bytes=32 * 2**20),
        cost_estimate=pl.CostEstimate(
            flops=12 * wh.shape[1] * x.size, bytes_accessed=4 * 2**20, transcendentals=0
        ),
        name="column_solve",
    )(mask, x, wh, wl, after)


def single_kernel(here_ref, mask_ref, *refs):
    layers = (len(refs) - 3 - LAYER)
    arrived, (wh_ref, wl_ref), by_place, lines = refs[:layers], refs[layers : layers + 2], refs[layers + 2 : -1], refs[-1]
    rows, lanes = lines.shape[1:]
    layer, place_ = here_ref[0] // LAYER, here_ref[0] % LAYER
    for d in range(layers):
        source = (layer + layers - d) % layers
        for s in range(LAYER):
            lines[LAYER * source + (place_ ^ s)] = arrived[d][s]
    insulated = mask_ref[:1, :] == 1
    extent = lines.shape[0] * rows
    xh, xl = halves(lines[...].reshape(extent, lanes))
    both = xh, jnp.concatenate([xh, xl], axis=1)
    step = 128
    for k in range(0, extent, step):
        solved = solved_lines(both, insulated, wh_ref, wl_ref, k, step)
        lines[k // rows : (k + step) // rows] = solved.reshape(step // rows, rows, lanes)
    for s in range(LAYER):
        for d in range(layers):
            by_place[s][d] = lines[LAYER * ((layer + d) % layers) + (place_ ^ s)]


def single_solve(here, mask, arrived, wh, wl):
    layers = len(arrived)
    rows, lanes = arrived[0].shape[1:]
    return pl.pallas_call(
        single_kernel,
        in_specs=[SMEM] + [VMEM] * (3 + layers),
        out_specs=[VMEM] * LAYER,
        out_shape=[jax.ShapeDtypeStruct((layers, rows, lanes), jnp.float32)] * LAYER,
        scratch_shapes=[pltpu.VMEM((LAYER * layers, rows, lanes), jnp.float32)],
        compiler_params=pltpu.CompilerParams(vmem_limit_bytes=32 * 2**20),
        cost_estimate=pl.CostEstimate(
            flops=12 * wh.shape[1] * LAYER * layers * rows * lanes, bytes_accessed=4 * 2**20, transcendentals=0
        ),
        name="single_solve",
    )(here, mask, *arrived, wh, wl)


def pack_kernel(*refs):
    by_place, by_layer = refs[:LAYER], refs[LAYER:]
    for d, out in enumerate(by_layer):
        for s in range(LAYER):
            out[s] = by_place[s][d]


def packed(by_place):
    layers, rows, lanes = by_place[0].shape
    return pl.pallas_call(
        pack_kernel,
        in_specs=[VMEM] * LAYER,
        out_specs=[VMEM] * layers,
        out_shape=[jax.ShapeDtypeStruct((LAYER, rows, lanes), jnp.float32)] * layers,
        compiler_params=pltpu.CompilerParams(vmem_limit_bytes=8 * 2**20),
        name="pack",
    )(*by_place)


def place_kernel(here_ref, x_ref, *rest):
    arrived, out_ref = rest[:-1], rest[-1]
    layers = len(arrived)
    layer, place_ = here_ref[0] // LAYER, here_ref[0] % LAYER
    for p in range(x_ref.shape[0]):
        q, b = p % LAYER, p // LAYER
        for i in range(BULK):
            out_ref[3 * q + i, :, b * LANES : (b + 1) * LANES] = x_ref[p, i]
    for d in range(layers):
        block = (layer + layers - d) % layers
        lanes = pl.ds(pl.multiple_of(block * LANES, LANES), LANES)
        for s in range(LAYER):
            out_ref[3 * (place_ ^ s) + BULK, :, lanes] = arrived[d][s]


def place(here, x, arrived, shape):
    return pl.pallas_call(
        place_kernel,
        in_specs=[SMEM] + [VMEM] * (1 + len(arrived)),
        out_specs=VMEM,
        out_shape=jax.ShapeDtypeStruct(shape, jnp.float32),
        compiler_params=pltpu.CompilerParams(vmem_limit_bytes=16 * 2**20),
        name="place",
    )(here, x, *arrived)


def swapped(x):
    return lax.all_to_all(x, "pencil", split_axis=0, concat_axis=0, tiled=True)


def moved(by_place):
    groups = lax.axis_size("pencil")
    by_place = [
        lax.ppermute(x, "pencil", [(i, i ^ s) for i in range(groups)]) if s else x for s, x in enumerate(by_place)
    ]
    return [
        lax.ppermute(x, "pencil", [(i, (i + LAYER * d) % groups) for i in range(groups)]) if d else x
        for d, x in enumerate(packed(by_place))
    ]


def on_device(t, u, v, w, downstream_solver_matrix, wallward_solver_matrices, wall_segments):
    planes, rows, nx = t.shape
    slabs, groups = lax.axis_size("slab"), lax.axis_size("pencil")
    here = lax.axis_index("pencil").astype(jnp.int32).reshape(1)
    up = [(i, i + 1) for i in range(groups - 1)]
    down = [(i + 1, i) for i in range(groups - 1)]
    y_first, y_last, z_low, z_high, mask = edges(here, wall_segments, t)
    halos = (
        lax.ppermute(y_last, "slab", [(i, (i + 1) % slabs) for i in range(slabs)]),
        lax.ppermute(y_first, "slab", [((i + 1) % slabs, i) for i in range(slabs)]),
        lax.ppermute(z_high, "pencil", up),
        lax.ppermute(z_low, "pencil", down),
    )
    ah, al, wh, wl, metric = prepare(here, downstream_solver_matrix, wallward_solver_matrices, rows)
    bulk, *single = row_solve(here, t, u, v, w, halos, metric, ah, al, groups)
    single = single_solve(here, mask, moved(single), wh, wl)
    bulk = swapped(column_solve(mask, swapped(bulk), wh, wl, single[0]))
    return place(here, bulk, moved(single), t.shape)


def solution(mesh):
    field = P("slab", "pencil", None)
    return jax.shard_map(
        on_device,
        mesh=mesh,
        in_specs=(field, field, field, field, P(), P(), P()),
        out_specs=field,
        check_vma=False,
    )
```

time: 83.8 us -> 95.6 us (1.14)
  blocking collectives: 60.3 us -> 0 us
  starting transfers between devices: 12.2 us -> 64.7 us
  waiting for transfers between devices: 0.01 us -> 18 us
  Pallas kernels: 10.2 us -> 11.5 us
    all_to_all x2 -> x0, blocking collectives: 60.3 us -> none  [swapped(): return lax.all_to_all(x, 'pencil', split_axis=0, concat_axis=0, tiled=True)]
    ppermute x0 -> x20, starting transfers between devices: none -> 35.3 us  [the longest x14 30.9 us: moved(): lax.ppermute(x, 'pencil', [(i, (i + LAYER * d) % groups) for i in range(g...]
    ppermute x0 -> x20, waiting for transfers between devices: none -> 17.3 us  [the longest x6 11.6 us: moved(): lax.ppermute(x, 'pencil', [(i, i ^ s) for i in range(groups)])]
    all_to_all x0 -> x2, starting transfers between devices: none -> 17.1 us  [swapped(): return lax.all_to_all(x, 'pencil', split_axis=0, concat_axis=0, tiled=True)]
    pallas_call x5 -> x8, Pallas kernels: 10.2 us -> 11.5 us  [the longest x1 3.86 us: row_solve(): pl.pallas_call(row_kernel, in_specs=[SMEM] + [VMEM] * 11, out_specs=[VMEM...]
  transfers between devices with their start and end apart: 4 -> 26, of which waited for: 0 -> 9; matrix products, arithmetic and copies ran while one was open for 0% -> 0% of each run, Pallas kernels for 4% -> 4%
where the time goes in v2:
time: 95.6 us; the launch traced here: 95.1 us
  starting transfers between devices  64.7 us (68%)
  waiting for transfers between devices  18 us (19%)
  Pallas kernels  11.5 us (12%)
    ppermute x14, starting transfers between devices, moved(): lax.ppermute(x, 'pencil', [(i, (i + LAYER * d) % groups) for i in range(g...  30.9 us
    all_to_all x2, starting transfers between devices, swapped(): return lax.all_to_all(x, 'pencil', split_axis=0, concat_axis=0, tiled=True)  17.1 us
    ppermute x6, waiting for transfers between devices, moved(): lax.ppermute(x, 'pencil', [(i, i ^ s) for i in range(groups)])  11.6 us
    ppermute x14, waiting for transfers between devices, moved(): lax.ppermute(x, 'pencil', [(i, (i + LAYER * d) % groups) for i in range(g...  5.73 us
    ppermute x6, starting transfers between devices, moved(): lax.ppermute(x, 'pencil', [(i, i ^ s) for i in range(groups)])  4.46 us
    ppermute x1, starting transfers between devices, on_device(): lax.ppermute(z_high, 'pencil', up)  4.19 us
    pallas_call x1, Pallas kernels, row_solve(): pl.pallas_call(row_kernel, in_specs=[SMEM] + [VMEM] * 11, out_specs=[VMEM...  3.86 us
    ppermute x1, starting transfers between devices, on_device(): lax.ppermute(y_last, 'slab', [(i, (i + 1) % slabs) for i in range(slabs)])  3.82 us
  transfers between devices with their start and end apart: 26, of which 9 were waited for; matrix products, arithmetic and copies ran while one was open for 0% of the time, Pallas kernels for 4%

profile of v2, /device:TPU:1, one launch (start us, length us, event | category | flops | bytes accessed | tf_op | source)
XLA Modules:
  0.0 95.1 jit_solution(10794252372467732112)
XLA Ops:
  1.8 3.8 %collective-permute-start = (f32[16,1024]{1,0:T(8,128)S(1)}, f32[16,1024]{1,0:T(8,128)S(1)}, u32[]{:S(2)}, u32[]{:S(2)}) collective-permute-start(f32[16,1024]{1,0:T(8,128)S(1)} %get-tuple-element.41), channel_id=1, source_target_pairs={{0,32},{32,64},{64,96},{96,128},{128,160},{160,192},{192,224},{224... | collective-permute-start | bytes 196616 | tf_op jit(solution)/shard_map/ppermute | solution.py:344
  5.7 2.3 %collective-permute-start.1 = (f32[16,1024]{1,0:T(8,128)S(1)}, f32[16,1024]{1,0:T(8,128)S(1)}, u32[]{:S(2)}, u32[]{:S(2)}) collective-permute-start(f32[16,1024]{1,0:T(8,128)S(1)} %get-tuple-element.42), channel_id=1, source_target_pairs={{32,0},{64,32},{96,64},{128,96},{160,128},{192,160},{224,192},{0,2... | collective-permute-start | bytes 196616 | tf_op jit(solution)/shard_map/ppermute | solution.py:345
  7.9 4.2 %collective-permute-start.2 = (f32[12,1024]{1,0:T(8,128)S(1)}, f32[12,1024]{1,0:T(8,128)S(1)}, u32[]{:S(2)}, u32[]{:S(2)}) collective-permute-start(f32[12,1024]{1,0:T(8,128)S(1)} %get-tuple-element.43), channel_id=1, source_target_pairs={{0,1},{1,2},{2,3},{3,4},{4,5},{5,6},{6,7},{7,8},{8,9},{9,10},{10,1... | collective-permute-start | bytes 147464 | tf_op jit(solution)/shard_map/ppermute | solution.py:346
  12.2 2.1 %collective-permute-start.3 = (f32[12,1024]{1,0:T(8,128)S(1)}, f32[12,1024]{1,0:T(8,128)S(1)}, u32[]{:S(2)}, u32[]{:S(2)}) collective-permute-start(f32[12,1024]{1,0:T(8,128)S(1)} %get-tuple-element.44), channel_id=1, source_target_pairs={{1,0},{2,1},{3,2},{4,3},{5,4},{6,5},{7,6},{8,7},{9,8},{10,9},{11,1... | collective-permute-start | bytes 147464 | tf_op jit(solution)/shard_map/ppermute | solution.py:347
  14.3 2.9 %prepare.1 = (bf16[1024,1024]{1,0:T(8,128)(2,1)S(1)}, bf16[1024,1024]{1,0:T(8,128)(2,1)S(1)}, bf16[2,512,512]{2,1,0:T(8,128)(2,1)S(1)}, bf16[2,512,512]{2,1,0:T(8,128)(2,1)S(1)}, f32[16,128]{1,0:T(8,128)S(1)}) custom-call(s32[1]{0:T(128)} %bitcast.here_ref, f32[1024,1024]{1,0:T(8,128)} %a_hbm.1, f32[2,512,512]{2,1,0:T(8,128)} %w_hbm.1), custom_call_target="tpu_custom_call" | custom-call | flops 6291456 | bytes 12582912 | tf_op jit(solution)/shard_map/prepare/pallas_call | solution.py:108
  18.0 3.9 %row_solve.1 = (f32[32,2,16,128]{3,2,1,0:T(8,128)}, f32[8,16,128]{2,1,0:T(8,128)S(1)}, f32[8,16,128]{2,1,0:T(8,128)S(1)}, f32[8,16,128]{2,1,0:T(8,128)S(1)}, f32[8,16,128]{2,1,0:T(8,128)S(1)}) custom-call(s32[1]{0:T(128)} %bitcast.here_ref, f32[12,16,1024]{2,1,0:T(8,128)S(1)} %copy-done, bf16[12,16,1024]{2,1,0:T(8,128)(2,1)S(1)} %copy-done.1, ...), custom_call_target="tpu_custom_call" | custom-call | flops 1207959552 | bytes 8388608 | tf_op jit(solution)/shard_map/row_solve/pallas_call | solution.py:180
  21.8 10.7 %all-to-all-start = ((f32[32,2,16,128]{3,2,1,0:T(8,128)}), f32[32,2,16,128]{3,2,1,0:T(8,128)S(1)}, u32[]{:S(2)}, u32[]{:S(2)}) async-start(f32[32,2,16,128]{3,2,1,0:T(8,128)} %get-tuple-element.48), calls=%async_computation | async-start | bytes 1048576 | tf_op jit(solution)/shard_map/all_to_all | solution.py:322
  34.8 2.1 %collective-permute-done.5.refs_2_ = f32[8,16,128]{2,1,0:T(8,128)S(1)} collective-permute-done((f32[8,16,128]{2,1,0:T(8,128)S(1)}, f32[8,16,128]{2,1,0:T(8,128)S(1)}, u32[]{:S(2)}, u32[]{:S(2)}) %collective-permute-start.5) | collective-permute-done | bytes 65568 | tf_op jit(solution)/shard_map/ppermute | solution.py:328
  36.8 3.7 %collective-permute-done.6.refs_3_ = f32[8,16,128]{2,1,0:T(8,128)S(1)} collective-permute-done((f32[8,16,128]{2,1,0:T(8,128)S(1)}, f32[8,16,128]{2,1,0:T(8,128)S(1)}, u32[]{:S(2)}, u32[]{:S(2)}) %collective-permute-start.6) | collective-permute-done | bytes 65568 | tf_op jit(solution)/shard_map/ppermute | solution.py:328
  40.6 1.5 %collective-permute-start.7 = (f32[4,16,128]{2,1,0:T(8,128)S(1)}, f32[4,16,128]{2,1,0:T(8,128)S(1)}, u32[]{:S(2)}, u32[]{:S(2)}) collective-permute-start(f32[4,16,128]{2,1,0:T(8,128)S(1)} %get-tuple-element.56), channel_id=1, source_target_pairs={{0,4},{1,5},{2,6},{3,7},{4,8},{5,9},{6,10},{7,11},{8,12},{9,13},{1... | collective-permute-start | bytes 98312 | tf_op jit(solution)/shard_map/ppermute | solution.py:331
  42.1 1.9 %collective-permute-start.8 = (f32[4,16,128]{2,1,0:T(8,128)S(1)}, f32[4,16,128]{2,1,0:T(8,128)S(1)}, u32[]{:S(2)}, u32[]{:S(2)}) collective-permute-start(f32[4,16,128]{2,1,0:T(8,128)S(1)} %get-tuple-element.57), channel_id=1, source_target_pairs={{0,8},{1,9},{2,10},{3,11},{4,12},{5,13},{6,14},{7,15},{8,16},{9,17... | collective-permute-start | bytes 98312 | tf_op jit(solution)/shard_map/ppermute | solution.py:331
  44.0 3.3 %collective-permute-start.9 = (f32[4,16,128]{2,1,0:T(8,128)S(1)}, f32[4,16,128]{2,1,0:T(8,128)S(1)}, u32[]{:S(2)}, u32[]{:S(2)}) collective-permute-start(f32[4,16,128]{2,1,0:T(8,128)S(1)} %get-tuple-element.58), channel_id=1, source_target_pairs={{0,12},{1,13},{2,14},{3,15},{4,16},{5,17},{6,18},{7,19},{8,20},{9,... | collective-permute-start | bytes 98312 | tf_op jit(solution)/shard_map/ppermute | solution.py:331
  48.7 3.0 %collective-permute-start.11 = (f32[4,16,128]{2,1,0:T(8,128)S(1)}, f32[4,16,128]{2,1,0:T(8,128)S(1)}, u32[]{:S(2)}, u32[]{:S(2)}) collective-permute-start(f32[4,16,128]{2,1,0:T(8,128)S(1)} %get-tuple-element.60), channel_id=1, source_target_pairs={{0,20},{1,21},{2,22},{3,23},{4,24},{5,25},{6,26},{7,27},{8,28},{9,... | collective-permute-start | bytes 98312 | tf_op jit(solution)/shard_map/ppermute | solution.py:331
  51.8 3.3 %collective-permute-start.12 = (f32[4,16,128]{2,1,0:T(8,128)S(1)}, f32[4,16,128]{2,1,0:T(8,128)S(1)}, u32[]{:S(2)}, u32[]{:S(2)}) collective-permute-start(f32[4,16,128]{2,1,0:T(8,128)S(1)} %get-tuple-element.61), channel_id=1, source_target_pairs={{0,24},{1,25},{2,26},{3,27},{4,28},{5,29},{6,30},{7,31},{8,0},{9,1... | collective-permute-start | bytes 98312 | tf_op jit(solution)/shard_map/ppermute | solution.py:331
  56.0 2.1 %collective-permute-done.12.refs_6_ = f32[4,16,128]{2,1,0:T(8,128)S(1)} collective-permute-done((f32[4,16,128]{2,1,0:T(8,128)S(1)}, f32[4,16,128]{2,1,0:T(8,128)S(1)}, u32[]{:S(2)}, u32[]{:S(2)}) %collective-permute-start.12) | collective-permute-done | bytes 32800 | tf_op jit(solution)/shard_map/ppermute | solution.py:331
  59.7 1.8 %column_solve.1 = f32[32,2,16,128]{3,2,1,0:T(8,128)} custom-call(s32[8,128]{1,0:T(8,128)S(1)} %get-tuple-element.40.mask_ref, f32[32,2,16,128]{3,2,1,0:T(8,128)S(1)} %all-to-all-done.x_ref, bf16[2,512,512]{2,1,0:T(8,128)(2,1)S(1)} %get-tuple-element.49.refs_8_.wh_ref, bf16[2,512,512]{2,1,0:T(8,128)(2,1)S(1)} %get-tuple-element.50.refs_9_.wl_ref, ...), custom_call_target="tpu_custom_call" | custom-call | flops 805306368 | bytes 4194304 | tf_op jit(solution)/shard_map/column_solve/pallas_call | solution.py:224
  61.5 6.3 %all-to-all-start.1 = ((f32[32,2,16,128]{3,2,1,0:T(8,128)}), f32[32,2,16,128]{3,2,1,0:T(8,128)S(1)}, u32[]{:S(2)}, u32[]{:S(2)}) async-start(f32[32,2,16,128]{3,2,1,0:T(8,128)} %column_solve.1), calls=%async_computation.1 | async-start | bytes 1048576 | tf_op jit(solution)/shard_map/all_to_all | solution.py:322
  70.0 2.1 %collective-permute-done.15.refs_2_ = f32[8,16,128]{2,1,0:T(8,128)S(1)} collective-permute-done((f32[8,16,128]{2,1,0:T(8,128)S(1)}, f32[8,16,128]{2,1,0:T(8,128)S(1)}, u32[]{:S(2)}, u32[]{:S(2)}) %collective-permute-start.15) | collective-permute-done | bytes 65568 | tf_op jit(solution)/shard_map/ppermute | solution.py:328
  72.1 3.7 %collective-permute-done.16.refs_3_ = f32[8,16,128]{2,1,0:T(8,128)S(1)} collective-permute-done((f32[8,16,128]{2,1,0:T(8,128)S(1)}, f32[8,16,128]{2,1,0:T(8,128)S(1)}, u32[]{:S(2)}, u32[]{:S(2)}) %collective-permute-start.16) | collective-permute-done | bytes 65568 | tf_op jit(solution)/shard_map/ppermute | solution.py:328
  77.4 1.9 %collective-permute-start.18 = (f32[4,16,128]{2,1,0:T(8,128)S(1)}, f32[4,16,128]{2,1,0:T(8,128)S(1)}, u32[]{:S(2)}, u32[]{:S(2)}) collective-permute-start(f32[4,16,128]{2,1,0:T(8,128)S(1)} %get-tuple-element.69), channel_id=1, source_target_pairs={{0,8},{1,9},{2,10},{3,11},{4,12},{5,13},{6,14},{7,15},{8,16},{9,17... | collective-permute-start | bytes 98312 | tf_op jit(solution)/shard_map/ppermute | solution.py:331
  79.3 3.3 %collective-permute-start.19 = (f32[4,16,128]{2,1,0:T(8,128)S(1)}, f32[4,16,128]{2,1,0:T(8,128)S(1)}, u32[]{:S(2)}, u32[]{:S(2)}) collective-permute-start(f32[4,16,128]{2,1,0:T(8,128)S(1)} %get-tuple-element.70), channel_id=1, source_target_pairs={{0,12},{1,13},{2,14},{3,15},{4,16},{5,17},{6,18},{7,19},{8,20},{9,... | collective-permute-start | bytes 98312 | tf_op jit(solution)/shard_map/ppermute | solution.py:331
  84.0 3.0 %collective-permute-start.21 = (f32[4,16,128]{2,1,0:T(8,128)S(1)}, f32[4,16,128]{2,1,0:T(8,128)S(1)}, u32[]{:S(2)}, u32[]{:S(2)}) collective-permute-start(f32[4,16,128]{2,1,0:T(8,128)S(1)} %get-tuple-element.72), channel_id=1, source_target_pairs={{0,20},{1,21},{2,22},{3,23},{4,24},{5,25},{6,26},{7,27},{8,28},{9,... | collective-permute-start | bytes 98312 | tf_op jit(solution)/shard_map/ppermute | solution.py:331
  87.0 3.3 %collective-permute-start.22 = (f32[4,16,128]{2,1,0:T(8,128)S(1)}, f32[4,16,128]{2,1,0:T(8,128)S(1)}, u32[]{:S(2)}, u32[]{:S(2)}) collective-permute-start(f32[4,16,128]{2,1,0:T(8,128)S(1)} %get-tuple-element.73), channel_id=1, source_target_pairs={{0,24},{1,25},{2,26},{3,27},{4,28},{5,29},{6,30},{7,31},{8,0},{9,1... | collective-permute-start | bytes 98312 | tf_op jit(solution)/shard_map/ppermute | solution.py:331
  91.3 2.1 %collective-permute-done.22.rest_6_ = f32[4,16,128]{2,1,0:T(8,128)S(1)} collective-permute-done((f32[4,16,128]{2,1,0:T(8,128)S(1)}, f32[4,16,128]{2,1,0:T(8,128)S(1)}, u32[]{:S(2)}, u32[]{:S(2)}) %collective-permute-start.22) | collective-permute-done | bytes 32800 | tf_op jit(solution)/shard_map/ppermute | solution.py:331
  (46 shorter events, 16.8 us)
Async XLA Ops:
  1.8 16.1 %collective-permute-start = (f32[16,1024]{1,0:T(8,128)S(1)}, f32[16,1024]{1,0:T(8,128)S(1)}, u32[]{:S(2)}, u32[]{:S(2)}) collective-permute-start(f32[16,1024]{1,0:T(8,128)S(1)} %get-tuple-element.41), channel_id=1, source_target_pairs={{0,32},{32,64},{64,96},{96,128},{128,160},{160,192},{192,224},{224... | collective-permute-start | bytes 196616 | tf_op jit(solution)/shard_map/ppermute | solution.py:344
  5.7 12.3 %collective-permute-start.1 = (f32[16,1024]{1,0:T(8,128)S(1)}, f32[16,1024]{1,0:T(8,128)S(1)}, u32[]{:S(2)}, u32[]{:S(2)}) collective-permute-start(f32[16,1024]{1,0:T(8,128)S(1)} %get-tuple-element.42), channel_id=1, source_target_pairs={{32,0},{64,32},{96,64},{128,96},{160,128},{192,160},{224,192},{0,2... | collective-permute-start | bytes 196616 | tf_op jit(solution)/shard_map/ppermute | solution.py:345
  7.9 9.3 %collective-permute-start.2 = (f32[12,1024]{1,0:T(8,128)S(1)}, f32[12,1024]{1,0:T(8,128)S(1)}, u32[]{:S(2)}, u32[]{:S(2)}) collective-permute-start(f32[12,1024]{1,0:T(8,128)S(1)} %get-tuple-element.43), channel_id=1, source_target_pairs={{0,1},{1,2},{2,3},{3,4},{4,5},{5,6},{6,7},{7,8},{8,9},{9,10},{10,1... | collective-permute-start | bytes 147464 | tf_op jit(solution)/shard_map/ppermute | solution.py:346
  12.2 5.7 %collective-permute-start.3 = (f32[12,1024]{1,0:T(8,128)S(1)}, f32[12,1024]{1,0:T(8,128)S(1)}, u32[]{:S(2)}, u32[]{:S(2)}) collective-permute-start(f32[12,1024]{1,0:T(8,128)S(1)} %get-tuple-element.44), channel_id=1, source_target_pairs={{1,0},{2,1},{3,2},{4,3},{5,4},{6,5},{7,6},{8,7},{9,8},{10,9},{11,1... | collective-permute-start | bytes 147464 | tf_op jit(solution)/shard_map/ppermute | solution.py:347
  21.8 37.9 %all-to-all-start = ((f32[32,2,16,128]{3,2,1,0:T(8,128)}), f32[32,2,16,128]{3,2,1,0:T(8,128)S(1)}, u32[]{:S(2)}, u32[]{:S(2)}) async-start(f32[32,2,16,128]{3,2,1,0:T(8,128)} %get-tuple-element.48), calls=%async_computation | async-start | bytes 1048576 | tf_op jit(solution)/shard_map/all_to_all | solution.py:322
  32.9 4.0 %collective-permute-start.5 = (f32[8,16,128]{2,1,0:T(8,128)S(1)}, f32[8,16,128]{2,1,0:T(8,128)S(1)}, u32[]{:S(2)}, u32[]{:S(2)}) collective-permute-start(f32[8,16,128]{2,1,0:T(8,128)S(1)} %get-tuple-element.53), channel_id=1, source_target_pairs={{0,2},{1,3},{2,0},{3,1},{4,6},{5,7},{6,4},{7,5},{8,10},{9,11},{10,... | collective-permute-start | bytes 196616 | tf_op jit(solution)/shard_map/ppermute | solution.py:328
  34.4 6.2 %collective-permute-start.6 = (f32[8,16,128]{2,1,0:T(8,128)S(1)}, f32[8,16,128]{2,1,0:T(8,128)S(1)}, u32[]{:S(2)}, u32[]{:S(2)}) collective-permute-start(f32[8,16,128]{2,1,0:T(8,128)S(1)} %get-tuple-element.54), channel_id=1, source_target_pairs={{0,3},{1,2},{2,1},{3,0},{4,7},{5,6},{6,5},{7,4},{8,11},{9,10},{10,... | collective-permute-start | bytes 196616 | tf_op jit(solution)/shard_map/ppermute | solution.py:328
  40.6 11.2 %collective-permute-start.7 = (f32[4,16,128]{2,1,0:T(8,128)S(1)}, f32[4,16,128]{2,1,0:T(8,128)S(1)}, u32[]{:S(2)}, u32[]{:S(2)}) collective-permute-start(f32[4,16,128]{2,1,0:T(8,128)S(1)} %get-tuple-element.56), channel_id=1, source_target_pairs={{0,4},{1,5},{2,6},{3,7},{4,8},{5,9},{6,10},{7,11},{8,12},{9,13},{1... | collective-permute-start | bytes 98312 | tf_op jit(solution)/shard_map/ppermute | solution.py:331
  42.1 12.9 %collective-permute-start.8 = (f32[4,16,128]{2,1,0:T(8,128)S(1)}, f32[4,16,128]{2,1,0:T(8,128)S(1)}, u32[]{:S(2)}, u32[]{:S(2)}) collective-permute-start(f32[4,16,128]{2,1,0:T(8,128)S(1)} %get-tuple-element.57), channel_id=1, source_target_pairs={{0,8},{1,9},{2,10},{3,11},{4,12},{5,13},{6,14},{7,15},{8,16},{9,17... | collective-permute-start | bytes 98312 | tf_op jit(solution)/shard_map/ppermute | solution.py:331
  44.0 12.0 %collective-permute-start.9 = (f32[4,16,128]{2,1,0:T(8,128)S(1)}, f32[4,16,128]{2,1,0:T(8,128)S(1)}, u32[]{:S(2)}, u32[]{:S(2)}) collective-permute-start(f32[4,16,128]{2,1,0:T(8,128)S(1)} %get-tuple-element.58), channel_id=1, source_target_pairs={{0,12},{1,13},{2,14},{3,15},{4,16},{5,17},{6,18},{7,19},{8,20},{9,... | collective-permute-start | bytes 98312 | tf_op jit(solution)/shard_map/ppermute | solution.py:331
  47.3 8.8 %collective-permute-start.10 = (f32[4,16,128]{2,1,0:T(8,128)S(1)}, f32[4,16,128]{2,1,0:T(8,128)S(1)}, u32[]{:S(2)}, u32[]{:S(2)}) collective-permute-start(f32[4,16,128]{2,1,0:T(8,128)S(1)} %get-tuple-element.59), channel_id=1, source_target_pairs={{0,16},{1,17},{2,18},{3,19},{4,20},{5,21},{6,22},{7,23},{8,24},{9,... | collective-permute-start | bytes 98312 | tf_op jit(solution)/shard_map/ppermute | solution.py:331
  48.7 7.3 %collective-permute-start.11 = (f32[4,16,128]{2,1,0:T(8,128)S(1)}, f32[4,16,128]{2,1,0:T(8,128)S(1)}, u32[]{:S(2)}, u32[]{:S(2)}) collective-permute-start(f32[4,16,128]{2,1,0:T(8,128)S(1)} %get-tuple-element.60), channel_id=1, source_target_pairs={{0,20},{1,21},{2,22},{3,23},{4,24},{5,25},{6,26},{7,27},{8,28},{9,... | collective-permute-start | bytes 98312 | tf_op jit(solution)/shard_map/ppermute | solution.py:331
  51.8 6.4 %collective-permute-start.12 = (f32[4,16,128]{2,1,0:T(8,128)S(1)}, f32[4,16,128]{2,1,0:T(8,128)S(1)}, u32[]{:S(2)}, u32[]{:S(2)}) collective-permute-start(f32[4,16,128]{2,1,0:T(8,128)S(1)} %get-tuple-element.61), channel_id=1, source_target_pairs={{0,24},{1,25},{2,26},{3,27},{4,28},{5,29},{6,30},{7,31},{8,0},{9,1... | collective-permute-start | bytes 98312 | tf_op jit(solution)/shard_map/ppermute | solution.py:331
  55.0 3.9 %collective-permute-start.13 = (f32[4,16,128]{2,1,0:T(8,128)S(1)}, f32[4,16,128]{2,1,0:T(8,128)S(1)}, u32[]{:S(2)}, u32[]{:S(2)}) collective-permute-start(f32[4,16,128]{2,1,0:T(8,128)S(1)} %get-tuple-element.62), channel_id=1, source_target_pairs={{0,28},{1,29},{2,30},{3,31},{4,0},{5,1},{6,2},{7,3},{8,4},{9,5},{1... | collective-permute-start | bytes 98312 | tf_op jit(solution)/shard_map/ppermute | solution.py:331
  61.5 32.7 %all-to-all-start.1 = ((f32[32,2,16,128]{3,2,1,0:T(8,128)}), f32[32,2,16,128]{3,2,1,0:T(8,128)S(1)}, u32[]{:S(2)}, u32[]{:S(2)}) async-start(f32[32,2,16,128]{3,2,1,0:T(8,128)} %column_solve.1), calls=%async_computation.1 | async-start | bytes 1048576 | tf_op jit(solution)/shard_map/all_to_all | solution.py:322
  68.1 4.0 %collective-permute-start.15 = (f32[8,16,128]{2,1,0:T(8,128)S(1)}, f32[8,16,128]{2,1,0:T(8,128)S(1)}, u32[]{:S(2)}, u32[]{:S(2)}) collective-permute-start(f32[8,16,128]{2,1,0:T(8,128)S(1)} %get-tuple-element.65), channel_id=1, source_target_pairs={{0,2},{1,3},{2,0},{3,1},{4,6},{5,7},{6,4},{7,5},{8,10},{9,11},{10,... | collective-permute-start | bytes 196616 | tf_op jit(solution)/shard_map/ppermute | solution.py:328
  69.6 6.2 %collective-permute-start.16 = (f32[8,16,128]{2,1,0:T(8,128)S(1)}, f32[8,16,128]{2,1,0:T(8,128)S(1)}, u32[]{:S(2)}, u32[]{:S(2)}) collective-permute-start(f32[8,16,128]{2,1,0:T(8,128)S(1)} %get-tuple-element.66), channel_id=1, source_target_pairs={{0,3},{1,2},{2,1},{3,0},{4,7},{5,6},{6,5},{7,4},{8,11},{9,10},{10,... | collective-permute-start | bytes 196616 | tf_op jit(solution)/shard_map/ppermute | solution.py:328
  75.8 11.2 %collective-permute-start.17 = (f32[4,16,128]{2,1,0:T(8,128)S(1)}, f32[4,16,128]{2,1,0:T(8,128)S(1)}, u32[]{:S(2)}, u32[]{:S(2)}) collective-permute-start(f32[4,16,128]{2,1,0:T(8,128)S(1)} %get-tuple-element.68), channel_id=1, source_target_pairs={{0,4},{1,5},{2,6},{3,7},{4,8},{5,9},{6,10},{7,11},{8,12},{9,13},{1... | collective-permute-start | bytes 98312 | tf_op jit(solution)/shard_map/ppermute | solution.py:331
  77.4 12.9 %collective-permute-start.18 = (f32[4,16,128]{2,1,0:T(8,128)S(1)}, f32[4,16,128]{2,1,0:T(8,128)S(1)}, u32[]{:S(2)}, u32[]{:S(2)}) collective-permute-start(f32[4,16,128]{2,1,0:T(8,128)S(1)} %get-tuple-element.69), channel_id=1, source_target_pairs={{0,8},{1,9},{2,10},{3,11},{4,12},{5,13},{6,14},{7,15},{8,16},{9,17... | collective-permute-start | bytes 98312 | tf_op jit(solution)/shard_map/ppermute | solution.py:331
  79.3 12.0 %collective-permute-start.19 = (f32[4,16,128]{2,1,0:T(8,128)S(1)}, f32[4,16,128]{2,1,0:T(8,128)S(1)}, u32[]{:S(2)}, u32[]{:S(2)}) collective-permute-start(f32[4,16,128]{2,1,0:T(8,128)S(1)} %get-tuple-element.70), channel_id=1, source_target_pairs={{0,12},{1,13},{2,14},{3,15},{4,16},{5,17},{6,18},{7,19},{8,20},{9,... | collective-permute-start | bytes 98312 | tf_op jit(solution)/shard_map/ppermute | solution.py:331
  82.5 8.8 %collective-permute-start.20 = (f32[4,16,128]{2,1,0:T(8,128)S(1)}, f32[4,16,128]{2,1,0:T(8,128)S(1)}, u32[]{:S(2)}, u32[]{:S(2)}) collective-permute-start(f32[4,16,128]{2,1,0:T(8,128)S(1)} %get-tuple-element.71), channel_id=1, source_target_pairs={{0,16},{1,17},{2,18},{3,19},{4,20},{5,21},{6,22},{7,23},{8,24},{9,... | collective-permute-start | bytes 98312 | tf_op jit(solution)/shard_map/ppermute | solution.py:331
  84.0 7.3 %collective-permute-start.21 = (f32[4,16,128]{2,1,0:T(8,128)S(1)}, f32[4,16,128]{2,1,0:T(8,128)S(1)}, u32[]{:S(2)}, u32[]{:S(2)}) collective-permute-start(f32[4,16,128]{2,1,0:T(8,128)S(1)} %get-tuple-element.72), channel_id=1, source_target_pairs={{0,20},{1,21},{2,22},{3,23},{4,24},{5,25},{6,26},{7,27},{8,28},{9,... | collective-permute-start | bytes 98312 | tf_op jit(solution)/shard_map/ppermute | solution.py:331
  87.0 6.4 %collective-permute-start.22 = (f32[4,16,128]{2,1,0:T(8,128)S(1)}, f32[4,16,128]{2,1,0:T(8,128)S(1)}, u32[]{:S(2)}, u32[]{:S(2)}) collective-permute-start(f32[4,16,128]{2,1,0:T(8,128)S(1)} %get-tuple-element.73), channel_id=1, source_target_pairs={{0,24},{1,25},{2,26},{3,27},{4,28},{5,29},{6,30},{7,31},{8,0},{9,1... | collective-permute-start | bytes 98312 | tf_op jit(solution)/shard_map/ppermute | solution.py:331
  90.3 3.9 %collective-permute-start.23 = (f32[4,16,128]{2,1,0:T(8,128)S(1)}, f32[4,16,128]{2,1,0:T(8,128)S(1)}, u32[]{:S(2)}, u32[]{:S(2)}) collective-permute-start(f32[4,16,128]{2,1,0:T(8,128)S(1)} %get-tuple-element.74), channel_id=1, source_target_pairs={{0,28},{1,29},{2,30},{3,31},{4,0},{5,1},{6,2},{7,3},{8,4},{9,5},{1... | collective-permute-start | bytes 98312 | tf_op jit(solution)/shard_map/ppermute | solution.py:331
  (7 other events, 28.2 us)

commit v3 on v1

v3 whole, which is shorter than its diff:
```python
import jax
import jax.numpy as jnp
from jax import lax
from jax.experimental import pallas as pl
from jax.experimental.pallas import tpu as pltpu
from jax.sharding import PartitionSpec as P

TRANSPORT_PART = 0.25
CONDUCTION_PART = 0.2
LANES = 128
EDGE = 53
PREP = 46
VMEM = pl.BlockSpec(memory_space=pltpu.VMEM)
HBM = pl.BlockSpec(memory_space=pltpu.HBM)
SMEM = pl.BlockSpec(memory_space=pltpu.SMEM)


def metric_of(levels, extent):
    return 0.5 / (1.0 + jnp.sin(jnp.pi * (levels + 0.5) / extent))


def halves(wide):
    high = wide.astype(jnp.bfloat16)
    return high, (wide - high.astype(jnp.float32)).astype(jnp.bfloat16)


def edge_kernel(here_ref, t_hbm, yc_ref, yd_ref, za_ref, zb_ref, buf, sems):
    planes, rows, _ = t_hbm.shape
    half = buf.shape[2]
    pencil_even, slab_even = here_ref[0] % 2 == 0, here_ref[1] % 2 == 0
    copies = [
        pltpu.make_async_copy(t_hbm.at[:, pl.ds(0, half)], buf.at[0], sems.at[0]),
        pltpu.make_async_copy(t_hbm.at[:, pl.ds(rows - half, half)], buf.at[1], sems.at[1]),
        pltpu.make_async_copy(t_hbm.at[jnp.where(slab_even, planes - 1, 0)], yc_ref, sems.at[2]),
        pltpu.make_async_copy(t_hbm.at[jnp.where(slab_even, 0, planes - 1)], yd_ref, sems.at[3]),
    ]
    for copy in copies:
        copy.start()
    copies[0].wait()
    copies[1].wait()
    for y in range(planes):
        low, high = buf[0, y, :1, :], buf[1, y, half - 1 :, :]
        za_ref[y : y + 1, :] = jnp.where(pencil_even, high, low)
        zb_ref[y : y + 1, :] = jnp.where(pencil_even, low, high)
    copies[2].wait()
    copies[3].wait()


def edges(here, t):
    planes, rows, nx = t.shape
    half = 8
    plane = jax.ShapeDtypeStruct((rows, nx), t.dtype)
    level = jax.ShapeDtypeStruct((planes, nx), t.dtype)
    return pl.pallas_call(
        edge_kernel,
        in_specs=[SMEM, HBM],
        out_specs=[VMEM] * 4,
        out_shape=[plane, plane, level, level],
        scratch_shapes=[pltpu.VMEM((2, planes, half, nx), t.dtype), pltpu.SemaphoreType.DMA((4,))],
        compiler_params=pltpu.CompilerParams(vmem_limit_bytes=EDGE * 2**20),
        name="edges",
    )(here, t)


def prepare_kernel(here_ref, a_hbm, ah_ref, al_ref, g_ref, a_buf, sems):
    parts = sems.shape[0]
    a_rows = a_buf.shape[0] // parts
    copies = []
    for i in range(parts):
        cut = slice(i * a_rows, (i + 1) * a_rows)
        copies.append(pltpu.make_async_copy(a_hbm.at[cut], a_buf.at[cut], sems.at[i]))
    for copy in copies:
        copy.start()
    rows, lanes = g_ref.shape
    levels = (lax.broadcasted_iota(jnp.int32, (rows, lanes), 0) + here_ref[0] * rows).astype(jnp.float32)
    g_ref[...] = metric_of(levels, (here_ref[2] * rows).astype(jnp.float32))
    for i in range(parts):
        cut = slice(i * a_rows, (i + 1) * a_rows)
        copies[i].wait()
        ah_ref[cut], al_ref[cut] = halves(a_buf[cut])


def prepare(here, a, rows):
    a16 = jax.ShapeDtypeStruct(a.shape, jnp.bfloat16)
    parts = 4
    return pl.pallas_call(
        prepare_kernel,
        in_specs=[SMEM, HBM],
        out_specs=[VMEM] * 3,
        out_shape=[a16, a16, jax.ShapeDtypeStruct((rows, LANES), jnp.float32)],
        scratch_shapes=[pltpu.VMEM(a.shape, a.dtype), pltpu.SemaphoreType.DMA((parts,))],
        compiler_params=pltpu.CompilerParams(vmem_limit_bytes=PREP * 2**20),
        cost_estimate=pl.CostEstimate(flops=4 * a.size, bytes_accessed=8 * a.size, transcendentals=0),
        name="prepare",
    )(here, a)


def row_kernel(
    here_ref, t_ref, u_ref, v_ref, w_ref, yc_ref, yd_ref, za_ref, zb_ref, g_ref, ah_ref, al_ref, out_ref, rh, rl
):
    planes, rows, nx = t_ref.shape
    metric = jnp.concatenate([g_ref[...]] * (nx // LANES), axis=1)
    pencil_even, slab_even = here_ref[0] % 2 == 0, here_ref[1] % 2 == 0
    over = jnp.where(pencil_even, za_ref[...], zb_ref[...])
    under = jnp.where(pencil_even, zb_ref[...], za_ref[...])
    level = lax.broadcasted_iota(jnp.int32, (rows, nx), 0)
    for y in range(planes):
        t = t_ref[y]
        ahead = t_ref[y + 1] if y + 1 < planes else jnp.where(slab_even, yc_ref[...], yd_ref[...])
        behind = t_ref[y - 1] if y else jnp.where(slab_even, yd_ref[...], yc_ref[...])
        east = pltpu.roll(t, nx - 1, 1)
        west = pltpu.roll(t, 1, 1)
        above = jnp.where(level == rows - 1, over[y : y + 1, :], pltpu.roll(t, rows - 1, 0))
        below = jnp.where(level == 0, under[y : y + 1, :], pltpu.roll(t, 1, 0))
        u = u_ref[y].astype(jnp.float32)
        v = v_ref[y].astype(jnp.float32)
        w = w_ref[y].astype(jnp.float32)
        carried = 0.5 * u * (east - west) + 0.5 * v * (ahead - behind) + w * metric * (above - below)
        conducted = (
            (ahead - 2.0 * t + behind)
            + 0.5 * (east - 2.0 * t + west)
            + 0.5 * metric * (above - 2.0 * t + below)
        )
        side = t - TRANSPORT_PART * carried + CONDUCTION_PART * conducted
        rh[y * rows : (y + 1) * rows, :], rl[y * rows : (y + 1) * rows, :] = halves(side)
    wide = 2 * LANES
    unit_rows = 3 * rows
    blocks = nx // LANES
    for c in range(nx // wide):
        ah = ah_ref[c * wide : (c + 1) * wide, :]
        al = al_ref[c * wide : (c + 1) * wide, :]

        def dot(x, m):
            return lax.dot_general(x, m, (((1,), (1,)), ((), ())), preferred_element_type=jnp.float32)

        solved = dot(rh[...], ah) + (dot(rh[...], al) + dot(rl[...], ah))
        for q in range(planes // 3):
            for h in range(2):
                piece = solved[q * unit_rows : (q + 1) * unit_rows, h * LANES : (h + 1) * LANES]
                out_ref[q * blocks + 2 * c + h] = piece.reshape(3, rows, LANES)


def row_solve(here, t, u, v, w, halos, metric, ah, al, groups):
    planes, rows, nx = t.shape
    return pl.pallas_call(
        row_kernel,
        in_specs=[SMEM] + [VMEM] * 11,
        out_specs=VMEM,
        out_shape=jax.ShapeDtypeStruct((groups, 3, rows, LANES), jnp.float32),
        scratch_shapes=[pltpu.VMEM((planes * rows, nx), jnp.bfloat16)] * 2,
        compiler_params=pltpu.CompilerParams(vmem_limit_bytes=32 * 2**20),
        cost_estimate=pl.CostEstimate(
            flops=6 * planes * rows * nx * nx, bytes_accessed=8 * 2**20, transcendentals=0
        ),
        name="row_solve",
    )(here, t, u, v, w, *halos, metric, ah, al)


def column_kernel(here_ref, seg_ref, w_ref, x_ref, out_ref):
    groups, units, rows, lanes = x_ref.shape
    column = lax.broadcasted_iota(jnp.int32, (8, lanes), 1) + here_ref[0] % here_ref[3] * lanes
    crossed = jnp.zeros((8, lanes), jnp.int32)
    end = jnp.int32(0)
    for s in range(seg_ref.shape[0]):
        end = end + seg_ref[s]
        crossed = crossed + jnp.where(column >= end, 1, 0)
    insulated = jnp.concatenate([(crossed % 2)[:1, :]] * units, axis=1) == 1
    extent = groups * rows
    lines = jnp.concatenate([x_ref[:, i].reshape(extent, lanes) for i in range(units)], axis=1)
    xh, xl = halves(lines)
    both = jnp.concatenate([xh, xl], axis=1)
    width = units * lanes

    def solve(c, lo, hi):
        wh, wl = halves(w_ref[c, lo:hi, :])
        d = jnp.dot(wh, both, preferred_element_type=jnp.float32)
        e = jnp.dot(wl, xh, preferred_element_type=jnp.float32)
        return d[:, :width] + (d[:, width:] + e)

    step = 128
    for k in range(0, extent, step):
        solved = jnp.where(insulated, solve(1, k, k + step), solve(0, k, k + step))
        for i in range(units):
            out_ref[k // rows : (k + step) // rows, i] = solved[:, i * lanes : (i + 1) * lanes].reshape(
                step // rows, rows, lanes
            )


def column_solve(here, segments, w, x):
    return pl.pallas_call(
        column_kernel,
        in_specs=[SMEM, SMEM, VMEM, VMEM],
        out_specs=VMEM,
        out_shape=jax.ShapeDtypeStruct(x.shape, jnp.float32),
        compiler_params=pltpu.CompilerParams(vmem_limit_bytes=32 * 2**20),
        cost_estimate=pl.CostEstimate(
            flops=12 * w.shape[1] * x.size, bytes_accessed=4 * 2**20, transcendentals=0
        ),
        name="column_solve",
    )(here, segments, w, x)


def place_kernel(x_ref, out_ref):
    groups = x_ref.shape[0]
    blocks = out_ref.shape[2] // LANES
    for p in range(groups):
        q, b = p // blocks, p % blocks
        out_ref[3 * q : 3 * q + 3, :, b * LANES : (b + 1) * LANES] = x_ref[p]


def place(x, shape):
    return pl.pallas_call(
        place_kernel,
        in_specs=[VMEM],
        out_specs=VMEM,
        out_shape=jax.ShapeDtypeStruct(shape, jnp.float32),
        compiler_params=pltpu.CompilerParams(vmem_limit_bytes=16 * 2**20),
        name="place",
    )(x)


def swapped(x):
    return lax.all_to_all(x, "pencil", split_axis=0, concat_axis=0, tiled=True)


def on_device(t, u, v, w, downstream_solver_matrix, wallward_solver_matrices, wall_segments):
    planes, rows, nx = t.shape
    slabs, groups = lax.axis_size("slab"), lax.axis_size("pencil")
    here = jnp.stack(
        [
            lax.axis_index("pencil").astype(jnp.int32),
            lax.axis_index("slab").astype(jnp.int32),
            jnp.int32(groups),
            jnp.int32(nx // LANES),
        ]
    )
    yc, yd, za, zb = edges(here, t)
    halos = (
        lax.ppermute(yc, "slab", [(i, i ^ 1) for i in range(slabs)]),
        lax.ppermute(yd, "slab", [(i, ((i - 1) ^ 1) + 1 & slabs - 1) for i in range(slabs)]),
        lax.ppermute(za, "pencil", [(i, i ^ 1) for i in range(groups)]),
        lax.ppermute(zb, "pencil", [(i, ((i - 1) ^ 1) + 1) for i in range(1, groups - 1)]),
    )
    ah, al, metric = prepare(here, downstream_solver_matrix, rows)
    x = swapped(row_solve(here, t, u, v, w, halos, metric, ah, al, groups))
    x = swapped(column_solve(here, wall_segments, wallward_solver_matrices, x))
    return place(x, t.shape)


def solution(mesh):
    field = P("slab", "pencil", None)
    return jax.shard_map(
        on_device,
        mesh=mesh,
        in_specs=(field, field, field, field, P(), P(), P()),
        out_specs=field,
        check_vma=False,
    )
```

time: 83.8 us -> 81.6 us (0.974)
  starting transfers between devices: 12.2 us -> 10.6 us
  Pallas kernels: 10.2 us -> 11.4 us
  blocking collectives: 60.3 us -> 59.3 us
    ppermute x4, starting transfers between devices: 12.2 us -> 10.6 us  [the longest x1 3.83 us: on_device(): lax.ppermute(yc, 'slab', [(i, i ^ 1) for i in range(slabs)])]
    pallas_call x4, Pallas kernels: 9.31 us -> 10.4 us  [the longest x1 3.66 us: row_solve(): pl.pallas_call(row_kernel, in_specs=[SMEM] + [VMEM] * 11, out_specs=VMEM,...]
    all_to_all x2, blocking collectives: 60.3 us -> 59.3 us  [swapped(): return lax.all_to_all(x, 'pencil', split_axis=0, concat_axis=0, tiled=True)]
where the time goes in v3:
time: 81.6 us; the launch traced here: 81.4 us
  blocking collectives  59.3 us (73%)
  Pallas kernels  11.4 us (14%)
  starting transfers between devices  10.6 us (13%)
    all_to_all x2, blocking collectives, swapped(): return lax.all_to_all(x, 'pencil', split_axis=0, concat_axis=0, tiled=True)  59.3 us
    ppermute x1, starting transfers between devices, on_device(): lax.ppermute(yc, 'slab', [(i, i ^ 1) for i in range(slabs)])  3.83 us
    pallas_call x1, Pallas kernels, row_solve(): pl.pallas_call(row_kernel, in_specs=[SMEM] + [VMEM] * 11, out_specs=VMEM,...  3.66 us
    ppermute x1, starting transfers between devices, on_device(): lax.ppermute(zb, 'pencil', [(i, (i - 1 ^ 1) + 1) for i in range(1, groups...  3.24 us
    pallas_call x1, Pallas kernels, prepare(): pl.pallas_call(prepare_kernel, in_specs=[SMEM, HBM], out_specs=[VMEM] * 3...  2.89 us
    ppermute x1, starting transfers between devices, on_device(): lax.ppermute(yd, 'slab', [(i, (i - 1 ^ 1) + 1 & slabs - 1) for i in range...  2.29 us
    pallas_call x1, Pallas kernels, column_solve(): pl.pallas_call(column_kernel, in_specs=[SMEM, SMEM, VMEM, VMEM], out_spec...  2.17 us
    pallas_call x1, Pallas kernels, edges(): pl.pallas_call(edge_kernel, in_specs=[SMEM, HBM], out_specs=[VMEM] * 4, o...  1.72 us
  transfers between devices with their start and end apart: 4, of which 0 were waited for; matrix products, arithmetic and copies ran while one was open for 0% of the time, Pallas kernels for 4%

profile of v3, /device:TPU:1, one launch (start us, length us, event | category | flops | bytes accessed | tf_op | source)
XLA Modules:
  0.0 81.4 jit_solution(14873522796504202597)
XLA Ops:
  0.0 0.1 pad_add_fusion.here_ref
  0.1 1.7 %edges.1 = (f32[16,1024]{1,0:T(8,128)S(1)}, f32[16,1024]{1,0:T(8,128)S(1)}, f32[12,1024]{1,0:T(8,128)S(1)}, f32[12,1024]{1,0:T(8,128)S(1)}) custom-call(s32[4]{0:T(128)S(1)} %pad_add_fusion.here_ref, f32[12,16,1024]{2,1,0:T(8,128)} %t_ref.1), custom_call_target="tpu_custom_call" | custom-call | tf_op jit(solution)/shard_map/edges/pallas_call | solution.py:54
  1.8 3.8 %collective-permute-start = (f32[16,1024]{1,0:T(8,128)S(1)}, f32[16,1024]{1,0:T(8,128)S(1)}, u32[]{:S(2)}, u32[]{:S(2)}) collective-permute-start(f32[16,1024]{1,0:T(8,128)S(1)} %get-tuple-element.12), channel_id=1, source_target_pairs={{0,32},{32,0},{64,96},{96,64},{128,160},{160,128},{192,224},{224,1... | collective-permute-start | bytes 196616 | tf_op jit(solution)/shard_map/ppermute | solution.py:239
  5.6 2.3 %collective-permute-start.1 = (f32[16,1024]{1,0:T(8,128)S(1)}, f32[16,1024]{1,0:T(8,128)S(1)}, u32[]{:S(2)}, u32[]{:S(2)}) collective-permute-start(f32[16,1024]{1,0:T(8,128)S(1)} %get-tuple-element.13), channel_id=1, source_target_pairs={{0,224},{32,64},{64,32},{96,128},{128,96},{160,192},{192,160},{224... | collective-permute-start | bytes 196616 | tf_op jit(solution)/shard_map/ppermute | solution.py:240
  7.9 1.2 %collective-permute-start.2 = (f32[12,1024]{1,0:T(8,128)S(1)}, f32[12,1024]{1,0:T(8,128)S(1)}, u32[]{:S(2)}, u32[]{:S(2)}) collective-permute-start(f32[12,1024]{1,0:T(8,128)S(1)} %get-tuple-element.14), channel_id=1, source_target_pairs={{0,1},{1,0},{2,3},{3,2},{4,5},{5,4},{6,7},{7,6},{8,9},{9,8},{10,11... | collective-permute-start | bytes 147464 | tf_op jit(solution)/shard_map/ppermute | solution.py:241
  9.1 3.2 %collective-permute-start.3 = (f32[12,1024]{1,0:T(8,128)S(1)}, f32[12,1024]{1,0:T(8,128)S(1)}, u32[]{:S(2)}, u32[]{:S(2)}) collective-permute-start(f32[12,1024]{1,0:T(8,128)S(1)} %get-tuple-element.15), channel_id=1, source_target_pairs={{1,2},{2,1},{3,4},{4,3},{5,6},{6,5},{7,8},{8,7},{9,10},{10,9},{11,... | collective-permute-start | bytes 147464 | tf_op jit(solution)/shard_map/ppermute | solution.py:242
  12.4 2.9 %prepare.1 = (bf16[1024,1024]{1,0:T(8,128)(2,1)S(1)}, bf16[1024,1024]{1,0:T(8,128)(2,1)S(1)}, f32[16,128]{1,0:T(8,128)S(1)}) custom-call(s32[4]{0:T(128)S(1)} %pad_add_fusion.here_ref, f32[1024,1024]{1,0:T(8,128)} %a_hbm.1), custom_call_target="tpu_custom_call" | custom-call | flops 4194304 | bytes 8388608 | tf_op jit(solution)/shard_map/prepare/pallas_call | solution.py:86
  15.3 0.0 collective-permute-done.2.za_ref
  15.3 0.0 collective-permute-done.3.zb_ref
  15.3 0.0 collective-permute-done.yc_ref
  15.3 0.0 collective-permute-done.1.yd_ref
  15.3 0.0 copy-done
  15.3 0.0 copy-done.1
  15.3 0.0 copy-done.2
  15.3 0.0 copy-done.3
  15.4 0.0 copy-start.4
  15.4 0.0 copy-start.5
  15.4 3.7 %row_solve.1 = f32[32,3,16,128]{3,2,1,0:T(8,128)S(1)} custom-call(s32[4]{0:T(128)S(1)} %pad_add_fusion.here_ref, f32[12,16,1024]{2,1,0:T(8,128)S(1)} %copy-done, bf16[12,16,1024]{2,1,0:T(8,128)(2,1)S(1)} %copy-done.1, bf16[12,16,1024]{2,1,0:T(8,128)(2,1)S(1)} %copy-done.2, bf16[12,16,1024]{2,1,0:T(8,128)(2,1)S(1)} %copy-done.3, ...), custom_call_target="tpu_custom_call" | custom-call | flops 1207959552 | bytes 8388608 | tf_op jit(solution)/shard_map/row_solve/pallas_call | solution.py:145
  19.0 32.7 %all_to_all.10.x_ref = f32[32,3,16,128]{3,2,1,0:T(8,128)S(1)} all-to-all(f32[32,3,16,128]{3,2,1,0:T(8,128)S(1)} %row_solve.1), channel_id=1, replica_groups=mesh['slab'=8,'pencil'=32] {'pencil'}, dimensions={0} | all-to-all | bytes 1572864 | tf_op jit(solution)/shard_map/all_to_all | solution.py:223
  51.7 0.0 copy-done.4
  51.7 0.0 copy-done.5
  51.7 2.2 %column_solve.1 = f32[32,3,16,128]{3,2,1,0:T(8,128)S(1)} custom-call(s32[4]{0:T(128)S(1)} %pad_add_fusion.here_ref, s32[16]{0:T(128)S(1)} %copy-done.5, f32[2,512,512]{2,1,0:T(8,128)S(1)} %copy-done.4, f32[32,3,16,128]{3,2,1,0:T(8,128)S(1)} %all_to_all.10.x_ref), custom_call_target="tpu_custom_call" | custom-call | flops 1207959552 | bytes 4194304 | tf_op jit(solution)/shard_map/column_solve/pallas_call | solution.py:190
  53.9 26.6 %all_to_all.11.x_ref = f32[32,3,16,128]{3,2,1,0:T(8,128)S(1)} all-to-all(f32[32,3,16,128]{3,2,1,0:T(8,128)S(1)} %column_solve.1), channel_id=1, replica_groups=mesh['slab'=8,'pencil'=32] {'pencil'}, dimensions={0} | all-to-all | bytes 1572864 | tf_op jit(solution)/shard_map/all_to_all | solution.py:223
  80.5 0.9 %place.1 = f32[12,16,1024]{2,1,0:T(8,128)} custom-call(f32[32,3,16,128]{3,2,1,0:T(8,128)S(1)} %all_to_all.11.x_ref), custom_call_target="tpu_custom_call" | custom-call | tf_op jit(solution)/shard_map/place/pallas_call | solution.py:212
  (4 shorter events, 0.0 us)
Async XLA Ops:
  1.8 13.5 %collective-permute-start = (f32[16,1024]{1,0:T(8,128)S(1)}, f32[16,1024]{1,0:T(8,128)S(1)}, u32[]{:S(2)}, u32[]{:S(2)}) collective-permute-start(f32[16,1024]{1,0:T(8,128)S(1)} %get-tuple-element.12), channel_id=1, source_target_pairs={{0,32},{32,0},{64,96},{96,64},{128,160},{160,128},{192,224},{224,1... | collective-permute-start | bytes 196616 | tf_op jit(solution)/shard_map/ppermute | solution.py:239
  5.6 9.7 %collective-permute-start.1 = (f32[16,1024]{1,0:T(8,128)S(1)}, f32[16,1024]{1,0:T(8,128)S(1)}, u32[]{:S(2)}, u32[]{:S(2)}) collective-permute-start(f32[16,1024]{1,0:T(8,128)S(1)} %get-tuple-element.13), channel_id=1, source_target_pairs={{0,224},{32,64},{64,32},{96,128},{128,96},{160,192},{192,160},{224... | collective-permute-start | bytes 196616 | tf_op jit(solution)/shard_map/ppermute | solution.py:240
  7.9 7.3 %collective-permute-start.2 = (f32[12,1024]{1,0:T(8,128)S(1)}, f32[12,1024]{1,0:T(8,128)S(1)}, u32[]{:S(2)}, u32[]{:S(2)}) collective-permute-start(f32[12,1024]{1,0:T(8,128)S(1)} %get-tuple-element.14), channel_id=1, source_target_pairs={{0,1},{1,0},{2,3},{3,2},{4,5},{5,4},{6,7},{7,6},{8,9},{9,8},{10,11... | collective-permute-start | bytes 147464 | tf_op jit(solution)/shard_map/ppermute | solution.py:241
  9.1 6.2 %copy-start = (f32[12,16,1024]{2,1,0:T(8,128)S(1)}, f32[12,16,1024]{2,1,0:T(8,128)}, u32[]{:S(2)}) copy-start(f32[12,16,1024]{2,1,0:T(8,128)} %t_ref.1) | copy-start | bytes 2359300
  9.1 6.2 %copy-start.1 = (bf16[12,16,1024]{2,1,0:T(8,128)(2,1)S(1)}, bf16[12,16,1024]{2,1,0:T(8,128)(2,1)}, u32[]{:S(2)}) copy-start(bf16[12,16,1024]{2,1,0:T(8,128)(2,1)} %u_ref.1) | copy-start | bytes 1179652
  9.1 6.2 %copy-start.2 = (bf16[12,16,1024]{2,1,0:T(8,128)(2,1)S(1)}, bf16[12,16,1024]{2,1,0:T(8,128)(2,1)}, u32[]{:S(2)}) copy-start(bf16[12,16,1024]{2,1,0:T(8,128)(2,1)} %v_ref.1) | copy-start | bytes 1179652
  9.1 6.2 %copy-start.3 = (bf16[12,16,1024]{2,1,0:T(8,128)(2,1)S(1)}, bf16[12,16,1024]{2,1,0:T(8,128)(2,1)}, u32[]{:S(2)}) copy-start(bf16[12,16,1024]{2,1,0:T(8,128)(2,1)} %w_ref.2) | copy-start | bytes 1179652
  9.1 6.2 %collective-permute-start.3 = (f32[12,1024]{1,0:T(8,128)S(1)}, f32[12,1024]{1,0:T(8,128)S(1)}, u32[]{:S(2)}, u32[]{:S(2)}) collective-permute-start(f32[12,1024]{1,0:T(8,128)S(1)} %get-tuple-element.15), channel_id=1, source_target_pairs={{1,2},{2,1},{3,4},{4,3},{5,6},{6,5},{7,8},{8,7},{9,10},{10,9},{11,... | collective-permute-start | bytes 147464 | tf_op jit(solution)/shard_map/ppermute | solution.py:242
  15.4 36.4 %copy-start.4 = (f32[2,512,512]{2,1,0:T(8,128)S(1)}, f32[2,512,512]{2,1,0:T(8,128)}, u32[]{:S(2)}) copy-start(f32[2,512,512]{2,1,0:T(8,128)} %w_ref.3) | copy-start | bytes 6291460
  15.4 36.4 %copy-start.5 = (s32[16]{0:T(128)S(1)}, s32[16]{0:T(128)}, u32[]{:S(2)}) copy-start(s32[16]{0:T(128)} %seg_ref.1) | copy-start | bytes 196

commit v4 on v3

--- a/solution.py
+++ b/solution.py
@@ -1,3 +1,5 @@
+import functools
+
 import jax
 import jax.numpy as jnp
 from jax import lax
@@ -24,10 +26,10 @@
     return high, (wide - high.astype(jnp.float32)).astype(jnp.bfloat16)
 
 
-def edge_kernel(here_ref, t_hbm, yc_ref, yd_ref, za_ref, zb_ref, buf, sems):
+def edge_kernel(groups, here_ref, t_hbm, yc_ref, yd_ref, za_ref, zb_ref, buf, sems):
     planes, rows, _ = t_hbm.shape
     half = buf.shape[2]
-    pencil_even, slab_even = here_ref[0] % 2 == 0, here_ref[1] % 2 == 0
+    pencil_even, slab_even = here_ref[0] % 2 == 0, here_ref[0] // groups % 2 == 0
     copies = [
         pltpu.make_async_copy(t_hbm.at[:, pl.ds(0, half)], buf.at[0], sems.at[0]),
         pltpu.make_async_copy(t_hbm.at[:, pl.ds(rows - half, half)], buf.at[1], sems.at[1]),
@@ -46,13 +48,13 @@
     copies[3].wait()
 
 
-def edges(here, t):
+def edges(here, t, groups):
     planes, rows, nx = t.shape
     half = 8
     plane = jax.ShapeDtypeStruct((rows, nx), t.dtype)
     level = jax.ShapeDtypeStruct((planes, nx), t.dtype)
     return pl.pallas_call(
-        edge_kernel,
+        functools.partial(edge_kernel, groups),
         in_specs=[SMEM, HBM],
         out_specs=[VMEM] * 4,
         out_shape=[plane, plane, level, level],
@@ -62,7 +64,7 @@
     )(here, t)
 
 
-def prepare_kernel(here_ref, a_hbm, ah_ref, al_ref, g_ref, a_buf, sems):
+def prepare_kernel(groups, here_ref, a_hbm, ah_ref, al_ref, g_ref, a_buf, sems):
     parts = sems.shape[0]
     a_rows = a_buf.shape[0] // parts
     copies = []
@@ -72,19 +74,19 @@
     for copy in copies:
         copy.start()
     rows, lanes = g_ref.shape
-    levels = (lax.broadcasted_iota(jnp.int32, (rows, lanes), 0) + here_ref[0] * rows).astype(jnp.float32)
-    g_ref[...] = metric_of(levels, (here_ref[2] * rows).astype(jnp.float32))
+    levels = (lax.broadcasted_iota(jnp.int32, (rows, lanes), 0) + here_ref[0] % groups * rows).astype(jnp.float32)
+    g_ref[...] = metric_of(levels, groups * rows)
     for i in range(parts):
         cut = slice(i * a_rows, (i + 1) * a_rows)
         copies[i].wait()
         ah_ref[cut], al_ref[cut] = halves(a_buf[cut])
 
 
-def prepare(here, a, rows):
+def prepare(here, a, rows, groups):
     a16 = jax.ShapeDtypeStruct(a.shape, jnp.bfloat16)
     parts = 4
     return pl.pallas_call(
-        prepare_kernel,
+        functools.partial(prepare_kernel, groups),
         in_specs=[SMEM, HBM],
         out_specs=[VMEM] * 3,
         out_shape=[a16, a16, jax.ShapeDtypeStruct((rows, LANES), jnp.float32)],
@@ -100,7 +102,8 @@
 ):
     planes, rows, nx = t_ref.shape
     metric = jnp.concatenate([g_ref[...]] * (nx // LANES), axis=1)
-    pencil_even, slab_even = here_ref[0] % 2 == 0, here_ref[1] % 2 == 0
+    groups = out_ref.shape[0]
+    pencil_even, slab_even = here_ref[0] % 2 == 0, here_ref[0] // groups % 2 == 0
     over = jnp.where(pencil_even, za_ref[...], zb_ref[...])
     under = jnp.where(pencil_even, zb_ref[...], za_ref[...])
     level = lax.broadcasted_iota(jnp.int32, (rows, nx), 0)
@@ -156,9 +159,9 @@
     )(here, t, u, v, w, *halos, metric, ah, al)
 
 
-def column_kernel(here_ref, seg_ref, w_ref, x_ref, out_ref):
+def column_kernel(blocks, here_ref, seg_ref, w_ref, x_ref, out_ref):
     groups, units, rows, lanes = x_ref.shape
-    column = lax.broadcasted_iota(jnp.int32, (8, lanes), 1) + here_ref[0] % here_ref[3] * lanes
+    column = lax.broadcasted_iota(jnp.int32, (8, lanes), 1) + here_ref[0] % blocks * lanes
     crossed = jnp.zeros((8, lanes), jnp.int32)
     end = jnp.int32(0)
     for s in range(seg_ref.shape[0]):
@@ -186,9 +189,9 @@
             )
 
 
-def column_solve(here, segments, w, x):
-    return pl.pallas_call(
-        column_kernel,
+def column_solve(here, segments, w, x, blocks):
+    return pl.pallas_call(
+        functools.partial(column_kernel, blocks),
         in_specs=[SMEM, SMEM, VMEM, VMEM],
         out_specs=VMEM,
         out_shape=jax.ShapeDtypeStruct(x.shape, jnp.float32),
@@ -226,24 +229,17 @@
 def on_device(t, u, v, w, downstream_solver_matrix, wallward_solver_matrices, wall_segments):
     planes, rows, nx = t.shape
     slabs, groups = lax.axis_size("slab"), lax.axis_size("pencil")
-    here = jnp.stack(
-        [
-            lax.axis_index("pencil").astype(jnp.int32),
-            lax.axis_index("slab").astype(jnp.int32),
-            jnp.int32(groups),
-            jnp.int32(nx // LANES),
-        ]
-    )
-    yc, yd, za, zb = edges(here, t)
+    here = lax.axis_index(("slab", "pencil")).astype(jnp.int32).reshape(1)
+    yc, yd, za, zb = edges(here, t, groups)
     halos = (
         lax.ppermute(yc, "slab", [(i, i ^ 1) for i in range(slabs)]),
         lax.ppermute(yd, "slab", [(i, ((i - 1) ^ 1) + 1 & slabs - 1) for i in range(slabs)]),
         lax.ppermute(za, "pencil", [(i, i ^ 1) for i in range(groups)]),
         lax.ppermute(zb, "pencil", [(i, ((i - 1) ^ 1) + 1) for i in range(1, groups - 1)]),
     )
-    ah, al, metric = prepare(here, downstream_solver_matrix, rows)
+    ah, al, metric = prepare(here, downstream_solver_matrix, rows, groups)
     x = swapped(row_solve(here, t, u, v, w, halos, metric, ah, al, groups))
-    x = swapped(column_solve(here, wall_segments, wallward_solver_matrices, x))
+    x = swapped(column_solve(here, wall_segments, wallward_solver_matrices, x, nx // LANES))
     return place(x, t.shape)
 
 

time: 81.6 us -> 80.5 us (0.987)
  Pallas kernels: 11.4 us -> 9.74 us
    pallas_call x3, Pallas kernels: 6.78 us -> 5.69 us  [the longest x1 2.35 us: prepare(): pl.pallas_call(functools.partial(prepare_kernel, groups), in_specs=[SMEM,...]
  transfers between devices with their start and end apart: 4 -> 4, of which waited for: 0 -> 1; matrix products, arithmetic and copies ran while one was open for 0% -> 0% of each run, Pallas kernels for 4% -> 3%
where the time goes in v4:
time: 80.5 us; the launch traced here: 80.3 us
  blocking collectives  59.7 us (74%)
  starting transfers between devices  10.6 us (13%)
  Pallas kernels  9.74 us (12%)
    all_to_all x2, blocking collectives, swapped(): return lax.all_to_all(x, 'pencil', split_axis=0, concat_axis=0, tiled=True)  59.7 us
    ppermute x1, starting transfers between devices, on_device(): lax.ppermute(yc, 'slab', [(i, i ^ 1) for i in range(slabs)])  3.83 us
    ppermute x1, starting transfers between devices, on_device(): lax.ppermute(zb, 'pencil', [(i, (i - 1 ^ 1) + 1) for i in range(1, groups...  3.24 us
    pallas_call x1, Pallas kernels, row_solve(): pl.pallas_call(row_kernel, in_specs=[SMEM] + [VMEM] * 11, out_specs=VMEM,...  3.12 us
    pallas_call x1, Pallas kernels, prepare(): pl.pallas_call(functools.partial(prepare_kernel, groups), in_specs=[SMEM,...  2.35 us
    ppermute x1, starting transfers between devices, on_device(): lax.ppermute(yd, 'slab', [(i, (i - 1 ^ 1) + 1 & slabs - 1) for i in range...  2.29 us
    pallas_call x1, Pallas kernels, column_solve(): pl.pallas_call(functools.partial(column_kernel, blocks), in_specs=[SMEM,...  2.16 us
  transfers between devices with their start and end apart: 4, of which 1 were waited for; matrix products, arithmetic and copies ran while one was open for 0% of the time, Pallas kernels for 3%

profile of v4, /device:TPU:1, one launch (start us, length us, event | category | flops | bytes accessed | tf_op | source)
XLA Modules:
  0.0 80.3 jit_solution(3747246022582477486)
XLA Ops:
  0.0 1.2 %edges.1 = (f32[16,1024]{1,0:T(8,128)S(1)}, f32[16,1024]{1,0:T(8,128)S(1)}, f32[12,1024]{1,0:T(8,128)S(1)}, f32[12,1024]{1,0:T(8,128)S(1)}) custom-call(s32[1]{0:T(128)} %bitcast.here_ref, f32[12,16,1024]{2,1,0:T(8,128)} %t_ref.1), custom_call_target="tpu_custom_call" | custom-call | tf_op jit(solution)/shard_map/edges/pallas_call | solution.py:56
  1.2 3.8 %collective-permute-start = (f32[16,1024]{1,0:T(8,128)S(1)}, f32[16,1024]{1,0:T(8,128)S(1)}, u32[]{:S(2)}, u32[]{:S(2)}) collective-permute-start(f32[16,1024]{1,0:T(8,128)S(1)} %get-tuple-element.12), channel_id=1, source_target_pairs={{0,32},{32,0},{64,96},{96,64},{128,160},{160,128},{192,224},{224,1... | collective-permute-start | bytes 196616 | tf_op jit(solution)/shard_map/ppermute | solution.py:235
  5.0 2.3 %collective-permute-start.1 = (f32[16,1024]{1,0:T(8,128)S(1)}, f32[16,1024]{1,0:T(8,128)S(1)}, u32[]{:S(2)}, u32[]{:S(2)}) collective-permute-start(f32[16,1024]{1,0:T(8,128)S(1)} %get-tuple-element.13), channel_id=1, source_target_pairs={{0,224},{32,64},{64,32},{96,128},{128,96},{160,192},{192,160},{224... | collective-permute-start | bytes 196616 | tf_op jit(solution)/shard_map/ppermute | solution.py:236
  7.3 1.2 %collective-permute-start.2 = (f32[12,1024]{1,0:T(8,128)S(1)}, f32[12,1024]{1,0:T(8,128)S(1)}, u32[]{:S(2)}, u32[]{:S(2)}) collective-permute-start(f32[12,1024]{1,0:T(8,128)S(1)} %get-tuple-element.14), channel_id=1, source_target_pairs={{0,1},{1,0},{2,3},{3,2},{4,5},{5,4},{6,7},{7,6},{8,9},{9,8},{10,11... | collective-permute-start | bytes 147464 | tf_op jit(solution)/shard_map/ppermute | solution.py:237
  8.5 0.0 copy-start
  8.5 3.2 %collective-permute-start.3 = (f32[12,1024]{1,0:T(8,128)S(1)}, f32[12,1024]{1,0:T(8,128)S(1)}, u32[]{:S(2)}, u32[]{:S(2)}) collective-permute-start(f32[12,1024]{1,0:T(8,128)S(1)} %get-tuple-element.15), channel_id=1, source_target_pairs={{1,2},{2,1},{3,4},{4,3},{5,6},{6,5},{7,8},{8,7},{9,10},{10,9},{11,... | collective-permute-start | bytes 147464 | tf_op jit(solution)/shard_map/ppermute | solution.py:238
  11.8 2.4 %prepare.1 = (bf16[1024,1024]{1,0:T(8,128)(2,1)S(1)}, bf16[1024,1024]{1,0:T(8,128)(2,1)S(1)}, f32[16,128]{1,0:T(8,128)S(1)}) custom-call(s32[1]{0:T(128)} %bitcast.here_ref, f32[1024,1024]{1,0:T(8,128)} %a_hbm.1), custom_call_target="tpu_custom_call" | custom-call | flops 4194304 | bytes 8388608 | tf_op jit(solution)/shard_map/prepare/pallas_call | solution.py:88
  14.1 0.0 collective-permute-done.2.za_ref
  14.1 0.1 collective-permute-done.3.zb_ref
  14.2 0.0 collective-permute-done.yc_ref
  14.2 0.0 collective-permute-done.1.yd_ref
  14.2 0.0 copy-done
  14.2 0.0 copy-done.1
  14.3 0.0 copy-done.2
  14.3 0.0 copy-done.3
  14.3 0.0 copy-start.4
  14.3 0.0 copy-start.5
  14.3 3.1 %row_solve.1 = f32[32,3,16,128]{3,2,1,0:T(8,128)S(1)} custom-call(s32[1]{0:T(128)} %bitcast.here_ref, f32[12,16,1024]{2,1,0:T(8,128)S(1)} %copy-done, bf16[12,16,1024]{2,1,0:T(8,128)(2,1)S(1)} %copy-done.1, bf16[12,16,1024]{2,1,0:T(8,128)(2,1)S(1)} %copy-done.2, bf16[12,16,1024]{2,1,0:T(8,128)(2,1)S(1)} %copy-done.3, ...), custom_call_target="tpu_custom_call" | custom-call | flops 1207959552 | bytes 8388608 | tf_op jit(solution)/shard_map/row_solve/pallas_call | solution.py:148
  17.4 33.1 %all_to_all.10.x_ref = f32[32,3,16,128]{3,2,1,0:T(8,128)S(1)} all-to-all(f32[32,3,16,128]{3,2,1,0:T(8,128)S(1)} %row_solve.1), channel_id=1, replica_groups=mesh['slab'=8,'pencil'=32] {'pencil'}, dimensions={0} | all-to-all | bytes 1572864 | tf_op jit(solution)/shard_map/all_to_all | solution.py:226
  50.6 0.0 copy-done.4
  50.6 0.0 copy-done.5
  50.6 2.2 %column_solve.1 = f32[32,3,16,128]{3,2,1,0:T(8,128)S(1)} custom-call(s32[1]{0:T(128)} %bitcast.here_ref, s32[16]{0:T(128)S(1)} %copy-done.5, f32[2,512,512]{2,1,0:T(8,128)S(1)} %copy-done.4, f32[32,3,16,128]{3,2,1,0:T(8,128)S(1)} %all_to_all.10.x_ref), custom_call_target="tpu_custom_call" | custom-call | flops 1207959552 | bytes 4194304 | tf_op jit(solution)/shard_map/column_solve/pallas_call | solution.py:193
  52.7 26.6 %all_to_all.11.x_ref = f32[32,3,16,128]{3,2,1,0:T(8,128)S(1)} all-to-all(f32[32,3,16,128]{3,2,1,0:T(8,128)S(1)} %column_solve.1), channel_id=1, replica_groups=mesh['slab'=8,'pencil'=32] {'pencil'}, dimensions={0} | all-to-all | bytes 1572864 | tf_op jit(solution)/shard_map/all_to_all | solution.py:226
  79.3 0.9 %place.1 = f32[12,16,1024]{2,1,0:T(8,128)} custom-call(f32[32,3,16,128]{3,2,1,0:T(8,128)S(1)} %all_to_all.11.x_ref), custom_call_target="tpu_custom_call" | custom-call | tf_op jit(solution)/shard_map/place/pallas_call | solution.py:215
  (3 shorter events, 0.0 us)
Async XLA Ops:
  1.2 13.0 %collective-permute-start = (f32[16,1024]{1,0:T(8,128)S(1)}, f32[16,1024]{1,0:T(8,128)S(1)}, u32[]{:S(2)}, u32[]{:S(2)}) collective-permute-start(f32[16,1024]{1,0:T(8,128)S(1)} %get-tuple-element.12), channel_id=1, source_target_pairs={{0,32},{32,0},{64,96},{96,64},{128,160},{160,128},{192,224},{224,1... | collective-permute-start | bytes 196616 | tf_op jit(solution)/shard_map/ppermute | solution.py:235
  5.0 9.2 %collective-permute-start.1 = (f32[16,1024]{1,0:T(8,128)S(1)}, f32[16,1024]{1,0:T(8,128)S(1)}, u32[]{:S(2)}, u32[]{:S(2)}) collective-permute-start(f32[16,1024]{1,0:T(8,128)S(1)} %get-tuple-element.13), channel_id=1, source_target_pairs={{0,224},{32,64},{64,32},{96,128},{128,96},{160,192},{192,160},{224... | collective-permute-start | bytes 196616 | tf_op jit(solution)/shard_map/ppermute | solution.py:236
  7.3 6.8 %collective-permute-start.2 = (f32[12,1024]{1,0:T(8,128)S(1)}, f32[12,1024]{1,0:T(8,128)S(1)}, u32[]{:S(2)}, u32[]{:S(2)}) collective-permute-start(f32[12,1024]{1,0:T(8,128)S(1)} %get-tuple-element.14), channel_id=1, source_target_pairs={{0,1},{1,0},{2,3},{3,2},{4,5},{5,4},{6,7},{7,6},{8,9},{9,8},{10,11... | collective-permute-start | bytes 147464 | tf_op jit(solution)/shard_map/ppermute | solution.py:237
  8.5 5.7 %copy-start = (f32[12,16,1024]{2,1,0:T(8,128)S(1)}, f32[12,16,1024]{2,1,0:T(8,128)}, u32[]{:S(2)}) copy-start(f32[12,16,1024]{2,1,0:T(8,128)} %t_ref.1) | copy-start | bytes 2359300
  8.5 5.7 %copy-start.1 = (bf16[12,16,1024]{2,1,0:T(8,128)(2,1)S(1)}, bf16[12,16,1024]{2,1,0:T(8,128)(2,1)}, u32[]{:S(2)}) copy-start(bf16[12,16,1024]{2,1,0:T(8,128)(2,1)} %u_ref.1) | copy-start | bytes 1179652
  8.5 5.7 %copy-start.2 = (bf16[12,16,1024]{2,1,0:T(8,128)(2,1)S(1)}, bf16[12,16,1024]{2,1,0:T(8,128)(2,1)}, u32[]{:S(2)}) copy-start(bf16[12,16,1024]{2,1,0:T(8,128)(2,1)} %v_ref.1) | copy-start | bytes 1179652
  8.5 5.8 %copy-start.3 = (bf16[12,16,1024]{2,1,0:T(8,128)(2,1)S(1)}, bf16[12,16,1024]{2,1,0:T(8,128)(2,1)}, u32[]{:S(2)}) copy-start(bf16[12,16,1024]{2,1,0:T(8,128)(2,1)} %w_ref.2) | copy-start | bytes 1179652
  8.5 5.7 %collective-permute-start.3 = (f32[12,1024]{1,0:T(8,128)S(1)}, f32[12,1024]{1,0:T(8,128)S(1)}, u32[]{:S(2)}, u32[]{:S(2)}) collective-permute-start(f32[12,1024]{1,0:T(8,128)S(1)} %get-tuple-element.15), channel_id=1, source_target_pairs={{1,2},{2,1},{3,4},{4,3},{5,6},{6,5},{7,8},{8,7},{9,10},{10,9},{11,... | collective-permute-start | bytes 147464 | tf_op jit(solution)/shard_map/ppermute | solution.py:238
  14.3 36.3 %copy-start.4 = (f32[2,512,512]{2,1,0:T(8,128)S(1)}, f32[2,512,512]{2,1,0:T(8,128)}, u32[]{:S(2)}) copy-start(f32[2,512,512]{2,1,0:T(8,128)} %w_ref.3) | copy-start | bytes 6291460
  14.3 36.3 %copy-start.5 = (s32[16]{0:T(128)S(1)}, s32[16]{0:T(128)}, u32[]{:S(2)}) copy-start(s32[16]{0:T(128)} %seg_ref.1) | copy-start | bytes 196

commit v5 on v4

--- a/solution.py
+++ b/solution.py
@@ -10,8 +10,6 @@
 TRANSPORT_PART = 0.25
 CONDUCTION_PART = 0.2
 LANES = 128
-EDGE = 53
-PREP = 46
 VMEM = pl.BlockSpec(memory_space=pltpu.VMEM)
 HBM = pl.BlockSpec(memory_space=pltpu.HBM)
 SMEM = pl.BlockSpec(memory_space=pltpu.SMEM)
@@ -19,6 +17,10 @@
 
 def metric_of(levels, extent):
     return 0.5 / (1.0 + jnp.sin(jnp.pi * (levels + 0.5) / extent))
+
+
+def pinned(x):
+    return pltpu.with_memory_space_constraint(x, pltpu.HBM)
 
 
 def halves(wide):
@@ -59,62 +61,59 @@
         out_specs=[VMEM] * 4,
         out_shape=[plane, plane, level, level],
         scratch_shapes=[pltpu.VMEM((2, planes, half, nx), t.dtype), pltpu.SemaphoreType.DMA((4,))],
-        compiler_params=pltpu.CompilerParams(vmem_limit_bytes=EDGE * 2**20),
+        compiler_params=pltpu.CompilerParams(vmem_limit_bytes=8 * 2**20),
         name="edges",
-    )(here, t)
-
-
-def prepare_kernel(groups, here_ref, a_hbm, ah_ref, al_ref, g_ref, a_buf, sems):
-    parts = sems.shape[0]
+    )(here, pinned(t))
+
+
+def prepare_kernel(
+    groups,
+    here_ref,
+    t_hbm,
+    u_hbm,
+    v_hbm,
+    w_hbm,
+    a_hbm,
+    side_ref,
+    cb_ref,
+    ca_ref,
+    cl_ref,
+    ch_ref,
+    ah_ref,
+    al_ref,
+    t_ref,
+    u_ref,
+    v_ref,
+    w_ref,
+    a_buf,
+    sems,
+):
+    planes, rows, nx = t_ref.shape
+    parts = sems.shape[0] - 4
     a_rows = a_buf.shape[0] // parts
+    fields = [
+        pltpu.make_async_copy(source, target, sems.at[i])
+        for i, (source, target) in enumerate(((t_hbm, t_ref), (u_hbm, u_ref), (v_hbm, v_ref), (w_hbm, w_ref)))
+    ]
     copies = []
     for i in range(parts):
         cut = slice(i * a_rows, (i + 1) * a_rows)
-        copies.append(pltpu.make_async_copy(a_hbm.at[cut], a_buf.at[cut], sems.at[i]))
-    for copy in copies:
+        copies.append(pltpu.make_async_copy(a_hbm.at[cut], a_buf.at[cut], sems.at[4 + i]))
+    for copy in fields + copies:
         copy.start()
-    rows, lanes = g_ref.shape
-    levels = (lax.broadcasted_iota(jnp.int32, (rows, lanes), 0) + here_ref[0] % groups * rows).astype(jnp.float32)
-    g_ref[...] = metric_of(levels, groups * rows)
-    for i in range(parts):
-        cut = slice(i * a_rows, (i + 1) * a_rows)
-        copies[i].wait()
-        ah_ref[cut], al_ref[cut] = halves(a_buf[cut])
-
-
-def prepare(here, a, rows, groups):
-    a16 = jax.ShapeDtypeStruct(a.shape, jnp.bfloat16)
-    parts = 4
-    return pl.pallas_call(
-        functools.partial(prepare_kernel, groups),
-        in_specs=[SMEM, HBM],
-        out_specs=[VMEM] * 3,
-        out_shape=[a16, a16, jax.ShapeDtypeStruct((rows, LANES), jnp.float32)],
-        scratch_shapes=[pltpu.VMEM(a.shape, a.dtype), pltpu.SemaphoreType.DMA((parts,))],
-        compiler_params=pltpu.CompilerParams(vmem_limit_bytes=PREP * 2**20),
-        cost_estimate=pl.CostEstimate(flops=4 * a.size, bytes_accessed=8 * a.size, transcendentals=0),
-        name="prepare",
-    )(here, a)
-
-
-def row_kernel(
-    here_ref, t_ref, u_ref, v_ref, w_ref, yc_ref, yd_ref, za_ref, zb_ref, g_ref, ah_ref, al_ref, out_ref, rh, rl
-):
-    planes, rows, nx = t_ref.shape
-    metric = jnp.concatenate([g_ref[...]] * (nx // LANES), axis=1)
-    groups = out_ref.shape[0]
-    pencil_even, slab_even = here_ref[0] % 2 == 0, here_ref[0] // groups % 2 == 0
-    over = jnp.where(pencil_even, za_ref[...], zb_ref[...])
-    under = jnp.where(pencil_even, zb_ref[...], za_ref[...])
+    levels = (lax.broadcasted_iota(jnp.int32, (rows, LANES), 0) + here_ref[0] % groups * rows).astype(jnp.float32)
+    metric = jnp.concatenate([metric_of(levels, groups * rows)] * (nx // LANES), axis=1)
     level = lax.broadcasted_iota(jnp.int32, (rows, nx), 0)
+    for copy in fields:
+        copy.wait()
     for y in range(planes):
         t = t_ref[y]
-        ahead = t_ref[y + 1] if y + 1 < planes else jnp.where(slab_even, yc_ref[...], yd_ref[...])
-        behind = t_ref[y - 1] if y else jnp.where(slab_even, yd_ref[...], yc_ref[...])
+        ahead = t_ref[y + 1] if y + 1 < planes else jnp.zeros_like(t)
+        behind = t_ref[y - 1] if y else jnp.zeros_like(t)
         east = pltpu.roll(t, nx - 1, 1)
         west = pltpu.roll(t, 1, 1)
-        above = jnp.where(level == rows - 1, over[y : y + 1, :], pltpu.roll(t, rows - 1, 0))
-        below = jnp.where(level == 0, under[y : y + 1, :], pltpu.roll(t, 1, 0))
+        above = jnp.where(level == rows - 1, 0.0, pltpu.roll(t, rows - 1, 0))
+        below = jnp.where(level == 0, 0.0, pltpu.roll(t, 1, 0))
         u = u_ref[y].astype(jnp.float32)
         v = v_ref[y].astype(jnp.float32)
         w = w_ref[y].astype(jnp.float32)
@@ -124,7 +123,57 @@
             + 0.5 * (east - 2.0 * t + west)
             + 0.5 * metric * (above - 2.0 * t + below)
         )
-        side = t - TRANSPORT_PART * carried + CONDUCTION_PART * conducted
+        side_ref[y] = t - TRANSPORT_PART * carried + CONDUCTION_PART * conducted
+        cl_ref[y : y + 1, :] = (metric * (0.5 * CONDUCTION_PART + TRANSPORT_PART * w))[:1, :]
+        ch_ref[y : y + 1, :] = (metric * (0.5 * CONDUCTION_PART - TRANSPORT_PART * w))[rows - 1 :, :]
+        if y == 0:
+            cb_ref[...] = CONDUCTION_PART + 0.5 * TRANSPORT_PART * v
+        if y == planes - 1:
+            ca_ref[...] = CONDUCTION_PART - 0.5 * TRANSPORT_PART * v
+    for i in range(parts):
+        cut = slice(i * a_rows, (i + 1) * a_rows)
+        copies[i].wait()
+        ah_ref[cut], al_ref[cut] = halves(a_buf[cut])
+
+
+def prepare(here, t, u, v, w, a, groups):
+    planes, rows, nx = t.shape
+    a16 = jax.ShapeDtypeStruct(a.shape, jnp.bfloat16)
+    plane = jax.ShapeDtypeStruct((rows, nx), t.dtype)
+    level = jax.ShapeDtypeStruct((planes, nx), t.dtype)
+    parts = 4
+    return pl.pallas_call(
+        functools.partial(prepare_kernel, groups),
+        in_specs=[SMEM] + [HBM] * 5,
+        out_specs=[VMEM] * 7,
+        out_shape=[jax.ShapeDtypeStruct(t.shape, t.dtype), plane, plane, level, level, a16, a16],
+        scratch_shapes=[pltpu.VMEM(x.shape, x.dtype) for x in (t, u, v, w, a)]
+        + [pltpu.SemaphoreType.DMA((4 + parts,))],
+        compiler_params=pltpu.CompilerParams(vmem_limit_bytes=16 * 2**20),
+        cost_estimate=pl.CostEstimate(
+            flops=4 * a.size + 40 * t.size, bytes_accessed=8 * a.size + 14 * t.size, transcendentals=0
+        ),
+        name="prepare",
+    )(here, *(pinned(x) for x in (t, u, v, w, a)))
+
+
+def row_kernel(
+    here_ref, side_ref, cb_ref, ca_ref, cl_ref, ch_ref, yc_ref, yd_ref, za_ref, zb_ref, ah_ref, al_ref, out_ref, rh, rl
+):
+    planes, rows, nx = side_ref.shape
+    groups = out_ref.shape[0]
+    pencil_even, slab_even = here_ref[0] % 2 == 0, here_ref[0] // groups % 2 == 0
+    low = cl_ref[...] * jnp.where(pencil_even, zb_ref[...], za_ref[...])
+    high = ch_ref[...] * jnp.where(pencil_even, za_ref[...], zb_ref[...])
+    level = lax.broadcasted_iota(jnp.int32, (rows, nx), 0)
+    for y in range(planes):
+        side = side_ref[y]
+        if y == 0:
+            side = side + cb_ref[...] * jnp.where(slab_even, yd_ref[...], yc_ref[...])
+        if y == planes - 1:
+            side = side + ca_ref[...] * jnp.where(slab_even, yc_ref[...], yd_ref[...])
+        side = side + jnp.where(level == 0, low[y : y + 1, :], 0.0)
+        side = side + jnp.where(level == rows - 1, high[y : y + 1, :], 0.0)
         rh[y * rows : (y + 1) * rows, :], rl[y * rows : (y + 1) * rows, :] = halves(side)
     wide = 2 * LANES
     unit_rows = 3 * rows
@@ -143,8 +192,8 @@
                 out_ref[q * blocks + 2 * c + h] = piece.reshape(3, rows, LANES)
 
 
-def row_solve(here, t, u, v, w, halos, metric, ah, al, groups):
-    planes, rows, nx = t.shape
+def row_solve(here, parts, halos, ah, al, groups):
+    planes, rows, nx = parts[0].shape
     return pl.pallas_call(
         row_kernel,
         in_specs=[SMEM] + [VMEM] * 11,
@@ -156,7 +205,7 @@
             flops=6 * planes * rows * nx * nx, bytes_accessed=8 * 2**20, transcendentals=0
         ),
         name="row_solve",
-    )(here, t, u, v, w, *halos, metric, ah, al)
+    )(here, *parts, *halos, ah, al)
 
 
 def column_kernel(blocks, here_ref, seg_ref, w_ref, x_ref, out_ref):
@@ -237,8 +286,8 @@
         lax.ppermute(za, "pencil", [(i, i ^ 1) for i in range(groups)]),
         lax.ppermute(zb, "pencil", [(i, ((i - 1) ^ 1) + 1) for i in range(1, groups - 1)]),
     )
-    ah, al, metric = prepare(here, downstream_solver_matrix, rows, groups)
-    x = swapped(row_solve(here, t, u, v, w, halos, metric, ah, al, groups))
+    *parts, ah, al = prepare(here, t, u, v, w, downstream_solver_matrix, groups)
+    x = swapped(row_solve(here, parts, halos, ah, al, groups))
     x = swapped(column_solve(here, wall_segments, wallward_solver_matrices, x, nx // LANES))
     return place(x, t.shape)
 

time: 80.5 us -> 79.3 us (0.985)
    pallas_call x1, Pallas kernels: 3.12 us -> 2.18 us  [row_solve(): pl.pallas_call(row_kernel, in_specs=[SMEM] + [VMEM] * 11, out_specs=VMEM,...]
    pallas_call x1, Pallas kernels: 2.35 us -> 3.28 us  [prepare(): pl.pallas_call(functools.partial(prepare_kernel, groups), in_specs=[SMEM]...]
    all_to_all x2, blocking collectives: 59.7 us -> 58.9 us  [swapped(): return lax.all_to_all(x, 'pencil', split_axis=0, concat_axis=0, tiled=True)]
  transfers between devices with their start and end apart: 4 -> 4, of which waited for: 1 -> 0; matrix products, arithmetic and copies ran while one was open for 0% -> 0% of each run, Pallas kernels for 3% -> 4%
where the time goes in v5:
time: 79.3 us; the launch traced here: 79.1 us
  blocking collectives  58.9 us (74%)
  starting transfers between devices  10.4 us (13%)
  Pallas kernels  9.75 us (12%)
    all_to_all x2, blocking collectives, swapped(): return lax.all_to_all(x, 'pencil', split_axis=0, concat_axis=0, tiled=True)  58.9 us
    ppermute x1, starting transfers between devices, on_device(): lax.ppermute(yc, 'slab', [(i, i ^ 1) for i in range(slabs)])  3.83 us
    pallas_call x1, Pallas kernels, prepare(): pl.pallas_call(functools.partial(prepare_kernel, groups), in_specs=[SMEM]...  3.28 us
    ppermute x1, starting transfers between devices, on_device(): lax.ppermute(zb, 'pencil', [(i, (i - 1 ^ 1) + 1) for i in range(1, groups...  3.08 us
    ppermute x1, starting transfers between devices, on_device(): lax.ppermute(yd, 'slab', [(i, (i - 1 ^ 1) + 1 & slabs - 1) for i in range...  2.29 us
    pallas_call x1, Pallas kernels, row_solve(): pl.pallas_call(row_kernel, in_specs=[SMEM] + [VMEM] * 11, out_specs=VMEM,...  2.18 us
    pallas_call x1, Pallas kernels, column_solve(): pl.pallas_call(functools.partial(column_kernel, blocks), in_specs=[SMEM,...  2.17 us
  transfers between devices with their start and end apart: 4, of which 0 were waited for; matrix products, arithmetic and copies ran while one was open for 0% of the time, Pallas kernels for 4%

profile of v5, /device:TPU:1, one launch (start us, length us, event | category | flops | bytes accessed | tf_op | source)
XLA Modules:
  0.0 79.1 jit_solution(9310553530518974719)
XLA Ops:
  0.0 1.2 %edges.1 = (f32[16,1024]{1,0:T(8,128)S(1)}, f32[16,1024]{1,0:T(8,128)S(1)}, f32[12,1024]{1,0:T(8,128)S(1)}, f32[12,1024]{1,0:T(8,128)S(1)}) custom-call(s32[1]{0:T(128)} %bitcast.here_ref, f32[12,16,1024]{2,1,0:T(8,128)} %t_hbm.3), custom_call_target="tpu_custom_call" | custom-call | tf_op jit(solution)/shard_map/edges/pallas_call | solution.py:58
  1.2 3.8 %collective-permute-start = (f32[16,1024]{1,0:T(8,128)S(1)}, f32[16,1024]{1,0:T(8,128)S(1)}, u32[]{:S(2)}, u32[]{:S(2)}) collective-permute-start(f32[16,1024]{1,0:T(8,128)S(1)} %get-tuple-element.21), channel_id=1, source_target_pairs={{0,32},{32,0},{64,96},{96,64},{128,160},{160,128},{192,224},{224,1... | collective-permute-start | bytes 196616 | tf_op jit(solution)/shard_map/ppermute | solution.py:284
  5.0 2.3 %collective-permute-start.1 = (f32[16,1024]{1,0:T(8,128)S(1)}, f32[16,1024]{1,0:T(8,128)S(1)}, u32[]{:S(2)}, u32[]{:S(2)}) collective-permute-start(f32[16,1024]{1,0:T(8,128)S(1)} %get-tuple-element.22), channel_id=1, source_target_pairs={{0,224},{32,64},{64,32},{96,128},{128,96},{160,192},{192,160},{224... | collective-permute-start | bytes 196616 | tf_op jit(solution)/shard_map/ppermute | solution.py:285
  7.3 1.2 %collective-permute-start.2 = (f32[12,1024]{1,0:T(8,128)S(1)}, f32[12,1024]{1,0:T(8,128)S(1)}, u32[]{:S(2)}, u32[]{:S(2)}) collective-permute-start(f32[12,1024]{1,0:T(8,128)S(1)} %get-tuple-element.23), channel_id=1, source_target_pairs={{0,1},{1,0},{2,3},{3,2},{4,5},{5,4},{6,7},{7,6},{8,9},{9,8},{10,11... | collective-permute-start | bytes 147464 | tf_op jit(solution)/shard_map/ppermute | solution.py:286
  8.5 3.1 %collective-permute-start.3 = (f32[12,1024]{1,0:T(8,128)S(1)}, f32[12,1024]{1,0:T(8,128)S(1)}, u32[]{:S(2)}, u32[]{:S(2)}) collective-permute-start(f32[12,1024]{1,0:T(8,128)S(1)} %get-tuple-element.24), channel_id=1, source_target_pairs={{1,2},{2,1},{3,4},{4,3},{5,6},{6,5},{7,8},{8,7},{9,10},{10,9},{11,... | collective-permute-start | bytes 147464 | tf_op jit(solution)/shard_map/ppermute | solution.py:287
  11.6 3.3 %prepare.1 = (f32[12,16,1024]{2,1,0:T(8,128)S(1)}, f32[16,1024]{1,0:T(8,128)S(1)}, f32[16,1024]{1,0:T(8,128)S(1)}, f32[12,1024]{1,0:T(8,128)S(1)}, f32[12,1024]{...) custom-call(s32[1]{0:T(128)} %bitcast.here_ref, f32[12,16,1024]{2,1,0:T(8,128)} %t_hbm.3, ...), custom_call_target="tpu_custom_call" | custom-call | flops 12058624 | bytes 11141120 | tf_op jit(solution)/shard_map/prepare/pallas_call | solution.py:145
  14.9 0.0 collective-permute-done.2.za_ref
  14.9 0.0 collective-permute-done.3.zb_ref
  14.9 0.0 collective-permute-done.yc_ref
  14.9 0.0 collective-permute-done.1.yd_ref
  14.9 0.0 copy-start
  14.9 0.0 copy-start.1
  15.0 2.2 %row_solve.1 = f32[32,3,16,128]{3,2,1,0:T(8,128)S(1)} custom-call(s32[1]{0:T(128)} %bitcast.here_ref, f32[12,16,1024]{2,1,0:T(8,128)S(1)} %get-tuple-element.16.side_ref, f32[16,1024]{1,0:T(8,128)S(1)} %get-tuple-element.17.cb_ref, f32[16,1024]{1,0:T(8,128)S(1)} %get-tuple-element.18.ca_ref, f32[12,1024]{1,0:T(8,128)S(1)} %get-tuple-element.19.cl_ref, ...), custom_call_target="tpu_custom_call" | custom-call | flops 1207959552 | bytes 8388608 | tf_op jit(solution)/shard_map/row_solve/pallas_call | solution.py:197
  17.1 32.3 %all_to_all.10.x_ref = f32[32,3,16,128]{3,2,1,0:T(8,128)S(1)} all-to-all(f32[32,3,16,128]{3,2,1,0:T(8,128)S(1)} %row_solve.1), channel_id=1, replica_groups=mesh['slab'=8,'pencil'=32] {'pencil'}, dimensions={0} | all-to-all | bytes 1572864 | tf_op jit(solution)/shard_map/all_to_all | solution.py:275
  49.4 0.0 copy-done
  49.4 0.0 copy-done.1
  49.4 2.2 %column_solve.1 = f32[32,3,16,128]{3,2,1,0:T(8,128)S(1)} custom-call(s32[1]{0:T(128)} %bitcast.here_ref, s32[16]{0:T(128)S(1)} %copy-done.1, f32[2,512,512]{2,1,0:T(8,128)S(1)} %copy-done, f32[32,3,16,128]{3,2,1,0:T(8,128)S(1)} %all_to_all.10.x_ref), custom_call_target="tpu_custom_call" | custom-call | flops 1207959552 | bytes 4194304 | tf_op jit(solution)/shard_map/column_solve/pallas_call | solution.py:242
  51.6 26.6 %all_to_all.11.x_ref = f32[32,3,16,128]{3,2,1,0:T(8,128)S(1)} all-to-all(f32[32,3,16,128]{3,2,1,0:T(8,128)S(1)} %column_solve.1), channel_id=1, replica_groups=mesh['slab'=8,'pencil'=32] {'pencil'}, dimensions={0} | all-to-all | bytes 1572864 | tf_op jit(solution)/shard_map/all_to_all | solution.py:275
  78.2 0.9 %place.1 = f32[12,16,1024]{2,1,0:T(8,128)} custom-call(f32[32,3,16,128]{3,2,1,0:T(8,128)S(1)} %all_to_all.11.x_ref), custom_call_target="tpu_custom_call" | custom-call | tf_op jit(solution)/shard_map/place/pallas_call | solution.py:264
Async XLA Ops:
  1.2 13.7 %collective-permute-start = (f32[16,1024]{1,0:T(8,128)S(1)}, f32[16,1024]{1,0:T(8,128)S(1)}, u32[]{:S(2)}, u32[]{:S(2)}) collective-permute-start(f32[16,1024]{1,0:T(8,128)S(1)} %get-tuple-element.21), channel_id=1, source_target_pairs={{0,32},{32,0},{64,96},{96,64},{128,160},{160,128},{192,224},{224,1... | collective-permute-start | bytes 196616 | tf_op jit(solution)/shard_map/ppermute | solution.py:284
  5.0 9.9 %collective-permute-start.1 = (f32[16,1024]{1,0:T(8,128)S(1)}, f32[16,1024]{1,0:T(8,128)S(1)}, u32[]{:S(2)}, u32[]{:S(2)}) collective-permute-start(f32[16,1024]{1,0:T(8,128)S(1)} %get-tuple-element.22), channel_id=1, source_target_pairs={{0,224},{32,64},{64,32},{96,128},{128,96},{160,192},{192,160},{224... | collective-permute-start | bytes 196616 | tf_op jit(solution)/shard_map/ppermute | solution.py:285
  7.3 7.6 %collective-permute-start.2 = (f32[12,1024]{1,0:T(8,128)S(1)}, f32[12,1024]{1,0:T(8,128)S(1)}, u32[]{:S(2)}, u32[]{:S(2)}) collective-permute-start(f32[12,1024]{1,0:T(8,128)S(1)} %get-tuple-element.23), channel_id=1, source_target_pairs={{0,1},{1,0},{2,3},{3,2},{4,5},{5,4},{6,7},{7,6},{8,9},{9,8},{10,11... | collective-permute-start | bytes 147464 | tf_op jit(solution)/shard_map/ppermute | solution.py:286
  8.5 6.4 %collective-permute-start.3 = (f32[12,1024]{1,0:T(8,128)S(1)}, f32[12,1024]{1,0:T(8,128)S(1)}, u32[]{:S(2)}, u32[]{:S(2)}) collective-permute-start(f32[12,1024]{1,0:T(8,128)S(1)} %get-tuple-element.24), channel_id=1, source_target_pairs={{1,2},{2,1},{3,4},{4,3},{5,6},{6,5},{7,8},{8,7},{9,10},{10,9},{11,... | collective-permute-start | bytes 147464 | tf_op jit(solution)/shard_map/ppermute | solution.py:287
  14.9 34.5 %copy-start = (f32[2,512,512]{2,1,0:T(8,128)S(1)}, f32[2,512,512]{2,1,0:T(8,128)}, u32[]{:S(2)}) copy-start(f32[2,512,512]{2,1,0:T(8,128)} %w_ref.1) | copy-start | bytes 6291460
  14.9 34.5 %copy-start.1 = (s32[16]{0:T(128)S(1)}, s32[16]{0:T(128)}, u32[]{:S(2)}) copy-start(s32[16]{0:T(128)} %seg_ref.1) | copy-start | bytes 196

commit v6 on v5

--- a/solution.py
+++ b/solution.py
@@ -44,23 +44,23 @@
     copies[1].wait()
     for y in range(planes):
         low, high = buf[0, y, :1, :], buf[1, y, half - 1 :, :]
-        za_ref[y : y + 1, :] = jnp.where(pencil_even, high, low)
-        zb_ref[y : y + 1, :] = jnp.where(pencil_even, low, high)
+        za_ref[y : y + 1, :] = jnp.where(pencil_even, low, high)
+        zb_ref[y : y + 1, :] = jnp.where(pencil_even, high, low)
     copies[2].wait()
     copies[3].wait()
 
 
 def edges(here, t, groups):
     planes, rows, nx = t.shape
-    half = 8
+    half = rows // 2
     plane = jax.ShapeDtypeStruct((rows, nx), t.dtype)
     level = jax.ShapeDtypeStruct((planes, nx), t.dtype)
     return pl.pallas_call(
         functools.partial(edge_kernel, groups),
         in_specs=[SMEM, HBM],
-        out_specs=[VMEM] * 4,
-        out_shape=[plane, plane, level, level],
-        scratch_shapes=[pltpu.VMEM((2, planes, half, nx), t.dtype), pltpu.SemaphoreType.DMA((4,))],
+        out_specs=[VMEM] * 5,
+        out_shape=[plane, plane, level, level, jax.ShapeDtypeStruct((2, planes, half, nx), t.dtype)],
+        scratch_shapes=[pltpu.SemaphoreType.DMA((4,))],
         compiler_params=pltpu.CompilerParams(vmem_limit_bytes=8 * 2**20),
         name="edges",
     )(here, pinned(t))
@@ -69,7 +69,7 @@
 def prepare_kernel(
     groups,
     here_ref,
-    t_hbm,
+    t_ref,
     u_hbm,
     v_hbm,
     w_hbm,
@@ -81,35 +81,40 @@
     ch_ref,
     ah_ref,
     al_ref,
-    t_ref,
     u_ref,
     v_ref,
     w_ref,
     a_buf,
     sems,
 ):
-    planes, rows, nx = t_ref.shape
-    parts = sems.shape[0] - 4
+    planes, rows, nx = side_ref.shape
+    parts = sems.shape[0] - 3
     a_rows = a_buf.shape[0] // parts
     fields = [
         pltpu.make_async_copy(source, target, sems.at[i])
-        for i, (source, target) in enumerate(((t_hbm, t_ref), (u_hbm, u_ref), (v_hbm, v_ref), (w_hbm, w_ref)))
+        for i, (source, target) in enumerate(((u_hbm, u_ref), (v_hbm, v_ref), (w_hbm, w_ref)))
     ]
     copies = []
     for i in range(parts):
         cut = slice(i * a_rows, (i + 1) * a_rows)
-        copies.append(pltpu.make_async_copy(a_hbm.at[cut], a_buf.at[cut], sems.at[4 + i]))
-    for copy in fields + copies:
+        copies.append(pltpu.make_async_copy(a_hbm.at[cut], a_buf.at[cut], sems.at[3 + i]))
+    for copy in fields:
         copy.start()
     levels = (lax.broadcasted_iota(jnp.int32, (rows, LANES), 0) + here_ref[0] % groups * rows).astype(jnp.float32)
     metric = jnp.concatenate([metric_of(levels, groups * rows)] * (nx // LANES), axis=1)
     level = lax.broadcasted_iota(jnp.int32, (rows, nx), 0)
     for copy in fields:
         copy.wait()
+    for copy in copies:
+        copy.start()
+
+    def plane(y):
+        if y < 0 or y == planes:
+            return jnp.zeros((rows, nx), jnp.float32)
+        return jnp.concatenate([t_ref[0, y], t_ref[1, y]], axis=0)
+
     for y in range(planes):
-        t = t_ref[y]
-        ahead = t_ref[y + 1] if y + 1 < planes else jnp.zeros_like(t)
-        behind = t_ref[y - 1] if y else jnp.zeros_like(t)
+        t, ahead, behind = plane(y), plane(y + 1), plane(y - 1)
         east = pltpu.roll(t, nx - 1, 1)
         west = pltpu.roll(t, 1, 1)
         above = jnp.where(level == rows - 1, 0.0, pltpu.roll(t, rows - 1, 0))
@@ -137,35 +142,36 @@
 
 
 def prepare(here, t, u, v, w, a, groups):
-    planes, rows, nx = t.shape
+    planes, rows, nx = u.shape
     a16 = jax.ShapeDtypeStruct(a.shape, jnp.bfloat16)
     plane = jax.ShapeDtypeStruct((rows, nx), t.dtype)
     level = jax.ShapeDtypeStruct((planes, nx), t.dtype)
     parts = 4
     return pl.pallas_call(
         functools.partial(prepare_kernel, groups),
-        in_specs=[SMEM] + [HBM] * 5,
+        in_specs=[SMEM, VMEM] + [HBM] * 4,
         out_specs=[VMEM] * 7,
-        out_shape=[jax.ShapeDtypeStruct(t.shape, t.dtype), plane, plane, level, level, a16, a16],
-        scratch_shapes=[pltpu.VMEM(x.shape, x.dtype) for x in (t, u, v, w, a)]
-        + [pltpu.SemaphoreType.DMA((4 + parts,))],
+        out_shape=[jax.ShapeDtypeStruct(u.shape, t.dtype), plane, plane, level, level, a16, a16],
+        scratch_shapes=[pltpu.VMEM(x.shape, x.dtype) for x in (u, v, w, a)]
+        + [pltpu.SemaphoreType.DMA((3 + parts,))],
         compiler_params=pltpu.CompilerParams(vmem_limit_bytes=16 * 2**20),
         cost_estimate=pl.CostEstimate(
             flops=4 * a.size + 40 * t.size, bytes_accessed=8 * a.size + 14 * t.size, transcendentals=0
         ),
         name="prepare",
-    )(here, *(pinned(x) for x in (t, u, v, w, a)))
+    )(here, t, *(pinned(x) for x in (u, v, w, a)))
 
 
 def row_kernel(
-    here_ref, side_ref, cb_ref, ca_ref, cl_ref, ch_ref, yc_ref, yd_ref, za_ref, zb_ref, ah_ref, al_ref, out_ref, rh, rl
+    here_ref, side_ref, cb_ref, ca_ref, cl_ref, ch_ref, yc_ref, yd_ref, za_ref, zb_ref, ah_ref, al_ref, out_ref, both
 ):
     planes, rows, nx = side_ref.shape
     groups = out_ref.shape[0]
     pencil_even, slab_even = here_ref[0] % 2 == 0, here_ref[0] // groups % 2 == 0
-    low = cl_ref[...] * jnp.where(pencil_even, zb_ref[...], za_ref[...])
-    high = ch_ref[...] * jnp.where(pencil_even, za_ref[...], zb_ref[...])
+    low = cl_ref[...] * jnp.where(pencil_even, za_ref[...], zb_ref[...])
+    high = ch_ref[...] * jnp.where(pencil_even, zb_ref[...], za_ref[...])
     level = lax.broadcasted_iota(jnp.int32, (rows, nx), 0)
+    extent = planes * rows
     for y in range(planes):
         side = side_ref[y]
         if y == 0:
@@ -174,7 +180,9 @@
             side = side + ca_ref[...] * jnp.where(slab_even, yc_ref[...], yd_ref[...])
         side = side + jnp.where(level == 0, low[y : y + 1, :], 0.0)
         side = side + jnp.where(level == rows - 1, high[y : y + 1, :], 0.0)
-        rh[y * rows : (y + 1) * rows, :], rl[y * rows : (y + 1) * rows, :] = halves(side)
+        high_part, low_part = halves(side)
+        both[y * rows : (y + 1) * rows, :] = high_part
+        both[extent + y * rows : extent + (y + 1) * rows, :] = low_part
     wide = 2 * LANES
     unit_rows = 3 * rows
     blocks = nx // LANES
@@ -185,7 +193,8 @@
         def dot(x, m):
             return lax.dot_general(x, m, (((1,), (1,)), ((), ())), preferred_element_type=jnp.float32)
 
-        solved = dot(rh[...], ah) + (dot(rh[...], al) + dot(rl[...], ah))
+        main = dot(both[...], ah)
+        solved = main[:extent] + (dot(both[:extent, :], al) + main[extent:])
         for q in range(planes // 3):
             for h in range(2):
                 piece = solved[q * unit_rows : (q + 1) * unit_rows, h * LANES : (h + 1) * LANES]
@@ -199,7 +208,7 @@
         in_specs=[SMEM] + [VMEM] * 11,
         out_specs=VMEM,
         out_shape=jax.ShapeDtypeStruct((groups, 3, rows, LANES), jnp.float32),
-        scratch_shapes=[pltpu.VMEM((planes * rows, nx), jnp.bfloat16)] * 2,
+        scratch_shapes=[pltpu.VMEM((2 * planes * rows, nx), jnp.bfloat16)],
         compiler_params=pltpu.CompilerParams(vmem_limit_bytes=32 * 2**20),
         cost_estimate=pl.CostEstimate(
             flops=6 * planes * rows * nx * nx, bytes_accessed=8 * 2**20, transcendentals=0
@@ -223,19 +232,15 @@
     both = jnp.concatenate([xh, xl], axis=1)
     width = units * lanes
 
-    def solve(c, lo, hi):
-        wh, wl = halves(w_ref[c, lo:hi, :])
+    def solve(c):
+        wh, wl = halves(w_ref[c])
         d = jnp.dot(wh, both, preferred_element_type=jnp.float32)
         e = jnp.dot(wl, xh, preferred_element_type=jnp.float32)
         return d[:, :width] + (d[:, width:] + e)
 
-    step = 128
-    for k in range(0, extent, step):
-        solved = jnp.where(insulated, solve(1, k, k + step), solve(0, k, k + step))
-        for i in range(units):
-            out_ref[k // rows : (k + step) // rows, i] = solved[:, i * lanes : (i + 1) * lanes].reshape(
-                step // rows, rows, lanes
-            )
+    solved = jnp.where(insulated, solve(1), solve(0))
+    for i in range(units):
+        out_ref[:, i] = solved[:, i * lanes : (i + 1) * lanes].reshape(groups, rows, lanes)
 
 
 def column_solve(here, segments, w, x, blocks):
@@ -252,20 +257,27 @@
     )(here, segments, w, x)
 
 
-def place_kernel(x_ref, out_ref):
-    groups = x_ref.shape[0]
-    blocks = out_ref.shape[2] // LANES
+def place_kernel(x_ref, out_hbm, sems):
+    groups, units, _, lanes = x_ref.shape
+    blocks = out_hbm.shape[2] // lanes
+    copies = []
     for p in range(groups):
         q, b = p // blocks, p % blocks
-        out_ref[3 * q : 3 * q + 3, :, b * LANES : (b + 1) * LANES] = x_ref[p]
+        target = out_hbm.at[pl.ds(units * q, units), :, pl.ds(b * lanes, lanes)]
+        copies.append(pltpu.make_async_copy(x_ref.at[p], target, sems.at[p]))
+    for copy in copies:
+        copy.start()
+    for copy in copies:
+        copy.wait()
 
 
 def place(x, shape):
     return pl.pallas_call(
         place_kernel,
         in_specs=[VMEM],
-        out_specs=VMEM,
+        out_specs=HBM,
         out_shape=jax.ShapeDtypeStruct(shape, jnp.float32),
+        scratch_shapes=[pltpu.SemaphoreType.DMA((x.shape[0],))],
         compiler_params=pltpu.CompilerParams(vmem_limit_bytes=16 * 2**20),
         name="place",
     )(x)
@@ -279,14 +291,13 @@
     planes, rows, nx = t.shape
     slabs, groups = lax.axis_size("slab"), lax.axis_size("pencil")
     here = lax.axis_index(("slab", "pencil")).astype(jnp.int32).reshape(1)
-    yc, yd, za, zb = edges(here, t, groups)
-    halos = (
-        lax.ppermute(yc, "slab", [(i, i ^ 1) for i in range(slabs)]),
-        lax.ppermute(yd, "slab", [(i, ((i - 1) ^ 1) + 1 & slabs - 1) for i in range(slabs)]),
-        lax.ppermute(za, "pencil", [(i, i ^ 1) for i in range(groups)]),
-        lax.ppermute(zb, "pencil", [(i, ((i - 1) ^ 1) + 1) for i in range(1, groups - 1)]),
-    )
-    *parts, ah, al = prepare(here, t, u, v, w, downstream_solver_matrix, groups)
+    yc, yd, za, zb, t_halves = edges(here, t, groups)
+    yc = lax.ppermute(yc, "slab", [(i, i ^ 1) for i in range(slabs)])
+    yd = lax.ppermute(yd, "slab", [(i, ((i - 1) ^ 1) + 1 & slabs - 1) for i in range(slabs)])
+    za = lax.ppermute(za, "pencil", [(i, ((i - 1) ^ 1) + 1) for i in range(1, groups - 1)])
+    zb = lax.ppermute(zb, "pencil", [(i, i ^ 1) for i in range(groups)])
+    halos = yc, yd, za, zb
+    *parts, ah, al = prepare(here, t_halves, u, v, w, downstream_solver_matrix, groups)
     x = swapped(row_solve(here, parts, halos, ah, al, groups))
     x = swapped(column_solve(here, wall_segments, wallward_solver_matrices, x, nx // LANES))
     return place(x, t.shape)

time: 79.3 us -> 79.5 us (level)
    pallas_call x2, Pallas kernels: 4.21 us -> 5.18 us  [the longest x1 4.04 us: prepare(): pl.pallas_call(functools.partial(prepare_kernel, groups), in_specs=[SMEM,...]
  transfers between devices with their start and end apart: 4 -> 4, of which waited for: 0 -> 0; matrix products, arithmetic and copies ran while one was open for 0% -> 0% of each run, Pallas kernels for 4% -> 5%
where the time goes in v6:
time: 79.5 us; the launch traced here: 79.2 us
  blocking collectives  58.5 us (74%)
  starting transfers between devices  10.5 us (13%)
  Pallas kernels  10.1 us (13%)
    all_to_all x2, blocking collectives, swapped(): return lax.all_to_all(x, 'pencil', split_axis=0, concat_axis=0, tiled=True)  58.5 us
    ppermute x1, starting transfers between devices, on_device(): lax.ppermute(za, 'pencil', [(i, (i - 1 ^ 1) + 1) for i in range(1, groups...  4.27 us
    pallas_call x1, Pallas kernels, prepare(): pl.pallas_call(functools.partial(prepare_kernel, groups), in_specs=[SMEM,...  4.04 us
    ppermute x1, starting transfers between devices, on_device(): yc = lax.ppermute(yc, 'slab', [(i, i ^ 1) for i in range(slabs)])  3.83 us
    ppermute x1, starting transfers between devices, on_device(): lax.ppermute(yd, 'slab', [(i, (i - 1 ^ 1) + 1 & slabs - 1) for i in range...  2.29 us
    pallas_call x1, Pallas kernels, column_solve(): pl.pallas_call(functools.partial(column_kernel, blocks), in_specs=[SMEM,...  2.12 us
    pallas_call x1, Pallas kernels, row_solve(): pl.pallas_call(row_kernel, in_specs=[SMEM] + [VMEM] * 11, out_specs=VMEM,...  1.67 us
  transfers between devices with their start and end apart: 4, of which 0 were waited for; matrix products, arithmetic and copies ran while one was open for 0% of the time, Pallas kernels for 5%

profile of v6, /device:TPU:1, one launch (start us, length us, event | category | flops | bytes accessed | tf_op | source)
XLA Modules:
  0.0 79.2 jit_solution(10470498898165328483)
XLA Ops:
  0.0 1.2 %edges.1 = (f32[16,1024]{1,0:T(8,128)S(1)}, f32[16,1024]{1,0:T(8,128)S(1)}, f32[12,1024]{1,0:T(8,128)S(1)}, f32[12,1024]{1,0:T(8,128)S(1)}, f32[2,12,8,1024]{3,2,1,0:T(8,128)S(1)}) custom-call(s32[1]{0:T(128)} %bitcast.here_ref, f32[12,16,1024]{2,1,0:T(8,128)} %t_hbm.1), custom_call_target="tpu_custom_call" | custom-call | tf_op jit(solution)/shard_map/edges/pallas_call | solution.py:58
  1.2 3.8 %collective-permute-start = (f32[16,1024]{1,0:T(8,128)S(1)}, f32[16,1024]{1,0:T(8,128)S(1)}, u32[]{:S(2)}, u32[]{:S(2)}) collective-permute-start(f32[16,1024]{1,0:T(8,128)S(1)} %get-tuple-element.23), channel_id=1, source_target_pairs={{0,32},{32,0},{64,96},{96,64},{128,160},{160,128},{192,224},{224,1... | collective-permute-start | bytes 196616 | tf_op jit(solution)/shard_map/ppermute | solution.py:295
  5.0 2.3 %collective-permute-start.1 = (f32[16,1024]{1,0:T(8,128)S(1)}, f32[16,1024]{1,0:T(8,128)S(1)}, u32[]{:S(2)}, u32[]{:S(2)}) collective-permute-start(f32[16,1024]{1,0:T(8,128)S(1)} %get-tuple-element.24), channel_id=1, source_target_pairs={{0,224},{32,64},{64,32},{96,128},{128,96},{160,192},{192,160},{224... | collective-permute-start | bytes 196616 | tf_op jit(solution)/shard_map/ppermute | solution.py:296
  7.3 4.3 %collective-permute-start.2 = (f32[12,1024]{1,0:T(8,128)S(1)}, f32[12,1024]{1,0:T(8,128)S(1)}, u32[]{:S(2)}, u32[]{:S(2)}) collective-permute-start(f32[12,1024]{1,0:T(8,128)S(1)} %get-tuple-element.25), channel_id=1, source_target_pairs={{1,2},{2,1},{3,4},{4,3},{5,6},{6,5},{7,8},{8,7},{9,10},{10,9},{11,... | collective-permute-start | bytes 147464 | tf_op jit(solution)/shard_map/ppermute | solution.py:297
  11.6 0.1 collective-permute-start.3
  11.7 4.0 %prepare.1 = (f32[12,16,1024]{2,1,0:T(8,128)S(1)}, f32[16,1024]{1,0:T(8,128)S(1)}, f32[16,1024]{1,0:T(8,128)S(1)}, f32[12,1024]{1,0:T(8,128)S(1)}, f32[12,1024]{...) custom-call(s32[1]{0:T(128)} %bitcast.here_ref, ...), custom_call_target="tpu_custom_call" | custom-call | flops 12058624 | bytes 11141120 | tf_op jit(solution)/shard_map/prepare/pallas_call | solution.py:150
  15.7 0.0 collective-permute-done.2.za_ref
  15.7 0.0 collective-permute-done.3.zb_ref
  15.8 0.0 collective-permute-done.yc_ref
  15.8 0.0 collective-permute-done.1.yd_ref
  15.8 0.0 copy-start
  15.8 0.0 copy-start.1
  15.8 1.7 %row_solve.1 = f32[32,3,16,128]{3,2,1,0:T(8,128)S(1)} custom-call(s32[1]{0:T(128)} %bitcast.here_ref, f32[12,16,1024]{2,1,0:T(8,128)S(1)} %get-tuple-element.18.side_ref, f32[16,1024]{1,0:T(8,128)S(1)} %get-tuple-element.19.cb_ref, f32[16,1024]{1,0:T(8,128)S(1)} %get-tuple-element.20.ca_ref, f32[12,1024]{1,0:T(8,128)S(1)} %get-tuple-element.21.cl_ref, ...), custom_call_target="tpu_custom_call" | custom-call | flops 1207959552 | bytes 8388608 | tf_op jit(solution)/shard_map/row_solve/pallas_call | solution.py:206
  17.5 31.8 %all_to_all.10.x_ref = f32[32,3,16,128]{3,2,1,0:T(8,128)S(1)} all-to-all(f32[32,3,16,128]{3,2,1,0:T(8,128)S(1)} %row_solve.1), channel_id=1, replica_groups=mesh['slab'=8,'pencil'=32] {'pencil'}, dimensions={0} | all-to-all | bytes 1572864 | tf_op jit(solution)/shard_map/all_to_all | solution.py:287
  49.3 0.0 copy-done
  49.3 0.0 copy-done.1
  49.3 2.1 %column_solve.1 = f32[32,3,16,128]{3,2,1,0:T(8,128)S(1)} custom-call(s32[1]{0:T(128)} %bitcast.here_ref, s32[16]{0:T(128)S(1)} %copy-done.1, f32[2,512,512]{2,1,0:T(8,128)S(1)} %copy-done, f32[32,3,16,128]{3,2,1,0:T(8,128)S(1)} %all_to_all.10.x_ref), custom_call_target="tpu_custom_call" | custom-call | flops 1207959552 | bytes 4194304 | tf_op jit(solution)/shard_map/column_solve/pallas_call | solution.py:247
  51.5 26.6 %all_to_all.11.x_ref = f32[32,3,16,128]{3,2,1,0:T(8,128)S(1)} all-to-all(f32[32,3,16,128]{3,2,1,0:T(8,128)S(1)} %column_solve.1), channel_id=1, replica_groups=mesh['slab'=8,'pencil'=32] {'pencil'}, dimensions={0} | all-to-all | bytes 1572864 | tf_op jit(solution)/shard_map/all_to_all | solution.py:287
  78.1 1.1 %place.1 = f32[12,16,1024]{2,1,0:T(8,128)} custom-call(f32[32,3,16,128]{3,2,1,0:T(8,128)S(1)} %all_to_all.11.x_ref), custom_call_target="tpu_custom_call" | custom-call | tf_op jit(solution)/shard_map/place/pallas_call | solution.py:275
Async XLA Ops:
  1.2 14.6 %collective-permute-start = (f32[16,1024]{1,0:T(8,128)S(1)}, f32[16,1024]{1,0:T(8,128)S(1)}, u32[]{:S(2)}, u32[]{:S(2)}) collective-permute-start(f32[16,1024]{1,0:T(8,128)S(1)} %get-tuple-element.23), channel_id=1, source_target_pairs={{0,32},{32,0},{64,96},{96,64},{128,160},{160,128},{192,224},{224,1... | collective-permute-start | bytes 196616 | tf_op jit(solution)/shard_map/ppermute | solution.py:295
  5.0 10.8 %collective-permute-start.1 = (f32[16,1024]{1,0:T(8,128)S(1)}, f32[16,1024]{1,0:T(8,128)S(1)}, u32[]{:S(2)}, u32[]{:S(2)}) collective-permute-start(f32[16,1024]{1,0:T(8,128)S(1)} %get-tuple-element.24), channel_id=1, source_target_pairs={{0,224},{32,64},{64,32},{96,128},{128,96},{160,192},{192,160},{224... | collective-permute-start | bytes 196616 | tf_op jit(solution)/shard_map/ppermute | solution.py:296
  7.3 8.4 %collective-permute-start.2 = (f32[12,1024]{1,0:T(8,128)S(1)}, f32[12,1024]{1,0:T(8,128)S(1)}, u32[]{:S(2)}, u32[]{:S(2)}) collective-permute-start(f32[12,1024]{1,0:T(8,128)S(1)} %get-tuple-element.25), channel_id=1, source_target_pairs={{1,2},{2,1},{3,4},{4,3},{5,6},{6,5},{7,8},{8,7},{9,10},{10,9},{11,... | collective-permute-start | bytes 147464 | tf_op jit(solution)/shard_map/ppermute | solution.py:297
  11.6 4.2 %collective-permute-start.3 = (f32[12,1024]{1,0:T(8,128)S(1)}, f32[12,1024]{1,0:T(8,128)S(1)}, u32[]{:S(2)}, u32[]{:S(2)}) collective-permute-start(f32[12,1024]{1,0:T(8,128)S(1)} %get-tuple-element.26), channel_id=1, source_target_pairs={{0,1},{1,0},{2,3},{3,2},{4,5},{5,4},{6,7},{7,6},{8,9},{9,8},{10,11... | collective-permute-start | bytes 147464 | tf_op jit(solution)/shard_map/ppermute | solution.py:298
  15.8 33.6 %copy-start = (f32[2,512,512]{2,1,0:T(8,128)S(1)}, f32[2,512,512]{2,1,0:T(8,128)}, u32[]{:S(2)}) copy-start(f32[2,512,512]{2,1,0:T(8,128)} %w_ref.1) | copy-start | bytes 6291460
  15.8 33.5 %copy-start.1 = (s32[16]{0:T(128)S(1)}, s32[16]{0:T(128)}, u32[]{:S(2)}) copy-start(s32[16]{0:T(128)} %seg_ref.1) | copy-start | bytes 196

commit v7 on v6

--- a/solution.py
+++ b/solution.py
@@ -98,15 +98,13 @@
     for i in range(parts):
         cut = slice(i * a_rows, (i + 1) * a_rows)
         copies.append(pltpu.make_async_copy(a_hbm.at[cut], a_buf.at[cut], sems.at[3 + i]))
-    for copy in fields:
+    for copy in fields + copies:
         copy.start()
     levels = (lax.broadcasted_iota(jnp.int32, (rows, LANES), 0) + here_ref[0] % groups * rows).astype(jnp.float32)
     metric = jnp.concatenate([metric_of(levels, groups * rows)] * (nx // LANES), axis=1)
     level = lax.broadcasted_iota(jnp.int32, (rows, nx), 0)
     for copy in fields:
         copy.wait()
-    for copy in copies:
-        copy.start()
 
     def plane(y):
         if y < 0 or y == planes:
@@ -257,27 +255,20 @@
     )(here, segments, w, x)
 
 
-def place_kernel(x_ref, out_hbm, sems):
-    groups, units, _, lanes = x_ref.shape
-    blocks = out_hbm.shape[2] // lanes
-    copies = []
+def place_kernel(x_ref, out_ref):
+    groups = x_ref.shape[0]
+    blocks = out_ref.shape[2] // LANES
     for p in range(groups):
         q, b = p // blocks, p % blocks
-        target = out_hbm.at[pl.ds(units * q, units), :, pl.ds(b * lanes, lanes)]
-        copies.append(pltpu.make_async_copy(x_ref.at[p], target, sems.at[p]))
-    for copy in copies:
-        copy.start()
-    for copy in copies:
-        copy.wait()
+        out_ref[3 * q : 3 * q + 3, :, b * LANES : (b + 1) * LANES] = x_ref[p]
 
 
 def place(x, shape):
     return pl.pallas_call(
         place_kernel,
         in_specs=[VMEM],
-        out_specs=HBM,
+        out_specs=VMEM,
         out_shape=jax.ShapeDtypeStruct(shape, jnp.float32),
-        scratch_shapes=[pltpu.SemaphoreType.DMA((x.shape[0],))],
         compiler_params=pltpu.CompilerParams(vmem_limit_bytes=16 * 2**20),
         name="place",
     )(x)

time: 79.5 us -> 78.8 us (level)
  Pallas kernels: 10.1 us -> 9.04 us
    pallas_call x1, Pallas kernels: 4.04 us -> 3.15 us  [prepare(): pl.pallas_call(functools.partial(prepare_kernel, groups), in_specs=[SMEM,...]
  transfers between devices with their start and end apart: 4 -> 4, of which waited for: 0 -> 0; matrix products, arithmetic and copies ran while one was open for 0% -> 0% of each run, Pallas kernels for 5% -> 4%
where the time goes in v7:
time: 78.8 us; the launch traced here: 78.6 us
  blocking collectives  58.9 us (75%)
  starting transfers between devices  10.5 us (13%)
  Pallas kernels  9.04 us (11%)
    all_to_all x2, blocking collectives, swapped(): return lax.all_to_all(x, 'pencil', split_axis=0, concat_axis=0, tiled=True)  58.9 us
    ppermute x1, starting transfers between devices, on_device(): lax.ppermute(za, 'pencil', [(i, (i - 1 ^ 1) + 1) for i in range(1, groups...  4.27 us
    ppermute x1, starting transfers between devices, on_device(): yc = lax.ppermute(yc, 'slab', [(i, i ^ 1) for i in range(slabs)])  3.83 us
    pallas_call x1, Pallas kernels, prepare(): pl.pallas_call(functools.partial(prepare_kernel, groups), in_specs=[SMEM,...  3.15 us
    ppermute x1, starting transfers between devices, on_device(): lax.ppermute(yd, 'slab', [(i, (i - 1 ^ 1) + 1 & slabs - 1) for i in range...  2.29 us
    pallas_call x1, Pallas kernels, column_solve(): pl.pallas_call(functools.partial(column_kernel, blocks), in_specs=[SMEM,...  2.12 us
    pallas_call x1, Pallas kernels, row_solve(): pl.pallas_call(row_kernel, in_specs=[SMEM] + [VMEM] * 11, out_specs=VMEM,...  1.67 us
  transfers between devices with their start and end apart: 4, of which 0 were waited for; matrix products, arithmetic and copies ran while one was open for 0% of the time, Pallas kernels for 4%

profile of v7, /device:TPU:1, one launch (start us, length us, event | category | flops | bytes accessed | tf_op | source)
XLA Modules:
  0.0 78.6 jit_solution(14118463681122975837)
XLA Ops:
  0.0 1.2 %edges.1 = (f32[16,1024]{1,0:T(8,128)S(1)}, f32[16,1024]{1,0:T(8,128)S(1)}, f32[12,1024]{1,0:T(8,128)S(1)}, f32[12,1024]{1,0:T(8,128)S(1)}, f32[2,12,8,1024]{3,2,1,0:T(8,128)S(1)}) custom-call(s32[1]{0:T(128)} %bitcast.here_ref, f32[12,16,1024]{2,1,0:T(8,128)} %t_hbm.1), custom_call_target="tpu_custom_call" | custom-call | tf_op jit(solution)/shard_map/edges/pallas_call | solution.py:58
  1.2 3.8 %collective-permute-start = (f32[16,1024]{1,0:T(8,128)S(1)}, f32[16,1024]{1,0:T(8,128)S(1)}, u32[]{:S(2)}, u32[]{:S(2)}) collective-permute-start(f32[16,1024]{1,0:T(8,128)S(1)} %get-tuple-element.23), channel_id=1, source_target_pairs={{0,32},{32,0},{64,96},{96,64},{128,160},{160,128},{192,224},{224,1... | collective-permute-start | bytes 196616 | tf_op jit(solution)/shard_map/ppermute | solution.py:286
  5.0 2.3 %collective-permute-start.1 = (f32[16,1024]{1,0:T(8,128)S(1)}, f32[16,1024]{1,0:T(8,128)S(1)}, u32[]{:S(2)}, u32[]{:S(2)}) collective-permute-start(f32[16,1024]{1,0:T(8,128)S(1)} %get-tuple-element.24), channel_id=1, source_target_pairs={{0,224},{32,64},{64,32},{96,128},{128,96},{160,192},{192,160},{224... | collective-permute-start | bytes 196616 | tf_op jit(solution)/shard_map/ppermute | solution.py:287
  7.3 4.3 %collective-permute-start.2 = (f32[12,1024]{1,0:T(8,128)S(1)}, f32[12,1024]{1,0:T(8,128)S(1)}, u32[]{:S(2)}, u32[]{:S(2)}) collective-permute-start(f32[12,1024]{1,0:T(8,128)S(1)} %get-tuple-element.25), channel_id=1, source_target_pairs={{1,2},{2,1},{3,4},{4,3},{5,6},{6,5},{7,8},{8,7},{9,10},{10,9},{11,... | collective-permute-start | bytes 147464 | tf_op jit(solution)/shard_map/ppermute | solution.py:288
  11.6 0.1 collective-permute-start.3
  11.7 3.1 %prepare.1 = (f32[12,16,1024]{2,1,0:T(8,128)S(1)}, f32[16,1024]{1,0:T(8,128)S(1)}, f32[16,1024]{1,0:T(8,128)S(1)}, f32[12,1024]{1,0:T(8,128)S(1)}, f32[12,1024]{...) custom-call(s32[1]{0:T(128)} %bitcast.here_ref, ...), custom_call_target="tpu_custom_call" | custom-call | flops 12058624 | bytes 11141120 | tf_op jit(solution)/shard_map/prepare/pallas_call | solution.py:148
  14.8 0.0 collective-permute-done.2.za_ref
  14.9 0.0 collective-permute-done.3.zb_ref
  14.9 0.0 collective-permute-done.yc_ref
  14.9 0.0 collective-permute-done.1.yd_ref
  14.9 0.0 copy-start
  14.9 0.0 copy-start.1
  14.9 1.7 %row_solve.1 = f32[32,3,16,128]{3,2,1,0:T(8,128)S(1)} custom-call(s32[1]{0:T(128)} %bitcast.here_ref, f32[12,16,1024]{2,1,0:T(8,128)S(1)} %get-tuple-element.18.side_ref, f32[16,1024]{1,0:T(8,128)S(1)} %get-tuple-element.19.cb_ref, f32[16,1024]{1,0:T(8,128)S(1)} %get-tuple-element.20.ca_ref, f32[12,1024]{1,0:T(8,128)S(1)} %get-tuple-element.21.cl_ref, ...), custom_call_target="tpu_custom_call" | custom-call | flops 1207959552 | bytes 8388608 | tf_op jit(solution)/shard_map/row_solve/pallas_call | solution.py:204
  16.6 32.3 %all_to_all.10.x_ref = f32[32,3,16,128]{3,2,1,0:T(8,128)S(1)} all-to-all(f32[32,3,16,128]{3,2,1,0:T(8,128)S(1)} %row_solve.1), channel_id=1, replica_groups=mesh['slab'=8,'pencil'=32] {'pencil'}, dimensions={0} | all-to-all | bytes 1572864 | tf_op jit(solution)/shard_map/all_to_all | solution.py:278
  48.9 0.0 copy-done
  48.9 0.0 copy-done.1
  48.9 2.1 %column_solve.1 = f32[32,3,16,128]{3,2,1,0:T(8,128)S(1)} custom-call(s32[1]{0:T(128)} %bitcast.here_ref, s32[16]{0:T(128)S(1)} %copy-done.1, f32[2,512,512]{2,1,0:T(8,128)S(1)} %copy-done, f32[32,3,16,128]{3,2,1,0:T(8,128)S(1)} %all_to_all.10.x_ref), custom_call_target="tpu_custom_call" | custom-call | flops 1207959552 | bytes 4194304 | tf_op jit(solution)/shard_map/column_solve/pallas_call | solution.py:245
  51.0 26.6 %all_to_all.11.x_ref = f32[32,3,16,128]{3,2,1,0:T(8,128)S(1)} all-to-all(f32[32,3,16,128]{3,2,1,0:T(8,128)S(1)} %column_solve.1), channel_id=1, replica_groups=mesh['slab'=8,'pencil'=32] {'pencil'}, dimensions={0} | all-to-all | bytes 1572864 | tf_op jit(solution)/shard_map/all_to_all | solution.py:278
  77.7 0.9 %place.1 = f32[12,16,1024]{2,1,0:T(8,128)} custom-call(f32[32,3,16,128]{3,2,1,0:T(8,128)S(1)} %all_to_all.11.x_ref), custom_call_target="tpu_custom_call" | custom-call | tf_op jit(solution)/shard_map/place/pallas_call | solution.py:267
Async XLA Ops:
  1.2 13.7 %collective-permute-start = (f32[16,1024]{1,0:T(8,128)S(1)}, f32[16,1024]{1,0:T(8,128)S(1)}, u32[]{:S(2)}, u32[]{:S(2)}) collective-permute-start(f32[16,1024]{1,0:T(8,128)S(1)} %get-tuple-element.23), channel_id=1, source_target_pairs={{0,32},{32,0},{64,96},{96,64},{128,160},{160,128},{192,224},{224,1... | collective-permute-start | bytes 196616 | tf_op jit(solution)/shard_map/ppermute | solution.py:286
  5.0 9.9 %collective-permute-start.1 = (f32[16,1024]{1,0:T(8,128)S(1)}, f32[16,1024]{1,0:T(8,128)S(1)}, u32[]{:S(2)}, u32[]{:S(2)}) collective-permute-start(f32[16,1024]{1,0:T(8,128)S(1)} %get-tuple-element.24), channel_id=1, source_target_pairs={{0,224},{32,64},{64,32},{96,128},{128,96},{160,192},{192,160},{224... | collective-permute-start | bytes 196616 | tf_op jit(solution)/shard_map/ppermute | solution.py:287
  7.3 7.5 %collective-permute-start.2 = (f32[12,1024]{1,0:T(8,128)S(1)}, f32[12,1024]{1,0:T(8,128)S(1)}, u32[]{:S(2)}, u32[]{:S(2)}) collective-permute-start(f32[12,1024]{1,0:T(8,128)S(1)} %get-tuple-element.25), channel_id=1, source_target_pairs={{1,2},{2,1},{3,4},{4,3},{5,6},{6,5},{7,8},{8,7},{9,10},{10,9},{11,... | collective-permute-start | bytes 147464 | tf_op jit(solution)/shard_map/ppermute | solution.py:288
  11.6 3.3 %collective-permute-start.3 = (f32[12,1024]{1,0:T(8,128)S(1)}, f32[12,1024]{1,0:T(8,128)S(1)}, u32[]{:S(2)}, u32[]{:S(2)}) collective-permute-start(f32[12,1024]{1,0:T(8,128)S(1)} %get-tuple-element.26), channel_id=1, source_target_pairs={{0,1},{1,0},{2,3},{3,2},{4,5},{5,4},{6,7},{7,6},{8,9},{9,8},{10,11... | collective-permute-start | bytes 147464 | tf_op jit(solution)/shard_map/ppermute | solution.py:289
  14.9 34.0 %copy-start = (f32[2,512,512]{2,1,0:T(8,128)S(1)}, f32[2,512,512]{2,1,0:T(8,128)}, u32[]{:S(2)}) copy-start(f32[2,512,512]{2,1,0:T(8,128)} %w_ref.1) | copy-start | bytes 6291460
  14.9 34.0 %copy-start.1 = (s32[16]{0:T(128)S(1)}, s32[16]{0:T(128)}, u32[]{:S(2)}) copy-start(s32[16]{0:T(128)} %seg_ref.1) | copy-start | bytes 196

commit v8 on v7

--- a/solution.py
+++ b/solution.py
@@ -141,29 +141,54 @@
 
 def prepare(here, t, u, v, w, a, groups):
     planes, rows, nx = u.shape
-    a16 = jax.ShapeDtypeStruct(a.shape, jnp.bfloat16)
+    half = (a.shape[0] // 2, a.shape[1])
+    a16 = jax.ShapeDtypeStruct(half, jnp.bfloat16)
     plane = jax.ShapeDtypeStruct((rows, nx), t.dtype)
     level = jax.ShapeDtypeStruct((planes, nx), t.dtype)
-    parts = 4
+    parts = 2
     return pl.pallas_call(
         functools.partial(prepare_kernel, groups),
         in_specs=[SMEM, VMEM] + [HBM] * 4,
         out_specs=[VMEM] * 7,
         out_shape=[jax.ShapeDtypeStruct(u.shape, t.dtype), plane, plane, level, level, a16, a16],
-        scratch_shapes=[pltpu.VMEM(x.shape, x.dtype) for x in (u, v, w, a)]
-        + [pltpu.SemaphoreType.DMA((3 + parts,))],
+        scratch_shapes=[pltpu.VMEM(x.shape, x.dtype) for x in (u, v, w)]
+        + [pltpu.VMEM(half, a.dtype), pltpu.SemaphoreType.DMA((3 + parts,))],
         compiler_params=pltpu.CompilerParams(vmem_limit_bytes=16 * 2**20),
         cost_estimate=pl.CostEstimate(
-            flops=4 * a.size + 40 * t.size, bytes_accessed=8 * a.size + 14 * t.size, transcendentals=0
+            flops=2 * a.size + 40 * t.size, bytes_accessed=4 * a.size + 14 * t.size, transcendentals=0
         ),
         name="prepare",
     )(here, t, *(pinned(x) for x in (u, v, w, a)))
 
 
 def row_kernel(
-    here_ref, side_ref, cb_ref, ca_ref, cl_ref, ch_ref, yc_ref, yd_ref, za_ref, zb_ref, ah_ref, al_ref, out_ref, both
+    here_ref,
+    side_ref,
+    cb_ref,
+    ca_ref,
+    cl_ref,
+    ch_ref,
+    yc_ref,
+    yd_ref,
+    za_ref,
+    zb_ref,
+    ah_ref,
+    al_ref,
+    a_hbm,
+    out_ref,
+    both,
+    a_buf,
+    sems,
 ):
     planes, rows, nx = side_ref.shape
+    wide = 2 * LANES
+    ready = ah_ref.shape[0] // wide
+    copies = []
+    for c in range(sems.shape[0]):
+        source = a_hbm.at[pl.ds((ready + c) * wide, wide)]
+        copies.append(pltpu.make_async_copy(source, a_buf.at[pl.ds(c * wide, wide)], sems.at[c]))
+    for copy in copies:
+        copy.start()
     groups = out_ref.shape[0]
     pencil_even, slab_even = here_ref[0] % 2 == 0, here_ref[0] // groups % 2 == 0
     low = cl_ref[...] * jnp.where(pencil_even, za_ref[...], zb_ref[...])
@@ -181,12 +206,14 @@
         high_part, low_part = halves(side)
         both[y * rows : (y + 1) * rows, :] = high_part
         both[extent + y * rows : extent + (y + 1) * rows, :] = low_part
-    wide = 2 * LANES
     unit_rows = 3 * rows
     blocks = nx // LANES
     for c in range(nx // wide):
-        ah = ah_ref[c * wide : (c + 1) * wide, :]
-        al = al_ref[c * wide : (c + 1) * wide, :]
+        if c < ready:
+            ah, al = ah_ref[c * wide : (c + 1) * wide, :], al_ref[c * wide : (c + 1) * wide, :]
+        else:
+            copies[c - ready].wait()
+            ah, al = halves(a_buf[(c - ready) * wide : (c - ready + 1) * wide, :])
 
         def dot(x, m):
             return lax.dot_general(x, m, (((1,), (1,)), ((), ())), preferred_element_type=jnp.float32)
@@ -199,20 +226,24 @@
                 out_ref[q * blocks + 2 * c + h] = piece.reshape(3, rows, LANES)
 
 
-def row_solve(here, parts, halos, ah, al, groups):
+def row_solve(here, parts, halos, ah, al, a, groups):
     planes, rows, nx = parts[0].shape
     return pl.pallas_call(
         row_kernel,
-        in_specs=[SMEM] + [VMEM] * 11,
+        in_specs=[SMEM] + [VMEM] * 11 + [HBM],
         out_specs=VMEM,
         out_shape=jax.ShapeDtypeStruct((groups, 3, rows, LANES), jnp.float32),
-        scratch_shapes=[pltpu.VMEM((2 * planes * rows, nx), jnp.bfloat16)],
+        scratch_shapes=[
+            pltpu.VMEM((2 * planes * rows, nx), jnp.bfloat16),
+            pltpu.VMEM((nx - ah.shape[0], nx), a.dtype),
+            pltpu.SemaphoreType.DMA(((nx - ah.shape[0]) // (2 * LANES),)),
+        ],
         compiler_params=pltpu.CompilerParams(vmem_limit_bytes=32 * 2**20),
         cost_estimate=pl.CostEstimate(
             flops=6 * planes * rows * nx * nx, bytes_accessed=8 * 2**20, transcendentals=0
         ),
         name="row_solve",
-    )(here, *parts, *halos, ah, al)
+    )(here, *parts, *halos, ah, al, pinned(a))
 
 
 def column_kernel(blocks, here_ref, seg_ref, w_ref, x_ref, out_ref):
@@ -289,7 +320,7 @@
     zb = lax.ppermute(zb, "pencil", [(i, i ^ 1) for i in range(groups)])
     halos = yc, yd, za, zb
     *parts, ah, al = prepare(here, t_halves, u, v, w, downstream_solver_matrix, groups)
-    x = swapped(row_solve(here, parts, halos, ah, al, groups))
+    x = swapped(row_solve(here, parts, halos, ah, al, downstream_solver_matrix, groups))
     x = swapped(column_solve(here, wall_segments, wallward_solver_matrices, x, nx // LANES))
     return place(x, t.shape)
 

time: 78.8 us -> 80.8 us (1.025)
  Pallas kernels: 9.04 us -> 10.7 us
    pallas_call x1, Pallas kernels: 1.67 us -> 3.68 us  [row_solve(): pl.pallas_call(row_kernel, in_specs=[SMEM] + [VMEM] * 11 + [HBM], out_spe...]
where the time goes in v8:
time: 80.8 us; the launch traced here: 80.6 us
  blocking collectives  59.2 us (73%)
  Pallas kernels  10.7 us (13%)
  starting transfers between devices  10.5 us (13%)
    all_to_all x2, blocking collectives, swapped(): return lax.all_to_all(x, 'pencil', split_axis=0, concat_axis=0, tiled=True)  59.2 us
    ppermute x1, starting transfers between devices, on_device(): lax.ppermute(za, 'pencil', [(i, (i - 1 ^ 1) + 1) for i in range(1, groups...  4.27 us
    ppermute x1, starting transfers between devices, on_device(): yc = lax.ppermute(yc, 'slab', [(i, i ^ 1) for i in range(slabs)])  3.83 us
    pallas_call x1, Pallas kernels, row_solve(): pl.pallas_call(row_kernel, in_specs=[SMEM] + [VMEM] * 11 + [HBM], out_spe...  3.68 us
    pallas_call x1, Pallas kernels, prepare(): pl.pallas_call(functools.partial(prepare_kernel, groups), in_specs=[SMEM,...  2.85 us
    ppermute x1, starting transfers between devices, on_device(): lax.ppermute(yd, 'slab', [(i, (i - 1 ^ 1) + 1 & slabs - 1) for i in range...  2.29 us
    pallas_call x1, Pallas kernels, column_solve(): pl.pallas_call(functools.partial(column_kernel, blocks), in_specs=[SMEM,...  2.12 us
  transfers between devices with their start and end apart: 4, of which 0 were waited for; matrix products, arithmetic and copies ran while one was open for 0% of the time, Pallas kernels for 4%

profile of v8, /device:TPU:1, one launch (start us, length us, event | category | flops | bytes accessed | tf_op | source)
XLA Modules:
  0.0 80.6 jit_solution(6797945948045775322)
XLA Ops:
  0.0 1.2 %edges.1 = (f32[16,1024]{1,0:T(8,128)S(1)}, f32[16,1024]{1,0:T(8,128)S(1)}, f32[12,1024]{1,0:T(8,128)S(1)}, f32[12,1024]{1,0:T(8,128)S(1)}, f32[2,12,8,1024]{3,2,1,0:T(8,128)S(1)}) custom-call(s32[1]{0:T(128)} %bitcast.here_ref, f32[12,16,1024]{2,1,0:T(8,128)} %t_hbm.1), custom_call_target="tpu_custom_call" | custom-call | tf_op jit(solution)/shard_map/edges/pallas_call | solution.py:58
  1.2 3.8 %collective-permute-start = (f32[16,1024]{1,0:T(8,128)S(1)}, f32[16,1024]{1,0:T(8,128)S(1)}, u32[]{:S(2)}, u32[]{:S(2)}) collective-permute-start(f32[16,1024]{1,0:T(8,128)S(1)} %get-tuple-element.23), channel_id=1, source_target_pairs={{0,32},{32,0},{64,96},{96,64},{128,160},{160,128},{192,224},{224,1... | collective-permute-start | bytes 196616 | tf_op jit(solution)/shard_map/ppermute | solution.py:317
  5.0 2.3 %collective-permute-start.1 = (f32[16,1024]{1,0:T(8,128)S(1)}, f32[16,1024]{1,0:T(8,128)S(1)}, u32[]{:S(2)}, u32[]{:S(2)}) collective-permute-start(f32[16,1024]{1,0:T(8,128)S(1)} %get-tuple-element.24), channel_id=1, source_target_pairs={{0,224},{32,64},{64,32},{96,128},{128,96},{160,192},{192,160},{224... | collective-permute-start | bytes 196616 | tf_op jit(solution)/shard_map/ppermute | solution.py:318
  7.3 4.3 %collective-permute-start.2 = (f32[12,1024]{1,0:T(8,128)S(1)}, f32[12,1024]{1,0:T(8,128)S(1)}, u32[]{:S(2)}, u32[]{:S(2)}) collective-permute-start(f32[12,1024]{1,0:T(8,128)S(1)} %get-tuple-element.25), channel_id=1, source_target_pairs={{1,2},{2,1},{3,4},{4,3},{5,6},{6,5},{7,8},{8,7},{9,10},{10,9},{11,... | collective-permute-start | bytes 147464 | tf_op jit(solution)/shard_map/ppermute | solution.py:319
  11.6 0.1 collective-permute-start.3
  11.7 2.8 %prepare.1 = (f32[12,16,1024]{2,1,0:T(8,128)S(1)}, f32[16,1024]{1,0:T(8,128)S(1)}, f32[16,1024]{1,0:T(8,128)S(1)}, f32[12,1024]{1,0:T(8,128)S(1)}, f32[12,1024]{...) custom-call(s32[1]{0:T(128)} %bitcast.here_ref, ...), custom_call_target="tpu_custom_call" | custom-call | flops 9961472 | bytes 6946816 | tf_op jit(solution)/shard_map/prepare/pallas_call | solution.py:149
  14.5 0.0 collective-permute-done.2.za_ref
  14.6 0.0 collective-permute-done.3.zb_ref
  14.6 0.0 collective-permute-done.yc_ref
  14.6 0.0 collective-permute-done.1.yd_ref
  14.6 0.0 copy-start
  14.6 0.0 copy-start.1
  14.6 3.7 %row_solve.1 = f32[32,3,16,128]{3,2,1,0:T(8,128)S(1)} custom-call(s32[1]{0:T(128)} %bitcast.here_ref, f32[12,16,1024]{2,1,0:T(8,128)S(1)} %get-tuple-element.18.side_ref, f32[16,1024]{1,0:T(8,128)S(1)} %get-tuple-element.19.cb_ref, f32[16,1024]{1,0:T(8,128)S(1)} %get-tuple-element.20.ca_ref, f32[12,1024]{1,0:T(8,128)S(1)} %get-tuple-element.21.cl_ref, ...), custom_call_target="tpu_custom_call" | custom-call | flops 1207959552 | bytes 8388608 | tf_op jit(solution)/shard_map/row_solve/pallas_call | solution.py:231
  18.3 32.6 %all_to_all.10.x_ref = f32[32,3,16,128]{3,2,1,0:T(8,128)S(1)} all-to-all(f32[32,3,16,128]{3,2,1,0:T(8,128)S(1)} %row_solve.1), channel_id=1, replica_groups=mesh['slab'=8,'pencil'=32] {'pencil'}, dimensions={0} | all-to-all | bytes 1572864 | tf_op jit(solution)/shard_map/all_to_all | solution.py:309
  50.9 0.0 copy-done
  50.9 0.0 copy-done.1
  50.9 2.1 %column_solve.1 = f32[32,3,16,128]{3,2,1,0:T(8,128)S(1)} custom-call(s32[1]{0:T(128)} %bitcast.here_ref, s32[16]{0:T(128)S(1)} %copy-done.1, f32[2,512,512]{2,1,0:T(8,128)S(1)} %copy-done, f32[32,3,16,128]{3,2,1,0:T(8,128)S(1)} %all_to_all.10.x_ref), custom_call_target="tpu_custom_call" | custom-call | flops 1207959552 | bytes 4194304 | tf_op jit(solution)/shard_map/column_solve/pallas_call | solution.py:276
  53.1 26.6 %all_to_all.11.x_ref = f32[32,3,16,128]{3,2,1,0:T(8,128)S(1)} all-to-all(f32[32,3,16,128]{3,2,1,0:T(8,128)S(1)} %column_solve.1), channel_id=1, replica_groups=mesh['slab'=8,'pencil'=32] {'pencil'}, dimensions={0} | all-to-all | bytes 1572864 | tf_op jit(solution)/shard_map/all_to_all | solution.py:309
  79.7 0.9 %place.1 = f32[12,16,1024]{2,1,0:T(8,128)} custom-call(f32[32,3,16,128]{3,2,1,0:T(8,128)S(1)} %all_to_all.11.x_ref), custom_call_target="tpu_custom_call" | custom-call | tf_op jit(solution)/shard_map/place/pallas_call | solution.py:298
Async XLA Ops:
  1.2 13.4 %collective-permute-start = (f32[16,1024]{1,0:T(8,128)S(1)}, f32[16,1024]{1,0:T(8,128)S(1)}, u32[]{:S(2)}, u32[]{:S(2)}) collective-permute-start(f32[16,1024]{1,0:T(8,128)S(1)} %get-tuple-element.23), channel_id=1, source_target_pairs={{0,32},{32,0},{64,96},{96,64},{128,160},{160,128},{192,224},{224,1... | collective-permute-start | bytes 196616 | tf_op jit(solution)/shard_map/ppermute | solution.py:317
  5.0 9.6 %collective-permute-start.1 = (f32[16,1024]{1,0:T(8,128)S(1)}, f32[16,1024]{1,0:T(8,128)S(1)}, u32[]{:S(2)}, u32[]{:S(2)}) collective-permute-start(f32[16,1024]{1,0:T(8,128)S(1)} %get-tuple-element.24), channel_id=1, source_target_pairs={{0,224},{32,64},{64,32},{96,128},{128,96},{160,192},{192,160},{224... | collective-permute-start | bytes 196616 | tf_op jit(solution)/shard_map/ppermute | solution.py:318
  7.3 7.2 %collective-permute-start.2 = (f32[12,1024]{1,0:T(8,128)S(1)}, f32[12,1024]{1,0:T(8,128)S(1)}, u32[]{:S(2)}, u32[]{:S(2)}) collective-permute-start(f32[12,1024]{1,0:T(8,128)S(1)} %get-tuple-element.25), channel_id=1, source_target_pairs={{1,2},{2,1},{3,4},{4,3},{5,6},{6,5},{7,8},{8,7},{9,10},{10,9},{11,... | collective-permute-start | bytes 147464 | tf_op jit(solution)/shard_map/ppermute | solution.py:319
  11.6 3.0 %collective-permute-start.3 = (f32[12,1024]{1,0:T(8,128)S(1)}, f32[12,1024]{1,0:T(8,128)S(1)}, u32[]{:S(2)}, u32[]{:S(2)}) collective-permute-start(f32[12,1024]{1,0:T(8,128)S(1)} %get-tuple-element.26), channel_id=1, source_target_pairs={{0,1},{1,0},{2,3},{3,2},{4,5},{5,4},{6,7},{7,6},{8,9},{9,8},{10,11... | collective-permute-start | bytes 147464 | tf_op jit(solution)/shard_map/ppermute | solution.py:320
  14.6 36.3 %copy-start = (f32[2,512,512]{2,1,0:T(8,128)S(1)}, f32[2,512,512]{2,1,0:T(8,128)}, u32[]{:S(2)}) copy-start(f32[2,512,512]{2,1,0:T(8,128)} %w_ref.1) | copy-start | bytes 6291460
  14.6 36.3 %copy-start.1 = (s32[16]{0:T(128)S(1)}, s32[16]{0:T(128)}, u32[]{:S(2)}) copy-start(s32[16]{0:T(128)} %seg_ref.1) | copy-start | bytes 196

commit v9 on v7

--- a/solution.py
+++ b/solution.py
@@ -84,6 +84,8 @@
     u_ref,
     v_ref,
     w_ref,
+    along_ref,
+    wallward_ref,
     a_buf,
     sems,
 ):
@@ -103,30 +105,36 @@
     levels = (lax.broadcasted_iota(jnp.int32, (rows, LANES), 0) + here_ref[0] % groups * rows).astype(jnp.float32)
     metric = jnp.concatenate([metric_of(levels, groups * rows)] * (nx // LANES), axis=1)
     level = lax.broadcasted_iota(jnp.int32, (rows, nx), 0)
-    for copy in fields:
-        copy.wait()
 
     def plane(y):
         if y < 0 or y == planes:
             return jnp.zeros((rows, nx), jnp.float32)
         return jnp.concatenate([t_ref[0, y], t_ref[1, y]], axis=0)
 
+    own = (1.0 - 3.0 * CONDUCTION_PART) - CONDUCTION_PART * metric
+    near, far = 0.5 * CONDUCTION_PART * metric, TRANSPORT_PART * metric
     for y in range(planes):
         t, ahead, behind = plane(y), plane(y + 1), plane(y - 1)
         east = pltpu.roll(t, nx - 1, 1)
         west = pltpu.roll(t, 1, 1)
         above = jnp.where(level == rows - 1, 0.0, pltpu.roll(t, rows - 1, 0))
         below = jnp.where(level == 0, 0.0, pltpu.roll(t, 1, 0))
+        side_ref[y] = (
+            own * t
+            + CONDUCTION_PART * (ahead + behind)
+            + 0.5 * CONDUCTION_PART * (east + west)
+            + near * (above + below)
+        )
+        along_ref[y] = 0.5 * TRANSPORT_PART * (east - west)
+        wallward_ref[y] = far * (above - below)
+    for copy in fields:
+        copy.wait()
+    for y in range(planes):
         u = u_ref[y].astype(jnp.float32)
         v = v_ref[y].astype(jnp.float32)
         w = w_ref[y].astype(jnp.float32)
-        carried = 0.5 * u * (east - west) + 0.5 * v * (ahead - behind) + w * metric * (above - below)
-        conducted = (
-            (ahead - 2.0 * t + behind)
-            + 0.5 * (east - 2.0 * t + west)
-            + 0.5 * metric * (above - 2.0 * t + below)
-        )
-        side_ref[y] = t - TRANSPORT_PART * carried + CONDUCTION_PART * conducted
+        across = 0.5 * TRANSPORT_PART * (plane(y + 1) - plane(y - 1))
+        side_ref[y] = side_ref[y] - (u * along_ref[y] + v * across + w * wallward_ref[y])
         cl_ref[y : y + 1, :] = (metric * (0.5 * CONDUCTION_PART + TRANSPORT_PART * w))[:1, :]
         ch_ref[y : y + 1, :] = (metric * (0.5 * CONDUCTION_PART - TRANSPORT_PART * w))[rows - 1 :, :]
         if y == 0:
@@ -150,9 +158,11 @@
         in_specs=[SMEM, VMEM] + [HBM] * 4,
         out_specs=[VMEM] * 7,
         out_shape=[jax.ShapeDtypeStruct(u.shape, t.dtype), plane, plane, level, level, a16, a16],
-        scratch_shapes=[pltpu.VMEM(x.shape, x.dtype) for x in (u, v, w, a)]
+        scratch_shapes=[pltpu.VMEM(x.shape, x.dtype) for x in (u, v, w)]
+        + [pltpu.VMEM(u.shape, t.dtype)] * 2
+        + [pltpu.VMEM(a.shape, a.dtype)]
         + [pltpu.SemaphoreType.DMA((3 + parts,))],
-        compiler_params=pltpu.CompilerParams(vmem_limit_bytes=16 * 2**20),
+        compiler_params=pltpu.CompilerParams(vmem_limit_bytes=20 * 2**20),
         cost_estimate=pl.CostEstimate(
             flops=4 * a.size + 40 * t.size, bytes_accessed=8 * a.size + 14 * t.size, transcendentals=0
         ),
@@ -230,15 +240,19 @@
     both = jnp.concatenate([xh, xl], axis=1)
     width = units * lanes
 
-    def solve(c):
-        wh, wl = halves(w_ref[c])
+    def solve(c, cut):
+        wh, wl = halves(w_ref[c, cut])
         d = jnp.dot(wh, both, preferred_element_type=jnp.float32)
         e = jnp.dot(wl, xh, preferred_element_type=jnp.float32)
         return d[:, :width] + (d[:, width:] + e)
 
-    solved = jnp.where(insulated, solve(1), solve(0))
-    for i in range(units):
-        out_ref[:, i] = solved[:, i * lanes : (i + 1) * lanes].reshape(groups, rows, lanes)
+    step = 256
+    for k in range(0, extent, step):
+        cut = slice(k, k + step)
+        solved = jnp.where(insulated, solve(1, cut), solve(0, cut))
+        for i in range(units):
+            piece = solved[:, i * lanes : (i + 1) * lanes]
+            out_ref[k // rows : (k + step) // rows, i] = piece.reshape(step // rows, rows, lanes)
 
 
 def column_solve(here, segments, w, x, blocks):

time: 78.8 us -> 78.8 us (level)
  no operation moved by 1% of the time
where the time goes in v9:
time: 78.8 us; the launch traced here: 78.6 us
  blocking collectives  59 us (75%)
  starting transfers between devices  10.5 us (13%)
  Pallas kernels  8.98 us (11%)
    all_to_all x2, blocking collectives, swapped(): return lax.all_to_all(x, 'pencil', split_axis=0, concat_axis=0, tiled=True)  59 us
    ppermute x1, starting transfers between devices, on_device(): lax.ppermute(za, 'pencil', [(i, (i - 1 ^ 1) + 1) for i in range(1, groups...  4.27 us
    ppermute x1, starting transfers between devices, on_device(): yc = lax.ppermute(yc, 'slab', [(i, i ^ 1) for i in range(slabs)])  3.83 us
    pallas_call x1, Pallas kernels, prepare(): pl.pallas_call(functools.partial(prepare_kernel, groups), in_specs=[SMEM,...  3.03 us
    ppermute x1, starting transfers between devices, on_device(): lax.ppermute(yd, 'slab', [(i, (i - 1 ^ 1) + 1 & slabs - 1) for i in range...  2.29 us
    pallas_call x1, Pallas kernels, column_solve(): pl.pallas_call(functools.partial(column_kernel, blocks), in_specs=[SMEM,...  2.18 us
    pallas_call x1, Pallas kernels, row_solve(): pl.pallas_call(row_kernel, in_specs=[SMEM] + [VMEM] * 11, out_specs=VMEM,...  1.67 us
  transfers between devices with their start and end apart: 4, of which 0 were waited for; matrix products, arithmetic and copies ran while one was open for 0% of the time, Pallas kernels for 4%

profile of v9, /device:TPU:1, one launch (start us, length us, event | category | flops | bytes accessed | tf_op | source)
XLA Modules:
  0.0 78.6 jit_solution(11509940828329817837)
XLA Ops:
  0.0 1.2 %edges.1 = (f32[16,1024]{1,0:T(8,128)S(1)}, f32[16,1024]{1,0:T(8,128)S(1)}, f32[12,1024]{1,0:T(8,128)S(1)}, f32[12,1024]{1,0:T(8,128)S(1)}, f32[2,12,8,1024]{3,2,1,0:T(8,128)S(1)}) custom-call(s32[1]{0:T(128)} %bitcast.here_ref, f32[12,16,1024]{2,1,0:T(8,128)} %t_hbm.1), custom_call_target="tpu_custom_call" | custom-call | tf_op jit(solution)/shard_map/edges/pallas_call | solution.py:58
  1.2 3.8 %collective-permute-start = (f32[16,1024]{1,0:T(8,128)S(1)}, f32[16,1024]{1,0:T(8,128)S(1)}, u32[]{:S(2)}, u32[]{:S(2)}) collective-permute-start(f32[16,1024]{1,0:T(8,128)S(1)} %get-tuple-element.23), channel_id=1, source_target_pairs={{0,32},{32,0},{64,96},{96,64},{128,160},{160,128},{192,224},{224,1... | collective-permute-start | bytes 196616 | tf_op jit(solution)/shard_map/ppermute | solution.py:300
  5.0 2.3 %collective-permute-start.1 = (f32[16,1024]{1,0:T(8,128)S(1)}, f32[16,1024]{1,0:T(8,128)S(1)}, u32[]{:S(2)}, u32[]{:S(2)}) collective-permute-start(f32[16,1024]{1,0:T(8,128)S(1)} %get-tuple-element.24), channel_id=1, source_target_pairs={{0,224},{32,64},{64,32},{96,128},{128,96},{160,192},{192,160},{224... | collective-permute-start | bytes 196616 | tf_op jit(solution)/shard_map/ppermute | solution.py:301
  7.3 4.3 %collective-permute-start.2 = (f32[12,1024]{1,0:T(8,128)S(1)}, f32[12,1024]{1,0:T(8,128)S(1)}, u32[]{:S(2)}, u32[]{:S(2)}) collective-permute-start(f32[12,1024]{1,0:T(8,128)S(1)} %get-tuple-element.25), channel_id=1, source_target_pairs={{1,2},{2,1},{3,4},{4,3},{5,6},{6,5},{7,8},{8,7},{9,10},{10,9},{11,... | collective-permute-start | bytes 147464 | tf_op jit(solution)/shard_map/ppermute | solution.py:302
  11.6 0.1 collective-permute-start.3
  11.7 3.0 %prepare.1 = (f32[12,16,1024]{2,1,0:T(8,128)S(1)}, f32[16,1024]{1,0:T(8,128)S(1)}, f32[16,1024]{1,0:T(8,128)S(1)}, f32[12,1024]{1,0:T(8,128)S(1)}, f32[12,1024]{...) custom-call(s32[1]{0:T(128)} %bitcast.here_ref, ...), custom_call_target="tpu_custom_call" | custom-call | flops 12058624 | bytes 11141120 | tf_op jit(solution)/shard_map/prepare/pallas_call | solution.py:156
  14.7 0.0 collective-permute-done.2.za_ref
  14.7 0.0 collective-permute-done.3.zb_ref
  14.8 0.0 collective-permute-done.yc_ref
  14.8 0.0 collective-permute-done.1.yd_ref
  14.8 0.0 copy-start
  14.8 0.0 copy-start.1
  14.8 1.7 %row_solve.1 = f32[32,3,16,128]{3,2,1,0:T(8,128)S(1)} custom-call(s32[1]{0:T(128)} %bitcast.here_ref, f32[12,16,1024]{2,1,0:T(8,128)S(1)} %get-tuple-element.18.side_ref, f32[16,1024]{1,0:T(8,128)S(1)} %get-tuple-element.19.cb_ref, f32[16,1024]{1,0:T(8,128)S(1)} %get-tuple-element.20.ca_ref, f32[12,1024]{1,0:T(8,128)S(1)} %get-tuple-element.21.cl_ref, ...), custom_call_target="tpu_custom_call" | custom-call | flops 1207959552 | bytes 8388608 | tf_op jit(solution)/shard_map/row_solve/pallas_call | solution.py:214
  16.5 32.4 %all_to_all.10.x_ref = f32[32,3,16,128]{3,2,1,0:T(8,128)S(1)} all-to-all(f32[32,3,16,128]{3,2,1,0:T(8,128)S(1)} %row_solve.1), channel_id=1, replica_groups=mesh['slab'=8,'pencil'=32] {'pencil'}, dimensions={0} | all-to-all | bytes 1572864 | tf_op jit(solution)/shard_map/all_to_all | solution.py:292
  48.9 0.0 copy-done
  48.9 0.0 copy-done.1
  48.9 2.2 %column_solve.1 = f32[32,3,16,128]{3,2,1,0:T(8,128)S(1)} custom-call(s32[1]{0:T(128)} %bitcast.here_ref, s32[16]{0:T(128)S(1)} %copy-done.1, f32[2,512,512]{2,1,0:T(8,128)S(1)} %copy-done, f32[32,3,16,128]{3,2,1,0:T(8,128)S(1)} %all_to_all.10.x_ref), custom_call_target="tpu_custom_call" | custom-call | flops 1207959552 | bytes 4194304 | tf_op jit(solution)/shard_map/column_solve/pallas_call | solution.py:259
  51.1 26.6 %all_to_all.11.x_ref = f32[32,3,16,128]{3,2,1,0:T(8,128)S(1)} all-to-all(f32[32,3,16,128]{3,2,1,0:T(8,128)S(1)} %column_solve.1), channel_id=1, replica_groups=mesh['slab'=8,'pencil'=32] {'pencil'}, dimensions={0} | all-to-all | bytes 1572864 | tf_op jit(solution)/shard_map/all_to_all | solution.py:292
  77.7 0.9 %place.1 = f32[12,16,1024]{2,1,0:T(8,128)} custom-call(f32[32,3,16,128]{3,2,1,0:T(8,128)S(1)} %all_to_all.11.x_ref), custom_call_target="tpu_custom_call" | custom-call | tf_op jit(solution)/shard_map/place/pallas_call | solution.py:281
Async XLA Ops:
  1.2 13.6 %collective-permute-start = (f32[16,1024]{1,0:T(8,128)S(1)}, f32[16,1024]{1,0:T(8,128)S(1)}, u32[]{:S(2)}, u32[]{:S(2)}) collective-permute-start(f32[16,1024]{1,0:T(8,128)S(1)} %get-tuple-element.23), channel_id=1, source_target_pairs={{0,32},{32,0},{64,96},{96,64},{128,160},{160,128},{192,224},{224,1... | collective-permute-start | bytes 196616 | tf_op jit(solution)/shard_map/ppermute | solution.py:300
  5.0 9.7 %collective-permute-start.1 = (f32[16,1024]{1,0:T(8,128)S(1)}, f32[16,1024]{1,0:T(8,128)S(1)}, u32[]{:S(2)}, u32[]{:S(2)}) collective-permute-start(f32[16,1024]{1,0:T(8,128)S(1)} %get-tuple-element.24), channel_id=1, source_target_pairs={{0,224},{32,64},{64,32},{96,128},{128,96},{160,192},{192,160},{224... | collective-permute-start | bytes 196616 | tf_op jit(solution)/shard_map/ppermute | solution.py:301
  7.3 7.4 %collective-permute-start.2 = (f32[12,1024]{1,0:T(8,128)S(1)}, f32[12,1024]{1,0:T(8,128)S(1)}, u32[]{:S(2)}, u32[]{:S(2)}) collective-permute-start(f32[12,1024]{1,0:T(8,128)S(1)} %get-tuple-element.25), channel_id=1, source_target_pairs={{1,2},{2,1},{3,4},{4,3},{5,6},{6,5},{7,8},{8,7},{9,10},{10,9},{11,... | collective-permute-start | bytes 147464 | tf_op jit(solution)/shard_map/ppermute | solution.py:302
  11.6 3.2 %collective-permute-start.3 = (f32[12,1024]{1,0:T(8,128)S(1)}, f32[12,1024]{1,0:T(8,128)S(1)}, u32[]{:S(2)}, u32[]{:S(2)}) collective-permute-start(f32[12,1024]{1,0:T(8,128)S(1)} %get-tuple-element.26), channel_id=1, source_target_pairs={{0,1},{1,0},{2,3},{3,2},{4,5},{5,4},{6,7},{7,6},{8,9},{9,8},{10,11... | collective-permute-start | bytes 147464 | tf_op jit(solution)/shard_map/ppermute | solution.py:303
  14.8 34.1 %copy-start = (f32[2,512,512]{2,1,0:T(8,128)S(1)}, f32[2,512,512]{2,1,0:T(8,128)}, u32[]{:S(2)}) copy-start(f32[2,512,512]{2,1,0:T(8,128)} %w_ref.1) | copy-start | bytes 6291460
  14.8 34.1 %copy-start.1 = (s32[16]{0:T(128)S(1)}, s32[16]{0:T(128)}, u32[]{:S(2)}) copy-start(s32[16]{0:T(128)} %seg_ref.1) | copy-start | bytes 196

commit v10 on v8

--- a/solution.py
+++ b/solution.py
@@ -84,6 +84,8 @@
     u_ref,
     v_ref,
     w_ref,
+    along_ref,
+    wallward_ref,
     a_buf,
     sems,
 ):
@@ -103,30 +105,36 @@
     levels = (lax.broadcasted_iota(jnp.int32, (rows, LANES), 0) + here_ref[0] % groups * rows).astype(jnp.float32)
     metric = jnp.concatenate([metric_of(levels, groups * rows)] * (nx // LANES), axis=1)
     level = lax.broadcasted_iota(jnp.int32, (rows, nx), 0)
-    for copy in fields:
-        copy.wait()
 
     def plane(y):
         if y < 0 or y == planes:
             return jnp.zeros((rows, nx), jnp.float32)
         return jnp.concatenate([t_ref[0, y], t_ref[1, y]], axis=0)
 
+    own = (1.0 - 3.0 * CONDUCTION_PART) - CONDUCTION_PART * metric
+    near, far = 0.5 * CONDUCTION_PART * metric, TRANSPORT_PART * metric
     for y in range(planes):
         t, ahead, behind = plane(y), plane(y + 1), plane(y - 1)
         east = pltpu.roll(t, nx - 1, 1)
         west = pltpu.roll(t, 1, 1)
         above = jnp.where(level == rows - 1, 0.0, pltpu.roll(t, rows - 1, 0))
         below = jnp.where(level == 0, 0.0, pltpu.roll(t, 1, 0))
+        side_ref[y] = (
+            own * t
+            + CONDUCTION_PART * (ahead + behind)
+            + 0.5 * CONDUCTION_PART * (east + west)
+            + near * (above + below)
+        )
+        along_ref[y] = 0.5 * TRANSPORT_PART * (east - west)
+        wallward_ref[y] = far * (above - below)
+    for copy in fields:
+        copy.wait()
+    for y in range(planes):
         u = u_ref[y].astype(jnp.float32)
         v = v_ref[y].astype(jnp.float32)
         w = w_ref[y].astype(jnp.float32)
-        carried = 0.5 * u * (east - west) + 0.5 * v * (ahead - behind) + w * metric * (above - below)
-        conducted = (
-            (ahead - 2.0 * t + behind)
-            + 0.5 * (east - 2.0 * t + west)
-            + 0.5 * metric * (above - 2.0 * t + below)
-        )
-        side_ref[y] = t - TRANSPORT_PART * carried + CONDUCTION_PART * conducted
+        across = 0.5 * TRANSPORT_PART * (plane(y + 1) - plane(y - 1))
+        side_ref[y] = side_ref[y] - (u * along_ref[y] + v * across + w * wallward_ref[y])
         cl_ref[y : y + 1, :] = (metric * (0.5 * CONDUCTION_PART + TRANSPORT_PART * w))[:1, :]
         ch_ref[y : y + 1, :] = (metric * (0.5 * CONDUCTION_PART - TRANSPORT_PART * w))[rows - 1 :, :]
         if y == 0:
@@ -152,8 +160,10 @@
         out_specs=[VMEM] * 7,
         out_shape=[jax.ShapeDtypeStruct(u.shape, t.dtype), plane, plane, level, level, a16, a16],
         scratch_shapes=[pltpu.VMEM(x.shape, x.dtype) for x in (u, v, w)]
-        + [pltpu.VMEM(half, a.dtype), pltpu.SemaphoreType.DMA((3 + parts,))],
-        compiler_params=pltpu.CompilerParams(vmem_limit_bytes=16 * 2**20),
+        + [pltpu.VMEM(u.shape, t.dtype)] * 2
+        + [pltpu.VMEM(half, a.dtype)]
+        + [pltpu.SemaphoreType.DMA((3 + parts,))],
+        compiler_params=pltpu.CompilerParams(vmem_limit_bytes=20 * 2**20),
         cost_estimate=pl.CostEstimate(
             flops=2 * a.size + 40 * t.size, bytes_accessed=4 * a.size + 14 * t.size, transcendentals=0
         ),
@@ -261,15 +271,19 @@
     both = jnp.concatenate([xh, xl], axis=1)
     width = units * lanes
 
-    def solve(c):
-        wh, wl = halves(w_ref[c])
+    def solve(c, cut):
+        wh, wl = halves(w_ref[c, cut])
         d = jnp.dot(wh, both, preferred_element_type=jnp.float32)
         e = jnp.dot(wl, xh, preferred_element_type=jnp.float32)
         return d[:, :width] + (d[:, width:] + e)
 
-    solved = jnp.where(insulated, solve(1), solve(0))
-    for i in range(units):
-        out_ref[:, i] = solved[:, i * lanes : (i + 1) * lanes].reshape(groups, rows, lanes)
+    step = 256
+    for k in range(0, extent, step):
+        cut = slice(k, k + step)
+        solved = jnp.where(insulated, solve(1, cut), solve(0, cut))
+        for i in range(units):
+            piece = solved[:, i * lanes : (i + 1) * lanes]
+            out_ref[k // rows : (k + step) // rows, i] = piece.reshape(step // rows, rows, lanes)
 
 
 def column_solve(here, segments, w, x, blocks):
@@ -305,6 +319,11 @@
     )(x)
 
 
+def fetched(x):
+    groups = lax.axis_size("pencil")
+    return lax.ppermute(x, "pencil", [(i, i) for i in range(groups)])
+
+
 def swapped(x):
     return lax.all_to_all(x, "pencil", split_axis=0, concat_axis=0, tiled=True)
 
@@ -313,6 +332,7 @@
     planes, rows, nx = t.shape
     slabs, groups = lax.axis_size("slab"), lax.axis_size("pencil")
     here = lax.axis_index(("slab", "pencil")).astype(jnp.int32).reshape(1)
+    w_z = fetched(wallward_solver_matrices)
     yc, yd, za, zb, t_halves = edges(here, t, groups)
     yc = lax.ppermute(yc, "slab", [(i, i ^ 1) for i in range(slabs)])
     yd = lax.ppermute(yd, "slab", [(i, ((i - 1) ^ 1) + 1 & slabs - 1) for i in range(slabs)])
@@ -321,7 +341,7 @@
     halos = yc, yd, za, zb
     *parts, ah, al = prepare(here, t_halves, u, v, w, downstream_solver_matrix, groups)
     x = swapped(row_solve(here, parts, halos, ah, al, downstream_solver_matrix, groups))
-    x = swapped(column_solve(here, wall_segments, wallward_solver_matrices, x, nx // LANES))
+    x = swapped(column_solve(here, wall_segments, w_z, x, nx // LANES))
     return place(x, t.shape)
 
 

time: 80.8 us -> 82.4 us (1.020)
  starting transfers between devices: 10.5 us -> 12.1 us
    ppermute x0 -> x1, starting transfers between devices: none -> 1.59 us  [fetched(): return lax.ppermute(x, 'pencil', [(i, i) for i in range(groups)])]
  transfers between devices with their start and end apart: 4 -> 5, of which waited for: 0 -> 0; matrix products, arithmetic and copies ran while one was open for 0% -> 0% of each run, Pallas kernels for 4% -> 8%
where the time goes in v10:
time: 82.4 us; the launch traced here: 82.2 us
  blocking collectives  60 us (73%)
  starting transfers between devices  12.1 us (15%)
  Pallas kernels  9.99 us (12%)
    all_to_all x2, blocking collectives, swapped(): return lax.all_to_all(x, 'pencil', split_axis=0, concat_axis=0, tiled=True)  60 us
    ppermute x1, starting transfers between devices, on_device(): lax.ppermute(za, 'pencil', [(i, (i - 1 ^ 1) + 1) for i in range(1, groups...  4.27 us
    ppermute x1, starting transfers between devices, on_device(): yc = lax.ppermute(yc, 'slab', [(i, i ^ 1) for i in range(slabs)])  3.83 us
    pallas_call x1, Pallas kernels, row_solve(): pl.pallas_call(row_kernel, in_specs=[SMEM] + [VMEM] * 11 + [HBM], out_spe...  3.68 us
    ppermute x1, starting transfers between devices, on_device(): lax.ppermute(yd, 'slab', [(i, (i - 1 ^ 1) + 1 & slabs - 1) for i in range...  2.29 us
    pallas_call x1, Pallas kernels, column_solve(): pl.pallas_call(functools.partial(column_kernel, blocks), in_specs=[SMEM,...  2.1 us
    pallas_call x1, Pallas kernels, prepare(): pl.pallas_call(functools.partial(prepare_kernel, groups), in_specs=[SMEM,...  2.1 us
  transfers between devices with their start and end apart: 5, of which 0 were waited for; matrix products, arithmetic and copies ran while one was open for 0% of the time, Pallas kernels for 8%

profile of v10, /device:TPU:1, one launch (start us, length us, event | category | flops | bytes accessed | tf_op | source)
XLA Modules:
  0.0 82.2 jit_solution(10720515710945927825)
XLA Ops:
  0.0 1.6 %collective-permute-start = (f32[2,512,512]{2,1,0:T(8,128)}, f32[2,512,512]{2,1,0:T(8,128)S(1)}, u32[]{:S(2)}, u32[]{:S(2)}) collective-permute-start(f32[2,512,512]{2,1,0:T(8,128)} %param.12), channel_id=1, source_target_pairs={{0,0},{1,1},{2,2},{3,3},{4,4},{5,5},{6,6},{7,7},{8,8},{9,9},{10,10... | collective-permute-start | bytes 6291464 | tf_op jit(solution)/shard_map/ppermute | solution.py:324
  1.6 1.2 %edges.1 = (f32[16,1024]{1,0:T(8,128)S(1)}, f32[16,1024]{1,0:T(8,128)S(1)}, f32[12,1024]{1,0:T(8,128)S(1)}, f32[12,1024]{1,0:T(8,128)S(1)}, f32[2,12,8,1024]{3,2,1,0:T(8,128)S(1)}) custom-call(s32[1]{0:T(128)} %bitcast.here_ref, f32[12,16,1024]{2,1,0:T(8,128)} %t_hbm.1), custom_call_target="tpu_custom_call" | custom-call | tf_op jit(solution)/shard_map/edges/pallas_call | solution.py:58
  2.8 3.8 %collective-permute-start.1 = (f32[16,1024]{1,0:T(8,128)S(1)}, f32[16,1024]{1,0:T(8,128)S(1)}, u32[]{:S(2)}, u32[]{:S(2)}) collective-permute-start(f32[16,1024]{1,0:T(8,128)S(1)} %get-tuple-element.23), channel_id=1, source_target_pairs={{0,32},{32,0},{64,96},{96,64},{128,160},{160,128},{192,224},{224,1... | collective-permute-start | bytes 196616 | tf_op jit(solution)/shard_map/ppermute | solution.py:337
  6.6 2.3 %collective-permute-start.2 = (f32[16,1024]{1,0:T(8,128)S(1)}, f32[16,1024]{1,0:T(8,128)S(1)}, u32[]{:S(2)}, u32[]{:S(2)}) collective-permute-start(f32[16,1024]{1,0:T(8,128)S(1)} %get-tuple-element.24), channel_id=1, source_target_pairs={{0,224},{32,64},{64,32},{96,128},{128,96},{160,192},{192,160},{224... | collective-permute-start | bytes 196616 | tf_op jit(solution)/shard_map/ppermute | solution.py:338
  8.9 4.3 %collective-permute-start.3 = (f32[12,1024]{1,0:T(8,128)S(1)}, f32[12,1024]{1,0:T(8,128)S(1)}, u32[]{:S(2)}, u32[]{:S(2)}) collective-permute-start(f32[12,1024]{1,0:T(8,128)S(1)} %get-tuple-element.25), channel_id=1, source_target_pairs={{1,2},{2,1},{3,4},{4,3},{5,6},{6,5},{7,8},{8,7},{9,10},{10,9},{11,... | collective-permute-start | bytes 147464 | tf_op jit(solution)/shard_map/ppermute | solution.py:339
  13.2 0.1 collective-permute-start.4
  13.3 2.1 %prepare.1 = (f32[12,16,1024]{2,1,0:T(8,128)S(1)}, f32[16,1024]{1,0:T(8,128)S(1)}, f32[16,1024]{1,0:T(8,128)S(1)}, f32[12,1024]{1,0:T(8,128)S(1)}, f32[12,1024]{...) custom-call(s32[1]{0:T(128)} %bitcast.here_ref, ...), custom_call_target="tpu_custom_call" | custom-call | flops 9961472 | bytes 6946816 | tf_op jit(solution)/shard_map/prepare/pallas_call | solution.py:157
  15.4 0.0 collective-permute-done.3.za_ref
  15.4 0.0 collective-permute-done.4.zb_ref
  15.4 0.0 collective-permute-done.1.yc_ref
  15.4 0.0 collective-permute-done.2.yd_ref
  15.4 0.0 copy-start
  15.4 3.7 %row_solve.1 = f32[32,3,16,128]{3,2,1,0:T(8,128)S(1)} custom-call(s32[1]{0:T(128)} %bitcast.here_ref, f32[12,16,1024]{2,1,0:T(8,128)S(1)} %get-tuple-element.18.side_ref, f32[16,1024]{1,0:T(8,128)S(1)} %get-tuple-element.19.cb_ref, f32[16,1024]{1,0:T(8,128)S(1)} %get-tuple-element.20.ca_ref, f32[12,1024]{1,0:T(8,128)S(1)} %get-tuple-element.21.cl_ref, ...), custom_call_target="tpu_custom_call" | custom-call | flops 1207959552 | bytes 8388608 | tf_op jit(solution)/shard_map/row_solve/pallas_call | solution.py:241
  19.1 33.4 %all_to_all.10.x_ref = f32[32,3,16,128]{3,2,1,0:T(8,128)S(1)} all-to-all(f32[32,3,16,128]{3,2,1,0:T(8,128)S(1)} %row_solve.1), channel_id=1, replica_groups=mesh['slab'=8,'pencil'=32] {'pencil'}, dimensions={0} | all-to-all | bytes 1572864 | tf_op jit(solution)/shard_map/all_to_all | solution.py:328
  52.5 0.0 collective-permute-done.w_ref
  52.5 0.0 copy-done
  52.5 2.1 %column_solve.1 = f32[32,3,16,128]{3,2,1,0:T(8,128)S(1)} custom-call(s32[1]{0:T(128)} %bitcast.here_ref, s32[16]{0:T(128)S(1)} %copy-done, f32[2,512,512]{2,1,0:T(8,128)S(1)} %collective-permute-done.w_ref, f32[32,3,16,128]{3,2,1,0:T(8,128)S(1)} %all_to_all.10.x_ref), custom_call_target="tpu_custom_call" | custom-call | flops 1207959552 | bytes 4194304 | tf_op jit(solution)/shard_map/column_solve/pallas_call | solution.py:290
  54.6 26.6 %all_to_all.11.x_ref = f32[32,3,16,128]{3,2,1,0:T(8,128)S(1)} all-to-all(f32[32,3,16,128]{3,2,1,0:T(8,128)S(1)} %column_solve.1), channel_id=1, replica_groups=mesh['slab'=8,'pencil'=32] {'pencil'}, dimensions={0} | all-to-all | bytes 1572864 | tf_op jit(solution)/shard_map/all_to_all | solution.py:328
  81.2 0.9 %place.1 = f32[12,16,1024]{2,1,0:T(8,128)} custom-call(f32[32,3,16,128]{3,2,1,0:T(8,128)S(1)} %all_to_all.11.x_ref), custom_call_target="tpu_custom_call" | custom-call | tf_op jit(solution)/shard_map/place/pallas_call | solution.py:312
Async XLA Ops:
  0.0 52.5 %collective-permute-start = (f32[2,512,512]{2,1,0:T(8,128)}, f32[2,512,512]{2,1,0:T(8,128)S(1)}, u32[]{:S(2)}, u32[]{:S(2)}) collective-permute-start(f32[2,512,512]{2,1,0:T(8,128)} %param.12), channel_id=1, source_target_pairs={{0,0},{1,1},{2,2},{3,3},{4,4},{5,5},{6,6},{7,7},{8,8},{9,9},{10,10... | collective-permute-start | bytes 6291464 | tf_op jit(solution)/shard_map/ppermute | solution.py:324
  2.8 12.6 %collective-permute-start.1 = (f32[16,1024]{1,0:T(8,128)S(1)}, f32[16,1024]{1,0:T(8,128)S(1)}, u32[]{:S(2)}, u32[]{:S(2)}) collective-permute-start(f32[16,1024]{1,0:T(8,128)S(1)} %get-tuple-element.23), channel_id=1, source_target_pairs={{0,32},{32,0},{64,96},{96,64},{128,160},{160,128},{192,224},{224,1... | collective-permute-start | bytes 196616 | tf_op jit(solution)/shard_map/ppermute | solution.py:337
  6.6 8.8 %collective-permute-start.2 = (f32[16,1024]{1,0:T(8,128)S(1)}, f32[16,1024]{1,0:T(8,128)S(1)}, u32[]{:S(2)}, u32[]{:S(2)}) collective-permute-start(f32[16,1024]{1,0:T(8,128)S(1)} %get-tuple-element.24), channel_id=1, source_target_pairs={{0,224},{32,64},{64,32},{96,128},{128,96},{160,192},{192,160},{224... | collective-permute-start | bytes 196616 | tf_op jit(solution)/shard_map/ppermute | solution.py:338
  8.9 6.5 %collective-permute-start.3 = (f32[12,1024]{1,0:T(8,128)S(1)}, f32[12,1024]{1,0:T(8,128)S(1)}, u32[]{:S(2)}, u32[]{:S(2)}) collective-permute-start(f32[12,1024]{1,0:T(8,128)S(1)} %get-tuple-element.25), channel_id=1, source_target_pairs={{1,2},{2,1},{3,4},{4,3},{5,6},{6,5},{7,8},{8,7},{9,10},{10,9},{11,... | collective-permute-start | bytes 147464 | tf_op jit(solution)/shard_map/ppermute | solution.py:339
  13.2 2.2 %collective-permute-start.4 = (f32[12,1024]{1,0:T(8,128)S(1)}, f32[12,1024]{1,0:T(8,128)S(1)}, u32[]{:S(2)}, u32[]{:S(2)}) collective-permute-start(f32[12,1024]{1,0:T(8,128)S(1)} %get-tuple-element.26), channel_id=1, source_target_pairs={{0,1},{1,0},{2,3},{3,2},{4,5},{5,4},{6,7},{7,6},{8,9},{9,8},{10,11... | collective-permute-start | bytes 147464 | tf_op jit(solution)/shard_map/ppermute | solution.py:340
  15.4 37.1 %copy-start = (s32[16]{0:T(128)S(1)}, s32[16]{0:T(128)}, u32[]{:S(2)}) copy-start(s32[16]{0:T(128)} %seg_ref.1) | copy-start | bytes 196

commit v11 on v9

--- a/solution.py
+++ b/solution.py
@@ -236,20 +236,20 @@
     insulated = jnp.concatenate([(crossed % 2)[:1, :]] * units, axis=1) == 1
     extent = groups * rows
     lines = jnp.concatenate([x_ref[:, i].reshape(extent, lanes) for i in range(units)], axis=1)
-    xh, xl = halves(lines)
-    both = jnp.concatenate([xh, xl], axis=1)
     width = units * lanes
-
-    def solve(c, cut):
-        wh, wl = halves(w_ref[c, cut])
-        d = jnp.dot(wh, both, preferred_element_type=jnp.float32)
-        e = jnp.dot(wl, xh, preferred_element_type=jnp.float32)
-        return d[:, :width] + (d[:, width:] + e)
-
+    both = jnp.concatenate(
+        [
+            jnp.concatenate(halves(jnp.where(insulated, 0.0, lines)), axis=1),
+            jnp.concatenate(halves(jnp.where(insulated, lines, 0.0)), axis=1),
+        ],
+        axis=0,
+    )
     step = 256
     for k in range(0, extent, step):
-        cut = slice(k, k + step)
-        solved = jnp.where(insulated, solve(1, cut), solve(0, cut))
+        wh, wl = halves(jnp.concatenate([w_ref[0, k : k + step], w_ref[1, k : k + step]], axis=1))
+        d = jnp.dot(wh, both, preferred_element_type=jnp.float32)
+        e = jnp.dot(wl, both[:, :width], preferred_element_type=jnp.float32)
+        solved = d[:, :width] + (d[:, width:] + e)
         for i in range(units):
             piece = solved[:, i * lanes : (i + 1) * lanes]
             out_ref[k // rows : (k + step) // rows, i] = piece.reshape(step // rows, rows, lanes)

time: 78.8 us -> 78.8 us (level)
  no operation moved by 1% of the time
where the time goes in v11:
time: 78.8 us; the launch traced here: 78.6 us
  blocking collectives  59 us (75%)
  starting transfers between devices  10.5 us (13%)
  Pallas kernels  8.99 us (11%)
    all_to_all x2, blocking collectives, swapped(): return lax.all_to_all(x, 'pencil', split_axis=0, concat_axis=0, tiled=True)  59 us
    ppermute x1, starting transfers between devices, on_device(): lax.ppermute(za, 'pencil', [(i, (i - 1 ^ 1) + 1) for i in range(1, groups...  4.27 us
    ppermute x1, starting transfers between devices, on_device(): yc = lax.ppermute(yc, 'slab', [(i, i ^ 1) for i in range(slabs)])  3.83 us
    pallas_call x1, Pallas kernels, prepare(): pl.pallas_call(functools.partial(prepare_kernel, groups), in_specs=[SMEM,...  3.03 us
    ppermute x1, starting transfers between devices, on_device(): lax.ppermute(yd, 'slab', [(i, (i - 1 ^ 1) + 1 & slabs - 1) for i in range...  2.29 us
    pallas_call x1, Pallas kernels, column_solve(): pl.pallas_call(functools.partial(column_kernel, blocks), in_specs=[SMEM,...  2.19 us
    pallas_call x1, Pallas kernels, row_solve(): pl.pallas_call(row_kernel, in_specs=[SMEM] + [VMEM] * 11, out_specs=VMEM,...  1.67 us
  transfers between devices with their start and end apart: 4, of which 0 were waited for; matrix products, arithmetic and copies ran while one was open for 0% of the time, Pallas kernels for 4%

profile of v11, /device:TPU:1, one launch (start us, length us, event | category | flops | bytes accessed | tf_op | source)
XLA Modules:
  0.0 78.6 jit_solution(8238598543566984585)
XLA Ops:
  0.0 1.2 %edges.1 = (f32[16,1024]{1,0:T(8,128)S(1)}, f32[16,1024]{1,0:T(8,128)S(1)}, f32[12,1024]{1,0:T(8,128)S(1)}, f32[12,1024]{1,0:T(8,128)S(1)}, f32[2,12,8,1024]{3,2,1,0:T(8,128)S(1)}) custom-call(s32[1]{0:T(128)} %bitcast.here_ref, f32[12,16,1024]{2,1,0:T(8,128)} %t_hbm.1), custom_call_target="tpu_custom_call" | custom-call | tf_op jit(solution)/shard_map/edges/pallas_call | solution.py:58
  1.2 3.8 %collective-permute-start = (f32[16,1024]{1,0:T(8,128)S(1)}, f32[16,1024]{1,0:T(8,128)S(1)}, u32[]{:S(2)}, u32[]{:S(2)}) collective-permute-start(f32[16,1024]{1,0:T(8,128)S(1)} %get-tuple-element.23), channel_id=1, source_target_pairs={{0,32},{32,0},{64,96},{96,64},{128,160},{160,128},{192,224},{224,1... | collective-permute-start | bytes 196616 | tf_op jit(solution)/shard_map/ppermute | solution.py:300
  5.0 2.3 %collective-permute-start.1 = (f32[16,1024]{1,0:T(8,128)S(1)}, f32[16,1024]{1,0:T(8,128)S(1)}, u32[]{:S(2)}, u32[]{:S(2)}) collective-permute-start(f32[16,1024]{1,0:T(8,128)S(1)} %get-tuple-element.24), channel_id=1, source_target_pairs={{0,224},{32,64},{64,32},{96,128},{128,96},{160,192},{192,160},{224... | collective-permute-start | bytes 196616 | tf_op jit(solution)/shard_map/ppermute | solution.py:301
  7.3 4.3 %collective-permute-start.2 = (f32[12,1024]{1,0:T(8,128)S(1)}, f32[12,1024]{1,0:T(8,128)S(1)}, u32[]{:S(2)}, u32[]{:S(2)}) collective-permute-start(f32[12,1024]{1,0:T(8,128)S(1)} %get-tuple-element.25), channel_id=1, source_target_pairs={{1,2},{2,1},{3,4},{4,3},{5,6},{6,5},{7,8},{8,7},{9,10},{10,9},{11,... | collective-permute-start | bytes 147464 | tf_op jit(solution)/shard_map/ppermute | solution.py:302
  11.6 0.1 collective-permute-start.3
  11.7 3.0 %prepare.1 = (f32[12,16,1024]{2,1,0:T(8,128)S(1)}, f32[16,1024]{1,0:T(8,128)S(1)}, f32[16,1024]{1,0:T(8,128)S(1)}, f32[12,1024]{1,0:T(8,128)S(1)}, f32[12,1024]{...) custom-call(s32[1]{0:T(128)} %bitcast.here_ref, ...), custom_call_target="tpu_custom_call" | custom-call | flops 12058624 | bytes 11141120 | tf_op jit(solution)/shard_map/prepare/pallas_call | solution.py:156
  14.7 0.0 collective-permute-done.2.za_ref
  14.7 0.0 collective-permute-done.3.zb_ref
  14.8 0.0 collective-permute-done.yc_ref
  14.8 0.0 collective-permute-done.1.yd_ref
  14.8 0.0 copy-start
  14.8 0.0 copy-start.1
  14.8 1.7 %row_solve.1 = f32[32,3,16,128]{3,2,1,0:T(8,128)S(1)} custom-call(s32[1]{0:T(128)} %bitcast.here_ref, f32[12,16,1024]{2,1,0:T(8,128)S(1)} %get-tuple-element.18.side_ref, f32[16,1024]{1,0:T(8,128)S(1)} %get-tuple-element.19.cb_ref, f32[16,1024]{1,0:T(8,128)S(1)} %get-tuple-element.20.ca_ref, f32[12,1024]{1,0:T(8,128)S(1)} %get-tuple-element.21.cl_ref, ...), custom_call_target="tpu_custom_call" | custom-call | flops 1207959552 | bytes 8388608 | tf_op jit(solution)/shard_map/row_solve/pallas_call | solution.py:214
  16.5 32.4 %all_to_all.10.x_ref = f32[32,3,16,128]{3,2,1,0:T(8,128)S(1)} all-to-all(f32[32,3,16,128]{3,2,1,0:T(8,128)S(1)} %row_solve.1), channel_id=1, replica_groups=mesh['slab'=8,'pencil'=32] {'pencil'}, dimensions={0} | all-to-all | bytes 1572864 | tf_op jit(solution)/shard_map/all_to_all | solution.py:292
  48.9 0.0 copy-done
  48.9 0.0 copy-done.1
  48.9 2.2 %column_solve.1 = f32[32,3,16,128]{3,2,1,0:T(8,128)S(1)} custom-call(s32[1]{0:T(128)} %bitcast.here_ref, s32[16]{0:T(128)S(1)} %copy-done.1, f32[2,512,512]{2,1,0:T(8,128)S(1)} %copy-done, f32[32,3,16,128]{3,2,1,0:T(8,128)S(1)} %all_to_all.10.x_ref), custom_call_target="tpu_custom_call" | custom-call | flops 1207959552 | bytes 4194304 | tf_op jit(solution)/shard_map/column_solve/pallas_call | solution.py:259
  51.1 26.6 %all_to_all.11.x_ref = f32[32,3,16,128]{3,2,1,0:T(8,128)S(1)} all-to-all(f32[32,3,16,128]{3,2,1,0:T(8,128)S(1)} %column_solve.1), channel_id=1, replica_groups=mesh['slab'=8,'pencil'=32] {'pencil'}, dimensions={0} | all-to-all | bytes 1572864 | tf_op jit(solution)/shard_map/all_to_all | solution.py:292
  77.7 0.9 %place.1 = f32[12,16,1024]{2,1,0:T(8,128)} custom-call(f32[32,3,16,128]{3,2,1,0:T(8,128)S(1)} %all_to_all.11.x_ref), custom_call_target="tpu_custom_call" | custom-call | tf_op jit(solution)/shard_map/place/pallas_call | solution.py:281
Async XLA Ops:
  1.2 13.6 %collective-permute-start = (f32[16,1024]{1,0:T(8,128)S(1)}, f32[16,1024]{1,0:T(8,128)S(1)}, u32[]{:S(2)}, u32[]{:S(2)}) collective-permute-start(f32[16,1024]{1,0:T(8,128)S(1)} %get-tuple-element.23), channel_id=1, source_target_pairs={{0,32},{32,0},{64,96},{96,64},{128,160},{160,128},{192,224},{224,1... | collective-permute-start | bytes 196616 | tf_op jit(solution)/shard_map/ppermute | solution.py:300
  5.0 9.7 %collective-permute-start.1 = (f32[16,1024]{1,0:T(8,128)S(1)}, f32[16,1024]{1,0:T(8,128)S(1)}, u32[]{:S(2)}, u32[]{:S(2)}) collective-permute-start(f32[16,1024]{1,0:T(8,128)S(1)} %get-tuple-element.24), channel_id=1, source_target_pairs={{0,224},{32,64},{64,32},{96,128},{128,96},{160,192},{192,160},{224... | collective-permute-start | bytes 196616 | tf_op jit(solution)/shard_map/ppermute | solution.py:301
  7.3 7.4 %collective-permute-start.2 = (f32[12,1024]{1,0:T(8,128)S(1)}, f32[12,1024]{1,0:T(8,128)S(1)}, u32[]{:S(2)}, u32[]{:S(2)}) collective-permute-start(f32[12,1024]{1,0:T(8,128)S(1)} %get-tuple-element.25), channel_id=1, source_target_pairs={{1,2},{2,1},{3,4},{4,3},{5,6},{6,5},{7,8},{8,7},{9,10},{10,9},{11,... | collective-permute-start | bytes 147464 | tf_op jit(solution)/shard_map/ppermute | solution.py:302
  11.6 3.2 %collective-permute-start.3 = (f32[12,1024]{1,0:T(8,128)S(1)}, f32[12,1024]{1,0:T(8,128)S(1)}, u32[]{:S(2)}, u32[]{:S(2)}) collective-permute-start(f32[12,1024]{1,0:T(8,128)S(1)} %get-tuple-element.26), channel_id=1, source_target_pairs={{0,1},{1,0},{2,3},{3,2},{4,5},{5,4},{6,7},{7,6},{8,9},{9,8},{10,11... | collective-permute-start | bytes 147464 | tf_op jit(solution)/shard_map/ppermute | solution.py:303
  14.8 34.1 %copy-start = (f32[2,512,512]{2,1,0:T(8,128)S(1)}, f32[2,512,512]{2,1,0:T(8,128)}, u32[]{:S(2)}) copy-start(f32[2,512,512]{2,1,0:T(8,128)} %w_ref.1) | copy-start | bytes 6291460
  14.8 34.1 %copy-start.1 = (s32[16]{0:T(128)S(1)}, s32[16]{0:T(128)}, u32[]{:S(2)}) copy-start(s32[16]{0:T(128)} %seg_ref.1) | copy-start | bytes 196

commit v12 on v9

--- a/solution.py
+++ b/solution.py
@@ -225,7 +225,7 @@
     )(here, *parts, *halos, ah, al)
 
 
-def column_kernel(blocks, here_ref, seg_ref, w_ref, x_ref, out_ref):
+def column_kernel(blocks, here_ref, seg_ref, w_ref, x_ref, out_ref, high, low, both):
     groups, units, rows, lanes = x_ref.shape
     column = lax.broadcasted_iota(jnp.int32, (8, lanes), 1) + here_ref[0] % blocks * lanes
     crossed = jnp.zeros((8, lanes), jnp.int32)
@@ -235,18 +235,23 @@
         crossed = crossed + jnp.where(column >= end, 1, 0)
     insulated = jnp.concatenate([(crossed % 2)[:1, :]] * units, axis=1) == 1
     extent = groups * rows
-    lines = jnp.concatenate([x_ref[:, i].reshape(extent, lanes) for i in range(units)], axis=1)
-    xh, xl = halves(lines)
-    both = jnp.concatenate([xh, xl], axis=1)
     width = units * lanes
+    for i in range(units):
+        at = i * lanes
+        both[:, at : at + lanes], both[:, width + at : width + at + lanes] = halves(
+            x_ref[:, i].reshape(extent, lanes)
+        )
+    step = 128
+    for k in range(0, extent, step):
+        cut = slice(k, k + step)
+        for c in range(2):
+            high[c, cut], low[c, cut] = halves(w_ref[c, cut])
 
     def solve(c, cut):
-        wh, wl = halves(w_ref[c, cut])
-        d = jnp.dot(wh, both, preferred_element_type=jnp.float32)
-        e = jnp.dot(wl, xh, preferred_element_type=jnp.float32)
+        d = jnp.dot(high[c, cut], both[...], preferred_element_type=jnp.float32)
+        e = jnp.dot(low[c, cut], both[:, :width], preferred_element_type=jnp.float32)
         return d[:, :width] + (d[:, width:] + e)
 
-    step = 256
     for k in range(0, extent, step):
         cut = slice(k, k + step)
         solved = jnp.where(insulated, solve(1, cut), solve(0, cut))
@@ -261,6 +266,8 @@
         in_specs=[SMEM, SMEM, VMEM, VMEM],
         out_specs=VMEM,
         out_shape=jax.ShapeDtypeStruct(x.shape, jnp.float32),
+        scratch_shapes=[pltpu.VMEM(w.shape, jnp.bfloat16)] * 2
+        + [pltpu.VMEM((w.shape[1], 2 * x.shape[1] * LANES), jnp.bfloat16)],
         compiler_params=pltpu.CompilerParams(vmem_limit_bytes=32 * 2**20),
         cost_estimate=pl.CostEstimate(
             flops=12 * w.shape[1] * x.size, bytes_accessed=4 * 2**20, transcendentals=0

time: 78.8 us -> 78.9 us (level)
  no operation moved by 1% of the time
where the time goes in v12:
time: 78.9 us; the launch traced here: 78.7 us
  blocking collectives  59 us (75%)
  starting transfers between devices  10.5 us (13%)
  Pallas kernels  9.06 us (11%)
    all_to_all x2, blocking collectives, swapped(): return lax.all_to_all(x, 'pencil', split_axis=0, concat_axis=0, tiled=True)  59 us
    ppermute x1, starting transfers between devices, on_device(): lax.ppermute(za, 'pencil', [(i, (i - 1 ^ 1) + 1) for i in range(1, groups...  4.27 us
    ppermute x1, starting transfers between devices, on_device(): yc = lax.ppermute(yc, 'slab', [(i, i ^ 1) for i in range(slabs)])  3.83 us
    pallas_call x1, Pallas kernels, prepare(): pl.pallas_call(functools.partial(prepare_kernel, groups), in_specs=[SMEM,...  3.03 us
    ppermute x1, starting transfers between devices, on_device(): lax.ppermute(yd, 'slab', [(i, (i - 1 ^ 1) + 1 & slabs - 1) for i in range...  2.29 us
    pallas_call x1, Pallas kernels, column_solve(): pl.pallas_call(functools.partial(column_kernel, blocks), in_specs=[SMEM,...  2.25 us
    pallas_call x1, Pallas kernels, row_solve(): pl.pallas_call(row_kernel, in_specs=[SMEM] + [VMEM] * 11, out_specs=VMEM,...  1.67 us
  transfers between devices with their start and end apart: 4, of which 0 were waited for; matrix products, arithmetic and copies ran while one was open for 0% of the time, Pallas kernels for 4%

profile of v12, /device:TPU:1, one launch (start us, length us, event | category | flops | bytes accessed | tf_op | source)
XLA Modules:
  0.0 78.7 jit_solution(17001321636881608352)
XLA Ops:
  0.0 1.2 %edges.1 = (f32[16,1024]{1,0:T(8,128)S(1)}, f32[16,1024]{1,0:T(8,128)S(1)}, f32[12,1024]{1,0:T(8,128)S(1)}, f32[12,1024]{1,0:T(8,128)S(1)}, f32[2,12,8,1024]{3,2,1,0:T(8,128)S(1)}) custom-call(s32[1]{0:T(128)} %bitcast.here_ref, f32[12,16,1024]{2,1,0:T(8,128)} %t_hbm.1), custom_call_target="tpu_custom_call" | custom-call | tf_op jit(solution)/shard_map/edges/pallas_call | solution.py:58
  1.2 3.8 %collective-permute-start = (f32[16,1024]{1,0:T(8,128)S(1)}, f32[16,1024]{1,0:T(8,128)S(1)}, u32[]{:S(2)}, u32[]{:S(2)}) collective-permute-start(f32[16,1024]{1,0:T(8,128)S(1)} %get-tuple-element.23), channel_id=1, source_target_pairs={{0,32},{32,0},{64,96},{96,64},{128,160},{160,128},{192,224},{224,1... | collective-permute-start | bytes 196616 | tf_op jit(solution)/shard_map/ppermute | solution.py:307
  5.0 2.3 %collective-permute-start.1 = (f32[16,1024]{1,0:T(8,128)S(1)}, f32[16,1024]{1,0:T(8,128)S(1)}, u32[]{:S(2)}, u32[]{:S(2)}) collective-permute-start(f32[16,1024]{1,0:T(8,128)S(1)} %get-tuple-element.24), channel_id=1, source_target_pairs={{0,224},{32,64},{64,32},{96,128},{128,96},{160,192},{192,160},{224... | collective-permute-start | bytes 196616 | tf_op jit(solution)/shard_map/ppermute | solution.py:308
  7.3 4.3 %collective-permute-start.2 = (f32[12,1024]{1,0:T(8,128)S(1)}, f32[12,1024]{1,0:T(8,128)S(1)}, u32[]{:S(2)}, u32[]{:S(2)}) collective-permute-start(f32[12,1024]{1,0:T(8,128)S(1)} %get-tuple-element.25), channel_id=1, source_target_pairs={{1,2},{2,1},{3,4},{4,3},{5,6},{6,5},{7,8},{8,7},{9,10},{10,9},{11,... | collective-permute-start | bytes 147464 | tf_op jit(solution)/shard_map/ppermute | solution.py:309
  11.6 0.1 collective-permute-start.3
  11.7 3.0 %prepare.1 = (f32[12,16,1024]{2,1,0:T(8,128)S(1)}, f32[16,1024]{1,0:T(8,128)S(1)}, f32[16,1024]{1,0:T(8,128)S(1)}, f32[12,1024]{1,0:T(8,128)S(1)}, f32[12,1024]{...) custom-call(s32[1]{0:T(128)} %bitcast.here_ref, ...), custom_call_target="tpu_custom_call" | custom-call | flops 12058624 | bytes 11141120 | tf_op jit(solution)/shard_map/prepare/pallas_call | solution.py:156
  14.7 0.0 collective-permute-done.2.za_ref
  14.7 0.0 collective-permute-done.3.zb_ref
  14.8 0.0 collective-permute-done.yc_ref
  14.8 0.0 collective-permute-done.1.yd_ref
  14.8 0.0 copy-start
  14.8 0.0 copy-start.1
  14.8 1.7 %row_solve.1 = f32[32,3,16,128]{3,2,1,0:T(8,128)S(1)} custom-call(s32[1]{0:T(128)} %bitcast.here_ref, f32[12,16,1024]{2,1,0:T(8,128)S(1)} %get-tuple-element.18.side_ref, f32[16,1024]{1,0:T(8,128)S(1)} %get-tuple-element.19.cb_ref, f32[16,1024]{1,0:T(8,128)S(1)} %get-tuple-element.20.ca_ref, f32[12,1024]{1,0:T(8,128)S(1)} %get-tuple-element.21.cl_ref, ...), custom_call_target="tpu_custom_call" | custom-call | flops 1207959552 | bytes 8388608 | tf_op jit(solution)/shard_map/row_solve/pallas_call | solution.py:214
  16.5 32.4 %all_to_all.10.x_ref = f32[32,3,16,128]{3,2,1,0:T(8,128)S(1)} all-to-all(f32[32,3,16,128]{3,2,1,0:T(8,128)S(1)} %row_solve.1), channel_id=1, replica_groups=mesh['slab'=8,'pencil'=32] {'pencil'}, dimensions={0} | all-to-all | bytes 1572864 | tf_op jit(solution)/shard_map/all_to_all | solution.py:299
  48.9 0.0 copy-done
  48.9 0.0 copy-done.1
  48.9 2.3 %column_solve.1 = f32[32,3,16,128]{3,2,1,0:T(8,128)S(1)} custom-call(s32[1]{0:T(128)} %bitcast.here_ref, s32[16]{0:T(128)S(1)} %copy-done.1, f32[2,512,512]{2,1,0:T(8,128)S(1)} %copy-done, f32[32,3,16,128]{3,2,1,0:T(8,128)S(1)} %all_to_all.10.x_ref), custom_call_target="tpu_custom_call" | custom-call | flops 1207959552 | bytes 4194304 | tf_op jit(solution)/shard_map/column_solve/pallas_call | solution.py:264
  51.2 26.6 %all_to_all.11.x_ref = f32[32,3,16,128]{3,2,1,0:T(8,128)S(1)} all-to-all(f32[32,3,16,128]{3,2,1,0:T(8,128)S(1)} %column_solve.1), channel_id=1, replica_groups=mesh['slab'=8,'pencil'=32] {'pencil'}, dimensions={0} | all-to-all | bytes 1572864 | tf_op jit(solution)/shard_map/all_to_all | solution.py:299
  77.8 0.9 %place.1 = f32[12,16,1024]{2,1,0:T(8,128)} custom-call(f32[32,3,16,128]{3,2,1,0:T(8,128)S(1)} %all_to_all.11.x_ref), custom_call_target="tpu_custom_call" | custom-call | tf_op jit(solution)/shard_map/place/pallas_call | solution.py:288
Async XLA Ops:
  1.2 13.6 %collective-permute-start = (f32[16,1024]{1,0:T(8,128)S(1)}, f32[16,1024]{1,0:T(8,128)S(1)}, u32[]{:S(2)}, u32[]{:S(2)}) collective-permute-start(f32[16,1024]{1,0:T(8,128)S(1)} %get-tuple-element.23), channel_id=1, source_target_pairs={{0,32},{32,0},{64,96},{96,64},{128,160},{160,128},{192,224},{224,1... | collective-permute-start | bytes 196616 | tf_op jit(solution)/shard_map/ppermute | solution.py:307
  5.0 9.7 %collective-permute-start.1 = (f32[16,1024]{1,0:T(8,128)S(1)}, f32[16,1024]{1,0:T(8,128)S(1)}, u32[]{:S(2)}, u32[]{:S(2)}) collective-permute-start(f32[16,1024]{1,0:T(8,128)S(1)} %get-tuple-element.24), channel_id=1, source_target_pairs={{0,224},{32,64},{64,32},{96,128},{128,96},{160,192},{192,160},{224... | collective-permute-start | bytes 196616 | tf_op jit(solution)/shard_map/ppermute | solution.py:308
  7.3 7.4 %collective-permute-start.2 = (f32[12,1024]{1,0:T(8,128)S(1)}, f32[12,1024]{1,0:T(8,128)S(1)}, u32[]{:S(2)}, u32[]{:S(2)}) collective-permute-start(f32[12,1024]{1,0:T(8,128)S(1)} %get-tuple-element.25), channel_id=1, source_target_pairs={{1,2},{2,1},{3,4},{4,3},{5,6},{6,5},{7,8},{8,7},{9,10},{10,9},{11,... | collective-permute-start | bytes 147464 | tf_op jit(solution)/shard_map/ppermute | solution.py:309
  11.6 3.2 %collective-permute-start.3 = (f32[12,1024]{1,0:T(8,128)S(1)}, f32[12,1024]{1,0:T(8,128)S(1)}, u32[]{:S(2)}, u32[]{:S(2)}) collective-permute-start(f32[12,1024]{1,0:T(8,128)S(1)} %get-tuple-element.26), channel_id=1, source_target_pairs={{0,1},{1,0},{2,3},{3,2},{4,5},{5,4},{6,7},{7,6},{8,9},{9,8},{10,11... | collective-permute-start | bytes 147464 | tf_op jit(solution)/shard_map/ppermute | solution.py:310
  14.8 34.1 %copy-start = (f32[2,512,512]{2,1,0:T(8,128)S(1)}, f32[2,512,512]{2,1,0:T(8,128)}, u32[]{:S(2)}) copy-start(f32[2,512,512]{2,1,0:T(8,128)} %w_ref.1) | copy-start | bytes 6291460
  14.8 34.1 %copy-start.1 = (s32[16]{0:T(128)S(1)}, s32[16]{0:T(128)}, u32[]{:S(2)}) copy-start(s32[16]{0:T(128)} %seg_ref.1) | copy-start | bytes 196

commit v13 on v9

--- a/solution.py
+++ b/solution.py
@@ -31,23 +31,28 @@
 def edge_kernel(groups, here_ref, t_hbm, yc_ref, yd_ref, za_ref, zb_ref, buf, sems):
     planes, rows, _ = t_hbm.shape
     half = buf.shape[2]
+    cuts = (sems.shape[0] - 2) // 2
+    some = planes // cuts
     pencil_even, slab_even = here_ref[0] % 2 == 0, here_ref[0] // groups % 2 == 0
-    copies = [
-        pltpu.make_async_copy(t_hbm.at[:, pl.ds(0, half)], buf.at[0], sems.at[0]),
-        pltpu.make_async_copy(t_hbm.at[:, pl.ds(rows - half, half)], buf.at[1], sems.at[1]),
-        pltpu.make_async_copy(t_hbm.at[jnp.where(slab_even, planes - 1, 0)], yc_ref, sems.at[2]),
-        pltpu.make_async_copy(t_hbm.at[jnp.where(slab_even, 0, planes - 1)], yd_ref, sems.at[3]),
+    ends = [
+        pltpu.make_async_copy(t_hbm.at[jnp.where(slab_even, planes - 1, 0)], yc_ref, sems.at[0]),
+        pltpu.make_async_copy(t_hbm.at[jnp.where(slab_even, 0, planes - 1)], yd_ref, sems.at[1]),
     ]
+    copies = []
+    for i in range(cuts):
+        for h in range(2):
+            source = t_hbm.at[pl.ds(i * some, some), pl.ds(h * half, half)]
+            copies.append(pltpu.make_async_copy(source, buf.at[h, pl.ds(i * some, some)], sems.at[2 + 2 * i + h]))
+    for copy in copies + ends:
+        copy.start()
     for copy in copies:
-        copy.start()
-    copies[0].wait()
-    copies[1].wait()
+        copy.wait()
     for y in range(planes):
         low, high = buf[0, y, :1, :], buf[1, y, half - 1 :, :]
         za_ref[y : y + 1, :] = jnp.where(pencil_even, low, high)
         zb_ref[y : y + 1, :] = jnp.where(pencil_even, high, low)
-    copies[2].wait()
-    copies[3].wait()
+    for copy in ends:
+        copy.wait()
 
 
 def edges(here, t, groups):
@@ -60,7 +65,7 @@
         in_specs=[SMEM, HBM],
         out_specs=[VMEM] * 5,
         out_shape=[plane, plane, level, level, jax.ShapeDtypeStruct((2, planes, half, nx), t.dtype)],
-        scratch_shapes=[pltpu.SemaphoreType.DMA((4,))],
+        scratch_shapes=[pltpu.SemaphoreType.DMA((10,))],
         compiler_params=pltpu.CompilerParams(vmem_limit_bytes=8 * 2**20),
         name="edges",
     )(here, pinned(t))
@@ -152,7 +157,7 @@
     a16 = jax.ShapeDtypeStruct(a.shape, jnp.bfloat16)
     plane = jax.ShapeDtypeStruct((rows, nx), t.dtype)
     level = jax.ShapeDtypeStruct((planes, nx), t.dtype)
-    parts = 4
+    parts = 8
     return pl.pallas_call(
         functools.partial(prepare_kernel, groups),
         in_specs=[SMEM, VMEM] + [HBM] * 4,

time: 78.8 us -> 79 us (level)
  no operation moved by 1% of the time
where the time goes in v13:
time: 79 us; the launch traced here: 78.8 us
  blocking collectives  59 us (75%)
  starting transfers between devices  10.5 us (13%)
  Pallas kernels  9.17 us (12%)
    all_to_all x2, blocking collectives, swapped(): return lax.all_to_all(x, 'pencil', split_axis=0, concat_axis=0, tiled=True)  59 us
    ppermute x1, starting transfers between devices, on_device(): lax.ppermute(za, 'pencil', [(i, (i - 1 ^ 1) + 1) for i in range(1, groups...  4.27 us
    ppermute x1, starting transfers between devices, on_device(): yc = lax.ppermute(yc, 'slab', [(i, i ^ 1) for i in range(slabs)])  3.83 us
    pallas_call x1, Pallas kernels, prepare(): pl.pallas_call(functools.partial(prepare_kernel, groups), in_specs=[SMEM,...  3.08 us
    ppermute x1, starting transfers between devices, on_device(): lax.ppermute(yd, 'slab', [(i, (i - 1 ^ 1) + 1 & slabs - 1) for i in range...  2.29 us
    pallas_call x1, Pallas kernels, column_solve(): pl.pallas_call(functools.partial(column_kernel, blocks), in_specs=[SMEM,...  2.17 us
    pallas_call x1, Pallas kernels, row_solve(): pl.pallas_call(row_kernel, in_specs=[SMEM] + [VMEM] * 11, out_specs=VMEM,...  1.66 us
  transfers between devices with their start and end apart: 4, of which 0 were waited for; matrix products, arithmetic and copies ran while one was open for 0% of the time, Pallas kernels for 4%

profile of v13, /device:TPU:1, one launch (start us, length us, event | category | flops | bytes accessed | tf_op | source)
XLA Modules:
  0.0 78.8 jit_solution(1753816354595030529)
XLA Ops:
  0.0 1.3 %edges.1 = (f32[16,1024]{1,0:T(8,128)S(1)}, f32[16,1024]{1,0:T(8,128)S(1)}, f32[12,1024]{1,0:T(8,128)S(1)}, f32[12,1024]{1,0:T(8,128)S(1)}, f32[2,12,8,1024]{3,2,1,0:T(8,128)S(1)}) custom-call(s32[1]{0:T(128)} %bitcast.here_ref, f32[12,16,1024]{2,1,0:T(8,128)} %t_hbm.1), custom_call_target="tpu_custom_call" | custom-call | tf_op jit(solution)/shard_map/edges/pallas_call | solution.py:63
  1.3 3.8 %collective-permute-start = (f32[16,1024]{1,0:T(8,128)S(1)}, f32[16,1024]{1,0:T(8,128)S(1)}, u32[]{:S(2)}, u32[]{:S(2)}) collective-permute-start(f32[16,1024]{1,0:T(8,128)S(1)} %get-tuple-element.23), channel_id=1, source_target_pairs={{0,32},{32,0},{64,96},{96,64},{128,160},{160,128},{192,224},{224,1... | collective-permute-start | bytes 196616 | tf_op jit(solution)/shard_map/ppermute | solution.py:305
  5.2 2.3 %collective-permute-start.1 = (f32[16,1024]{1,0:T(8,128)S(1)}, f32[16,1024]{1,0:T(8,128)S(1)}, u32[]{:S(2)}, u32[]{:S(2)}) collective-permute-start(f32[16,1024]{1,0:T(8,128)S(1)} %get-tuple-element.24), channel_id=1, source_target_pairs={{0,224},{32,64},{64,32},{96,128},{128,96},{160,192},{192,160},{224... | collective-permute-start | bytes 196616 | tf_op jit(solution)/shard_map/ppermute | solution.py:306
  7.5 4.3 %collective-permute-start.2 = (f32[12,1024]{1,0:T(8,128)S(1)}, f32[12,1024]{1,0:T(8,128)S(1)}, u32[]{:S(2)}, u32[]{:S(2)}) collective-permute-start(f32[12,1024]{1,0:T(8,128)S(1)} %get-tuple-element.25), channel_id=1, source_target_pairs={{1,2},{2,1},{3,4},{4,3},{5,6},{6,5},{7,8},{8,7},{9,10},{10,9},{11,... | collective-permute-start | bytes 147464 | tf_op jit(solution)/shard_map/ppermute | solution.py:307
  11.7 0.1 collective-permute-start.3
  11.8 3.1 %prepare.1 = (f32[12,16,1024]{2,1,0:T(8,128)S(1)}, f32[16,1024]{1,0:T(8,128)S(1)}, f32[16,1024]{1,0:T(8,128)S(1)}, f32[12,1024]{1,0:T(8,128)S(1)}, f32[12,1024]{...) custom-call(s32[1]{0:T(128)} %bitcast.here_ref, ...), custom_call_target="tpu_custom_call" | custom-call | flops 12058624 | bytes 11141120 | tf_op jit(solution)/shard_map/prepare/pallas_call | solution.py:161
  14.9 0.0 collective-permute-done.2.za_ref
  14.9 0.0 collective-permute-done.3.zb_ref
  14.9 0.0 collective-permute-done.yc_ref
  15.0 0.0 collective-permute-done.1.yd_ref
  15.0 0.0 copy-start
  15.0 0.0 copy-start.1
  15.0 1.7 %row_solve.1 = f32[32,3,16,128]{3,2,1,0:T(8,128)S(1)} custom-call(s32[1]{0:T(128)} %bitcast.here_ref, f32[12,16,1024]{2,1,0:T(8,128)S(1)} %get-tuple-element.18.side_ref, f32[16,1024]{1,0:T(8,128)S(1)} %get-tuple-element.19.cb_ref, f32[16,1024]{1,0:T(8,128)S(1)} %get-tuple-element.20.ca_ref, f32[12,1024]{1,0:T(8,128)S(1)} %get-tuple-element.21.cl_ref, ...), custom_call_target="tpu_custom_call" | custom-call | flops 1207959552 | bytes 8388608 | tf_op jit(solution)/shard_map/row_solve/pallas_call | solution.py:219
  16.7 32.4 %all_to_all.10.x_ref = f32[32,3,16,128]{3,2,1,0:T(8,128)S(1)} all-to-all(f32[32,3,16,128]{3,2,1,0:T(8,128)S(1)} %row_solve.1), channel_id=1, replica_groups=mesh['slab'=8,'pencil'=32] {'pencil'}, dimensions={0} | all-to-all | bytes 1572864 | tf_op jit(solution)/shard_map/all_to_all | solution.py:297
  49.1 0.0 copy-done
  49.1 0.0 copy-done.1
  49.1 2.2 %column_solve.1 = f32[32,3,16,128]{3,2,1,0:T(8,128)S(1)} custom-call(s32[1]{0:T(128)} %bitcast.here_ref, s32[16]{0:T(128)S(1)} %copy-done.1, f32[2,512,512]{2,1,0:T(8,128)S(1)} %copy-done, f32[32,3,16,128]{3,2,1,0:T(8,128)S(1)} %all_to_all.10.x_ref), custom_call_target="tpu_custom_call" | custom-call | flops 1207959552 | bytes 4194304 | tf_op jit(solution)/shard_map/column_solve/pallas_call | solution.py:264
  51.2 26.6 %all_to_all.11.x_ref = f32[32,3,16,128]{3,2,1,0:T(8,128)S(1)} all-to-all(f32[32,3,16,128]{3,2,1,0:T(8,128)S(1)} %column_solve.1), channel_id=1, replica_groups=mesh['slab'=8,'pencil'=32] {'pencil'}, dimensions={0} | all-to-all | bytes 1572864 | tf_op jit(solution)/shard_map/all_to_all | solution.py:297
  77.8 0.9 %place.1 = f32[12,16,1024]{2,1,0:T(8,128)} custom-call(f32[32,3,16,128]{3,2,1,0:T(8,128)S(1)} %all_to_all.11.x_ref), custom_call_target="tpu_custom_call" | custom-call | tf_op jit(solution)/shard_map/place/pallas_call | solution.py:286
Async XLA Ops:
  1.3 13.6 %collective-permute-start = (f32[16,1024]{1,0:T(8,128)S(1)}, f32[16,1024]{1,0:T(8,128)S(1)}, u32[]{:S(2)}, u32[]{:S(2)}) collective-permute-start(f32[16,1024]{1,0:T(8,128)S(1)} %get-tuple-element.23), channel_id=1, source_target_pairs={{0,32},{32,0},{64,96},{96,64},{128,160},{160,128},{192,224},{224,1... | collective-permute-start | bytes 196616 | tf_op jit(solution)/shard_map/ppermute | solution.py:305
  5.2 9.8 %collective-permute-start.1 = (f32[16,1024]{1,0:T(8,128)S(1)}, f32[16,1024]{1,0:T(8,128)S(1)}, u32[]{:S(2)}, u32[]{:S(2)}) collective-permute-start(f32[16,1024]{1,0:T(8,128)S(1)} %get-tuple-element.24), channel_id=1, source_target_pairs={{0,224},{32,64},{64,32},{96,128},{128,96},{160,192},{192,160},{224... | collective-permute-start | bytes 196616 | tf_op jit(solution)/shard_map/ppermute | solution.py:306
  7.5 7.5 %collective-permute-start.2 = (f32[12,1024]{1,0:T(8,128)S(1)}, f32[12,1024]{1,0:T(8,128)S(1)}, u32[]{:S(2)}, u32[]{:S(2)}) collective-permute-start(f32[12,1024]{1,0:T(8,128)S(1)} %get-tuple-element.25), channel_id=1, source_target_pairs={{1,2},{2,1},{3,4},{4,3},{5,6},{6,5},{7,8},{8,7},{9,10},{10,9},{11,... | collective-permute-start | bytes 147464 | tf_op jit(solution)/shard_map/ppermute | solution.py:307
  11.7 3.2 %collective-permute-start.3 = (f32[12,1024]{1,0:T(8,128)S(1)}, f32[12,1024]{1,0:T(8,128)S(1)}, u32[]{:S(2)}, u32[]{:S(2)}) collective-permute-start(f32[12,1024]{1,0:T(8,128)S(1)} %get-tuple-element.26), channel_id=1, source_target_pairs={{0,1},{1,0},{2,3},{3,2},{4,5},{5,4},{6,7},{7,6},{8,9},{9,8},{10,11... | collective-permute-start | bytes 147464 | tf_op jit(solution)/shard_map/ppermute | solution.py:308
  15.0 34.1 %copy-start = (f32[2,512,512]{2,1,0:T(8,128)S(1)}, f32[2,512,512]{2,1,0:T(8,128)}, u32[]{:S(2)}) copy-start(f32[2,512,512]{2,1,0:T(8,128)} %w_ref.1) | copy-start | bytes 6291460
  15.0 34.1 %copy-start.1 = (s32[16]{0:T(128)S(1)}, s32[16]{0:T(128)}, u32[]{:S(2)}) copy-start(s32[16]{0:T(128)} %seg_ref.1) | copy-start | bytes 196

commit v14 on v9

--- a/solution.py
+++ b/solution.py
@@ -30,37 +30,33 @@
 
 def edge_kernel(groups, here_ref, t_hbm, yc_ref, yd_ref, za_ref, zb_ref, buf, sems):
     planes, rows, _ = t_hbm.shape
-    half = buf.shape[2]
     pencil_even, slab_even = here_ref[0] % 2 == 0, here_ref[0] // groups % 2 == 0
     copies = [
-        pltpu.make_async_copy(t_hbm.at[:, pl.ds(0, half)], buf.at[0], sems.at[0]),
-        pltpu.make_async_copy(t_hbm.at[:, pl.ds(rows - half, half)], buf.at[1], sems.at[1]),
-        pltpu.make_async_copy(t_hbm.at[jnp.where(slab_even, planes - 1, 0)], yc_ref, sems.at[2]),
-        pltpu.make_async_copy(t_hbm.at[jnp.where(slab_even, 0, planes - 1)], yd_ref, sems.at[3]),
+        pltpu.make_async_copy(t_hbm, buf, sems.at[0]),
+        pltpu.make_async_copy(t_hbm.at[jnp.where(slab_even, planes - 1, 0)], yc_ref, sems.at[1]),
+        pltpu.make_async_copy(t_hbm.at[jnp.where(slab_even, 0, planes - 1)], yd_ref, sems.at[2]),
     ]
     for copy in copies:
         copy.start()
     copies[0].wait()
-    copies[1].wait()
     for y in range(planes):
-        low, high = buf[0, y, :1, :], buf[1, y, half - 1 :, :]
+        low, high = buf[y, :1, :], buf[y, rows - 1 :, :]
         za_ref[y : y + 1, :] = jnp.where(pencil_even, low, high)
         zb_ref[y : y + 1, :] = jnp.where(pencil_even, high, low)
+    copies[1].wait()
     copies[2].wait()
-    copies[3].wait()
 
 
 def edges(here, t, groups):
     planes, rows, nx = t.shape
-    half = rows // 2
     plane = jax.ShapeDtypeStruct((rows, nx), t.dtype)
     level = jax.ShapeDtypeStruct((planes, nx), t.dtype)
     return pl.pallas_call(
         functools.partial(edge_kernel, groups),
         in_specs=[SMEM, HBM],
         out_specs=[VMEM] * 5,
-        out_shape=[plane, plane, level, level, jax.ShapeDtypeStruct((2, planes, half, nx), t.dtype)],
-        scratch_shapes=[pltpu.SemaphoreType.DMA((4,))],
+        out_shape=[plane, plane, level, level, jax.ShapeDtypeStruct(t.shape, t.dtype)],
+        scratch_shapes=[pltpu.SemaphoreType.DMA((3,))],
         compiler_params=pltpu.CompilerParams(vmem_limit_bytes=8 * 2**20),
         name="edges",
     )(here, pinned(t))
@@ -109,7 +105,7 @@
     def plane(y):
         if y < 0 or y == planes:
             return jnp.zeros((rows, nx), jnp.float32)
-        return jnp.concatenate([t_ref[0, y], t_ref[1, y]], axis=0)
+        return t_ref[y]
 
     own = (1.0 - 3.0 * CONDUCTION_PART) - CONDUCTION_PART * metric
     near, far = 0.5 * CONDUCTION_PART * metric, TRANSPORT_PART * metric
@@ -296,13 +292,13 @@
     planes, rows, nx = t.shape
     slabs, groups = lax.axis_size("slab"), lax.axis_size("pencil")
     here = lax.axis_index(("slab", "pencil")).astype(jnp.int32).reshape(1)
-    yc, yd, za, zb, t_halves = edges(here, t, groups)
+    yc, yd, za, zb, t_here = edges(here, t, groups)
     yc = lax.ppermute(yc, "slab", [(i, i ^ 1) for i in range(slabs)])
     yd = lax.ppermute(yd, "slab", [(i, ((i - 1) ^ 1) + 1 & slabs - 1) for i in range(slabs)])
     za = lax.ppermute(za, "pencil", [(i, ((i - 1) ^ 1) + 1) for i in range(1, groups - 1)])
     zb = lax.ppermute(zb, "pencil", [(i, i ^ 1) for i in range(groups)])
     halos = yc, yd, za, zb
-    *parts, ah, al = prepare(here, t_halves, u, v, w, downstream_solver_matrix, groups)
+    *parts, ah, al = prepare(here, t_here, u, v, w, downstream_solver_matrix, groups)
     x = swapped(row_solve(here, parts, halos, ah, al, groups))
     x = swapped(column_solve(here, wall_segments, wallward_solver_matrices, x, nx // LANES))
     return place(x, t.shape)

time: 78.8 us -> 78.8 us (level)
  no operation moved by 1% of the time
where the time goes in v14:
time: 78.8 us; the launch traced here: 78.6 us
  blocking collectives  59 us (75%)
  starting transfers between devices  10.5 us (13%)
  Pallas kernels  8.99 us (11%)
    all_to_all x2, blocking collectives, swapped(): return lax.all_to_all(x, 'pencil', split_axis=0, concat_axis=0, tiled=True)  59 us
    ppermute x1, starting transfers between devices, on_device(): lax.ppermute(za, 'pencil', [(i, (i - 1 ^ 1) + 1) for i in range(1, groups...  4.27 us
    ppermute x1, starting transfers between devices, on_device(): yc = lax.ppermute(yc, 'slab', [(i, i ^ 1) for i in range(slabs)])  3.83 us
    pallas_call x1, Pallas kernels, prepare(): pl.pallas_call(functools.partial(prepare_kernel, groups), in_specs=[SMEM,...  3.03 us
    ppermute x1, starting transfers between devices, on_device(): lax.ppermute(yd, 'slab', [(i, (i - 1 ^ 1) + 1 & slabs - 1) for i in range...  2.29 us
    pallas_call x1, Pallas kernels, column_solve(): pl.pallas_call(functools.partial(column_kernel, blocks), in_specs=[SMEM,...  2.18 us
    pallas_call x1, Pallas kernels, row_solve(): pl.pallas_call(row_kernel, in_specs=[SMEM] + [VMEM] * 11, out_specs=VMEM,...  1.66 us
  transfers between devices with their start and end apart: 4, of which 0 were waited for; matrix products, arithmetic and copies ran while one was open for 0% of the time, Pallas kernels for 4%

profile of v14, /device:TPU:1, one launch (start us, length us, event | category | flops | bytes accessed | tf_op | source)
XLA Modules:
  0.0 78.6 jit_solution(15540462968015642485)
XLA Ops:
  0.0 1.2 %edges.1 = (f32[16,1024]{1,0:T(8,128)S(1)}, f32[16,1024]{1,0:T(8,128)S(1)}, f32[12,1024]{1,0:T(8,128)S(1)}, f32[12,1024]{1,0:T(8,128)S(1)}, f32[12,16,1024]{2,1,0:T(8,128)S(1)}) custom-call(s32[1]{0:T(128)} %bitcast.here_ref, f32[12,16,1024]{2,1,0:T(8,128)} %t_hbm.1), custom_call_target="tpu_custom_call" | custom-call | tf_op jit(solution)/shard_map/edges/pallas_call | solution.py:54
  1.2 3.8 %collective-permute-start = (f32[16,1024]{1,0:T(8,128)S(1)}, f32[16,1024]{1,0:T(8,128)S(1)}, u32[]{:S(2)}, u32[]{:S(2)}) collective-permute-start(f32[16,1024]{1,0:T(8,128)S(1)} %get-tuple-element.23), channel_id=1, source_target_pairs={{0,32},{32,0},{64,96},{96,64},{128,160},{160,128},{192,224},{224,1... | collective-permute-start | bytes 196616 | tf_op jit(solution)/shard_map/ppermute | solution.py:296
  5.0 2.3 %collective-permute-start.1 = (f32[16,1024]{1,0:T(8,128)S(1)}, f32[16,1024]{1,0:T(8,128)S(1)}, u32[]{:S(2)}, u32[]{:S(2)}) collective-permute-start(f32[16,1024]{1,0:T(8,128)S(1)} %get-tuple-element.24), channel_id=1, source_target_pairs={{0,224},{32,64},{64,32},{96,128},{128,96},{160,192},{192,160},{224... | collective-permute-start | bytes 196616 | tf_op jit(solution)/shard_map/ppermute | solution.py:297
  7.3 4.3 %collective-permute-start.2 = (f32[12,1024]{1,0:T(8,128)S(1)}, f32[12,1024]{1,0:T(8,128)S(1)}, u32[]{:S(2)}, u32[]{:S(2)}) collective-permute-start(f32[12,1024]{1,0:T(8,128)S(1)} %get-tuple-element.25), channel_id=1, source_target_pairs={{1,2},{2,1},{3,4},{4,3},{5,6},{6,5},{7,8},{8,7},{9,10},{10,9},{11,... | collective-permute-start | bytes 147464 | tf_op jit(solution)/shard_map/ppermute | solution.py:298
  11.6 0.1 collective-permute-start.3
  11.7 3.0 %prepare.1 = (f32[12,16,1024]{2,1,0:T(8,128)S(1)}, f32[16,1024]{1,0:T(8,128)S(1)}, f32[16,1024]{1,0:T(8,128)S(1)}, f32[12,1024]{1,0:T(8,128)S(1)}, f32[12,1024]{...) custom-call(s32[1]{0:T(128)} %bitcast.here_ref, ...), custom_call_target="tpu_custom_call" | custom-call | flops 12058624 | bytes 11141120 | tf_op jit(solution)/shard_map/prepare/pallas_call | solution.py:152
  14.7 0.0 collective-permute-done.2.za_ref
  14.8 0.0 collective-permute-done.3.zb_ref
  14.8 0.0 collective-permute-done.yc_ref
  14.8 0.0 collective-permute-done.1.yd_ref
  14.8 0.0 copy-start
  14.8 0.0 copy-start.1
  14.8 1.7 %row_solve.1 = f32[32,3,16,128]{3,2,1,0:T(8,128)S(1)} custom-call(s32[1]{0:T(128)} %bitcast.here_ref, f32[12,16,1024]{2,1,0:T(8,128)S(1)} %get-tuple-element.18.side_ref, f32[16,1024]{1,0:T(8,128)S(1)} %get-tuple-element.19.cb_ref, f32[16,1024]{1,0:T(8,128)S(1)} %get-tuple-element.20.ca_ref, f32[12,1024]{1,0:T(8,128)S(1)} %get-tuple-element.21.cl_ref, ...), custom_call_target="tpu_custom_call" | custom-call | flops 1207959552 | bytes 8388608 | tf_op jit(solution)/shard_map/row_solve/pallas_call | solution.py:210
  16.5 32.4 %all_to_all.10.x_ref = f32[32,3,16,128]{3,2,1,0:T(8,128)S(1)} all-to-all(f32[32,3,16,128]{3,2,1,0:T(8,128)S(1)} %row_solve.1), channel_id=1, replica_groups=mesh['slab'=8,'pencil'=32] {'pencil'}, dimensions={0} | all-to-all | bytes 1572864 | tf_op jit(solution)/shard_map/all_to_all | solution.py:288
  48.9 0.0 copy-done
  48.9 0.0 copy-done.1
  48.9 2.2 %column_solve.1 = f32[32,3,16,128]{3,2,1,0:T(8,128)S(1)} custom-call(s32[1]{0:T(128)} %bitcast.here_ref, s32[16]{0:T(128)S(1)} %copy-done.1, f32[2,512,512]{2,1,0:T(8,128)S(1)} %copy-done, f32[32,3,16,128]{3,2,1,0:T(8,128)S(1)} %all_to_all.10.x_ref), custom_call_target="tpu_custom_call" | custom-call | flops 1207959552 | bytes 4194304 | tf_op jit(solution)/shard_map/column_solve/pallas_call | solution.py:255
  51.1 26.6 %all_to_all.11.x_ref = f32[32,3,16,128]{3,2,1,0:T(8,128)S(1)} all-to-all(f32[32,3,16,128]{3,2,1,0:T(8,128)S(1)} %column_solve.1), channel_id=1, replica_groups=mesh['slab'=8,'pencil'=32] {'pencil'}, dimensions={0} | all-to-all | bytes 1572864 | tf_op jit(solution)/shard_map/all_to_all | solution.py:288
  77.7 0.9 %place.1 = f32[12,16,1024]{2,1,0:T(8,128)} custom-call(f32[32,3,16,128]{3,2,1,0:T(8,128)S(1)} %all_to_all.11.x_ref), custom_call_target="tpu_custom_call" | custom-call | tf_op jit(solution)/shard_map/place/pallas_call | solution.py:277
Async XLA Ops:
  1.2 13.6 %collective-permute-start = (f32[16,1024]{1,0:T(8,128)S(1)}, f32[16,1024]{1,0:T(8,128)S(1)}, u32[]{:S(2)}, u32[]{:S(2)}) collective-permute-start(f32[16,1024]{1,0:T(8,128)S(1)} %get-tuple-element.23), channel_id=1, source_target_pairs={{0,32},{32,0},{64,96},{96,64},{128,160},{160,128},{192,224},{224,1... | collective-permute-start | bytes 196616 | tf_op jit(solution)/shard_map/ppermute | solution.py:296
  5.0 9.7 %collective-permute-start.1 = (f32[16,1024]{1,0:T(8,128)S(1)}, f32[16,1024]{1,0:T(8,128)S(1)}, u32[]{:S(2)}, u32[]{:S(2)}) collective-permute-start(f32[16,1024]{1,0:T(8,128)S(1)} %get-tuple-element.24), channel_id=1, source_target_pairs={{0,224},{32,64},{64,32},{96,128},{128,96},{160,192},{192,160},{224... | collective-permute-start | bytes 196616 | tf_op jit(solution)/shard_map/ppermute | solution.py:297
  7.3 7.4 %collective-permute-start.2 = (f32[12,1024]{1,0:T(8,128)S(1)}, f32[12,1024]{1,0:T(8,128)S(1)}, u32[]{:S(2)}, u32[]{:S(2)}) collective-permute-start(f32[12,1024]{1,0:T(8,128)S(1)} %get-tuple-element.25), channel_id=1, source_target_pairs={{1,2},{2,1},{3,4},{4,3},{5,6},{6,5},{7,8},{8,7},{9,10},{10,9},{11,... | collective-permute-start | bytes 147464 | tf_op jit(solution)/shard_map/ppermute | solution.py:298
  11.6 3.2 %collective-permute-start.3 = (f32[12,1024]{1,0:T(8,128)S(1)}, f32[12,1024]{1,0:T(8,128)S(1)}, u32[]{:S(2)}, u32[]{:S(2)}) collective-permute-start(f32[12,1024]{1,0:T(8,128)S(1)} %get-tuple-element.26), channel_id=1, source_target_pairs={{0,1},{1,0},{2,3},{3,2},{4,5},{5,4},{6,7},{7,6},{8,9},{9,8},{10,11... | collective-permute-start | bytes 147464 | tf_op jit(solution)/shard_map/ppermute | solution.py:299
  14.8 34.1 %copy-start = (f32[2,512,512]{2,1,0:T(8,128)S(1)}, f32[2,512,512]{2,1,0:T(8,128)}, u32[]{:S(2)}) copy-start(f32[2,512,512]{2,1,0:T(8,128)} %w_ref.1) | copy-start | bytes 6291460
  14.8 34.1 %copy-start.1 = (s32[16]{0:T(128)S(1)}, s32[16]{0:T(128)}, u32[]{:S(2)}) copy-start(s32[16]{0:T(128)} %seg_ref.1) | copy-start | bytes 196

commit v15 on v14

--- a/solution.py
+++ b/solution.py
@@ -28,23 +28,18 @@
     return high, (wide - high.astype(jnp.float32)).astype(jnp.bfloat16)
 
 
-def edge_kernel(groups, here_ref, t_hbm, yc_ref, yd_ref, za_ref, zb_ref, buf, sems):
+def edge_kernel(groups, here_ref, t_hbm, yc_ref, yd_ref, za_ref, zb_ref, buf, sem):
     planes, rows, _ = t_hbm.shape
     pencil_even, slab_even = here_ref[0] % 2 == 0, here_ref[0] // groups % 2 == 0
-    copies = [
-        pltpu.make_async_copy(t_hbm, buf, sems.at[0]),
-        pltpu.make_async_copy(t_hbm.at[jnp.where(slab_even, planes - 1, 0)], yc_ref, sems.at[1]),
-        pltpu.make_async_copy(t_hbm.at[jnp.where(slab_even, 0, planes - 1)], yd_ref, sems.at[2]),
-    ]
-    for copy in copies:
-        copy.start()
-    copies[0].wait()
+    copy = pltpu.make_async_copy(t_hbm, buf, sem)
+    copy.start()
+    copy.wait()
+    yc_ref[...] = jnp.where(slab_even, buf[planes - 1], buf[0])
+    yd_ref[...] = jnp.where(slab_even, buf[0], buf[planes - 1])
     for y in range(planes):
         low, high = buf[y, :1, :], buf[y, rows - 1 :, :]
         za_ref[y : y + 1, :] = jnp.where(pencil_even, low, high)
         zb_ref[y : y + 1, :] = jnp.where(pencil_even, high, low)
-    copies[1].wait()
-    copies[2].wait()
 
 
 def edges(here, t, groups):
@@ -56,7 +51,7 @@
         in_specs=[SMEM, HBM],
         out_specs=[VMEM] * 5,
         out_shape=[plane, plane, level, level, jax.ShapeDtypeStruct(t.shape, t.dtype)],
-        scratch_shapes=[pltpu.SemaphoreType.DMA((3,))],
+        scratch_shapes=[pltpu.SemaphoreType.DMA],
         compiler_params=pltpu.CompilerParams(vmem_limit_bytes=8 * 2**20),
         name="edges",
     )(here, pinned(t))

time: 78.8 us -> 78.8 us (level)
  no operation moved by 1% of the time
where the time goes in v15:
time: 78.8 us; the launch traced here: 78.6 us
  blocking collectives  59 us (75%)
  starting transfers between devices  10.5 us (13%)
  Pallas kernels  8.98 us (11%)
    all_to_all x2, blocking collectives, swapped(): return lax.all_to_all(x, 'pencil', split_axis=0, concat_axis=0, tiled=True)  59 us
    ppermute x1, starting transfers between devices, on_device(): lax.ppermute(za, 'pencil', [(i, (i - 1 ^ 1) + 1) for i in range(1, groups...  4.27 us
    ppermute x1, starting transfers between devices, on_device(): yc = lax.ppermute(yc, 'slab', [(i, i ^ 1) for i in range(slabs)])  3.83 us
    pallas_call x1, Pallas kernels, prepare(): pl.pallas_call(functools.partial(prepare_kernel, groups), in_specs=[SMEM,...  3.03 us
    ppermute x1, starting transfers between devices, on_device(): lax.ppermute(yd, 'slab', [(i, (i - 1 ^ 1) + 1 & slabs - 1) for i in range...  2.29 us
    pallas_call x1, Pallas kernels, column_solve(): pl.pallas_call(functools.partial(column_kernel, blocks), in_specs=[SMEM,...  2.18 us
    pallas_call x1, Pallas kernels, row_solve(): pl.pallas_call(row_kernel, in_specs=[SMEM] + [VMEM] * 11, out_specs=VMEM,...  1.67 us
  transfers between devices with their start and end apart: 4, of which 0 were waited for; matrix products, arithmetic and copies ran while one was open for 0% of the time, Pallas kernels for 4%

profile of v15, /device:TPU:1, one launch (start us, length us, event | category | flops | bytes accessed | tf_op | source)
XLA Modules:
  0.0 78.6 jit_solution(16332491841895748719)
XLA Ops:
  0.0 1.2 %edges.1 = (f32[16,1024]{1,0:T(8,128)S(1)}, f32[16,1024]{1,0:T(8,128)S(1)}, f32[12,1024]{1,0:T(8,128)S(1)}, f32[12,1024]{1,0:T(8,128)S(1)}, f32[12,16,1024]{2,1,0:T(8,128)S(1)}) custom-call(s32[1]{0:T(128)} %bitcast.here_ref, f32[12,16,1024]{2,1,0:T(8,128)} %t_hbm.1), custom_call_target="tpu_custom_call" | custom-call | tf_op jit(solution)/shard_map/edges/pallas_call | solution.py:49
  1.2 3.8 %collective-permute-start = (f32[16,1024]{1,0:T(8,128)S(1)}, f32[16,1024]{1,0:T(8,128)S(1)}, u32[]{:S(2)}, u32[]{:S(2)}) collective-permute-start(f32[16,1024]{1,0:T(8,128)S(1)} %get-tuple-element.23), channel_id=1, source_target_pairs={{0,32},{32,0},{64,96},{96,64},{128,160},{160,128},{192,224},{224,1... | collective-permute-start | bytes 196616 | tf_op jit(solution)/shard_map/ppermute | solution.py:291
  5.0 2.3 %collective-permute-start.1 = (f32[16,1024]{1,0:T(8,128)S(1)}, f32[16,1024]{1,0:T(8,128)S(1)}, u32[]{:S(2)}, u32[]{:S(2)}) collective-permute-start(f32[16,1024]{1,0:T(8,128)S(1)} %get-tuple-element.24), channel_id=1, source_target_pairs={{0,224},{32,64},{64,32},{96,128},{128,96},{160,192},{192,160},{224... | collective-permute-start | bytes 196616 | tf_op jit(solution)/shard_map/ppermute | solution.py:292
  7.3 4.3 %collective-permute-start.2 = (f32[12,1024]{1,0:T(8,128)S(1)}, f32[12,1024]{1,0:T(8,128)S(1)}, u32[]{:S(2)}, u32[]{:S(2)}) collective-permute-start(f32[12,1024]{1,0:T(8,128)S(1)} %get-tuple-element.25), channel_id=1, source_target_pairs={{1,2},{2,1},{3,4},{4,3},{5,6},{6,5},{7,8},{8,7},{9,10},{10,9},{11,... | collective-permute-start | bytes 147464 | tf_op jit(solution)/shard_map/ppermute | solution.py:293
  11.6 0.1 collective-permute-start.3
  11.7 3.0 %prepare.1 = (f32[12,16,1024]{2,1,0:T(8,128)S(1)}, f32[16,1024]{1,0:T(8,128)S(1)}, f32[16,1024]{1,0:T(8,128)S(1)}, f32[12,1024]{1,0:T(8,128)S(1)}, f32[12,1024]{...) custom-call(s32[1]{0:T(128)} %bitcast.here_ref, ...), custom_call_target="tpu_custom_call" | custom-call | flops 12058624 | bytes 11141120 | tf_op jit(solution)/shard_map/prepare/pallas_call | solution.py:147
  14.7 0.0 collective-permute-done.2.za_ref
  14.7 0.0 collective-permute-done.3.zb_ref
  14.7 0.0 collective-permute-done.yc_ref
  14.8 0.0 collective-permute-done.1.yd_ref
  14.8 0.0 copy-start
  14.8 0.0 copy-start.1
  14.8 1.7 %row_solve.1 = f32[32,3,16,128]{3,2,1,0:T(8,128)S(1)} custom-call(s32[1]{0:T(128)} %bitcast.here_ref, f32[12,16,1024]{2,1,0:T(8,128)S(1)} %get-tuple-element.18.side_ref, f32[16,1024]{1,0:T(8,128)S(1)} %get-tuple-element.19.cb_ref, f32[16,1024]{1,0:T(8,128)S(1)} %get-tuple-element.20.ca_ref, f32[12,1024]{1,0:T(8,128)S(1)} %get-tuple-element.21.cl_ref, ...), custom_call_target="tpu_custom_call" | custom-call | flops 1207959552 | bytes 8388608 | tf_op jit(solution)/shard_map/row_solve/pallas_call | solution.py:205
  16.5 32.4 %all_to_all.10.x_ref = f32[32,3,16,128]{3,2,1,0:T(8,128)S(1)} all-to-all(f32[32,3,16,128]{3,2,1,0:T(8,128)S(1)} %row_solve.1), channel_id=1, replica_groups=mesh['slab'=8,'pencil'=32] {'pencil'}, dimensions={0} | all-to-all | bytes 1572864 | tf_op jit(solution)/shard_map/all_to_all | solution.py:283
  48.9 0.0 copy-done
  48.9 0.0 copy-done.1
  48.9 2.2 %column_solve.1 = f32[32,3,16,128]{3,2,1,0:T(8,128)S(1)} custom-call(s32[1]{0:T(128)} %bitcast.here_ref, s32[16]{0:T(128)S(1)} %copy-done.1, f32[2,512,512]{2,1,0:T(8,128)S(1)} %copy-done, f32[32,3,16,128]{3,2,1,0:T(8,128)S(1)} %all_to_all.10.x_ref), custom_call_target="tpu_custom_call" | custom-call | flops 1207959552 | bytes 4194304 | tf_op jit(solution)/shard_map/column_solve/pallas_call | solution.py:250
  51.1 26.6 %all_to_all.11.x_ref = f32[32,3,16,128]{3,2,1,0:T(8,128)S(1)} all-to-all(f32[32,3,16,128]{3,2,1,0:T(8,128)S(1)} %column_solve.1), channel_id=1, replica_groups=mesh['slab'=8,'pencil'=32] {'pencil'}, dimensions={0} | all-to-all | bytes 1572864 | tf_op jit(solution)/shard_map/all_to_all | solution.py:283
  77.7 0.9 %place.1 = f32[12,16,1024]{2,1,0:T(8,128)} custom-call(f32[32,3,16,128]{3,2,1,0:T(8,128)S(1)} %all_to_all.11.x_ref), custom_call_target="tpu_custom_call" | custom-call | tf_op jit(solution)/shard_map/place/pallas_call | solution.py:272
Async XLA Ops:
  1.2 13.6 %collective-permute-start = (f32[16,1024]{1,0:T(8,128)S(1)}, f32[16,1024]{1,0:T(8,128)S(1)}, u32[]{:S(2)}, u32[]{:S(2)}) collective-permute-start(f32[16,1024]{1,0:T(8,128)S(1)} %get-tuple-element.23), channel_id=1, source_target_pairs={{0,32},{32,0},{64,96},{96,64},{128,160},{160,128},{192,224},{224,1... | collective-permute-start | bytes 196616 | tf_op jit(solution)/shard_map/ppermute | solution.py:291
  5.0 9.7 %collective-permute-start.1 = (f32[16,1024]{1,0:T(8,128)S(1)}, f32[16,1024]{1,0:T(8,128)S(1)}, u32[]{:S(2)}, u32[]{:S(2)}) collective-permute-start(f32[16,1024]{1,0:T(8,128)S(1)} %get-tuple-element.24), channel_id=1, source_target_pairs={{0,224},{32,64},{64,32},{96,128},{128,96},{160,192},{192,160},{224... | collective-permute-start | bytes 196616 | tf_op jit(solution)/shard_map/ppermute | solution.py:292
  7.3 7.4 %collective-permute-start.2 = (f32[12,1024]{1,0:T(8,128)S(1)}, f32[12,1024]{1,0:T(8,128)S(1)}, u32[]{:S(2)}, u32[]{:S(2)}) collective-permute-start(f32[12,1024]{1,0:T(8,128)S(1)} %get-tuple-element.25), channel_id=1, source_target_pairs={{1,2},{2,1},{3,4},{4,3},{5,6},{6,5},{7,8},{8,7},{9,10},{10,9},{11,... | collective-permute-start | bytes 147464 | tf_op jit(solution)/shard_map/ppermute | solution.py:293
  11.6 3.2 %collective-permute-start.3 = (f32[12,1024]{1,0:T(8,128)S(1)}, f32[12,1024]{1,0:T(8,128)S(1)}, u32[]{:S(2)}, u32[]{:S(2)}) collective-permute-start(f32[12,1024]{1,0:T(8,128)S(1)} %get-tuple-element.26), channel_id=1, source_target_pairs={{0,1},{1,0},{2,3},{3,2},{4,5},{5,4},{6,7},{7,6},{8,9},{9,8},{10,11... | collective-permute-start | bytes 147464 | tf_op jit(solution)/shard_map/ppermute | solution.py:294
  14.8 34.1 %copy-start = (f32[2,512,512]{2,1,0:T(8,128)S(1)}, f32[2,512,512]{2,1,0:T(8,128)}, u32[]{:S(2)}) copy-start(f32[2,512,512]{2,1,0:T(8,128)} %w_ref.1) | copy-start | bytes 6291460
  14.8 34.1 %copy-start.1 = (s32[16]{0:T(128)S(1)}, s32[16]{0:T(128)}, u32[]{:S(2)}) copy-start(s32[16]{0:T(128)} %seg_ref.1) | copy-start | bytes 196

commit v16 on v14

--- a/solution.py
+++ b/solution.py
@@ -148,7 +148,7 @@
     a16 = jax.ShapeDtypeStruct(a.shape, jnp.bfloat16)
     plane = jax.ShapeDtypeStruct((rows, nx), t.dtype)
     level = jax.ShapeDtypeStruct((planes, nx), t.dtype)
-    parts = 4
+    parts = 2
     return pl.pallas_call(
         functools.partial(prepare_kernel, groups),
         in_specs=[SMEM, VMEM] + [HBM] * 4,

time: 78.8 us -> 78.8 us (level)
  no operation moved by 1% of the time
where the time goes in v16:
time: 78.8 us; the launch traced here: 78.6 us
  blocking collectives  59.1 us (75%)
  starting transfers between devices  10.5 us (13%)
  Pallas kernels  8.92 us (11%)
    all_to_all x2, blocking collectives, swapped(): return lax.all_to_all(x, 'pencil', split_axis=0, concat_axis=0, tiled=True)  59.1 us
    ppermute x1, starting transfers between devices, on_device(): lax.ppermute(za, 'pencil', [(i, (i - 1 ^ 1) + 1) for i in range(1, groups...  4.27 us
    ppermute x1, starting transfers between devices, on_device(): yc = lax.ppermute(yc, 'slab', [(i, i ^ 1) for i in range(slabs)])  3.83 us
    pallas_call x1, Pallas kernels, prepare(): pl.pallas_call(functools.partial(prepare_kernel, groups), in_specs=[SMEM,...  2.95 us
    ppermute x1, starting transfers between devices, on_device(): lax.ppermute(yd, 'slab', [(i, (i - 1 ^ 1) + 1 & slabs - 1) for i in range...  2.29 us
    pallas_call x1, Pallas kernels, column_solve(): pl.pallas_call(functools.partial(column_kernel, blocks), in_specs=[SMEM,...  2.18 us
    pallas_call x1, Pallas kernels, row_solve(): pl.pallas_call(row_kernel, in_specs=[SMEM] + [VMEM] * 11, out_specs=VMEM,...  1.67 us
  transfers between devices with their start and end apart: 4, of which 0 were waited for; matrix products, arithmetic and copies ran while one was open for 0% of the time, Pallas kernels for 4%

profile of v16, /device:TPU:1, one launch (start us, length us, event | category | flops | bytes accessed | tf_op | source)
XLA Modules:
  0.0 78.6 jit_solution(4581082083560349961)
XLA Ops:
  0.0 1.2 %edges.1 = (f32[16,1024]{1,0:T(8,128)S(1)}, f32[16,1024]{1,0:T(8,128)S(1)}, f32[12,1024]{1,0:T(8,128)S(1)}, f32[12,1024]{1,0:T(8,128)S(1)}, f32[12,16,1024]{2,1,0:T(8,128)S(1)}) custom-call(s32[1]{0:T(128)} %bitcast.here_ref, f32[12,16,1024]{2,1,0:T(8,128)} %t_hbm.1), custom_call_target="tpu_custom_call" | custom-call | tf_op jit(solution)/shard_map/edges/pallas_call | solution.py:54
  1.2 3.8 %collective-permute-start = (f32[16,1024]{1,0:T(8,128)S(1)}, f32[16,1024]{1,0:T(8,128)S(1)}, u32[]{:S(2)}, u32[]{:S(2)}) collective-permute-start(f32[16,1024]{1,0:T(8,128)S(1)} %get-tuple-element.23), channel_id=1, source_target_pairs={{0,32},{32,0},{64,96},{96,64},{128,160},{160,128},{192,224},{224,1... | collective-permute-start | bytes 196616 | tf_op jit(solution)/shard_map/ppermute | solution.py:296
  5.0 2.3 %collective-permute-start.1 = (f32[16,1024]{1,0:T(8,128)S(1)}, f32[16,1024]{1,0:T(8,128)S(1)}, u32[]{:S(2)}, u32[]{:S(2)}) collective-permute-start(f32[16,1024]{1,0:T(8,128)S(1)} %get-tuple-element.24), channel_id=1, source_target_pairs={{0,224},{32,64},{64,32},{96,128},{128,96},{160,192},{192,160},{224... | collective-permute-start | bytes 196616 | tf_op jit(solution)/shard_map/ppermute | solution.py:297
  7.3 4.3 %collective-permute-start.2 = (f32[12,1024]{1,0:T(8,128)S(1)}, f32[12,1024]{1,0:T(8,128)S(1)}, u32[]{:S(2)}, u32[]{:S(2)}) collective-permute-start(f32[12,1024]{1,0:T(8,128)S(1)} %get-tuple-element.25), channel_id=1, source_target_pairs={{1,2},{2,1},{3,4},{4,3},{5,6},{6,5},{7,8},{8,7},{9,10},{10,9},{11,... | collective-permute-start | bytes 147464 | tf_op jit(solution)/shard_map/ppermute | solution.py:298
  11.6 0.1 collective-permute-start.3
  11.7 3.0 %prepare.1 = (f32[12,16,1024]{2,1,0:T(8,128)S(1)}, f32[16,1024]{1,0:T(8,128)S(1)}, f32[16,1024]{1,0:T(8,128)S(1)}, f32[12,1024]{1,0:T(8,128)S(1)}, f32[12,1024]{...) custom-call(s32[1]{0:T(128)} %bitcast.here_ref, ...), custom_call_target="tpu_custom_call" | custom-call | flops 12058624 | bytes 11141120 | tf_op jit(solution)/shard_map/prepare/pallas_call | solution.py:152
  14.7 0.0 collective-permute-done.2.za_ref
  14.7 0.0 collective-permute-done.3.zb_ref
  14.7 0.0 collective-permute-done.yc_ref
  14.7 0.0 collective-permute-done.1.yd_ref
  14.7 0.0 copy-start
  14.7 0.0 copy-start.1
  14.7 1.7 %row_solve.1 = f32[32,3,16,128]{3,2,1,0:T(8,128)S(1)} custom-call(s32[1]{0:T(128)} %bitcast.here_ref, f32[12,16,1024]{2,1,0:T(8,128)S(1)} %get-tuple-element.18.side_ref, f32[16,1024]{1,0:T(8,128)S(1)} %get-tuple-element.19.cb_ref, f32[16,1024]{1,0:T(8,128)S(1)} %get-tuple-element.20.ca_ref, f32[12,1024]{1,0:T(8,128)S(1)} %get-tuple-element.21.cl_ref, ...), custom_call_target="tpu_custom_call" | custom-call | flops 1207959552 | bytes 8388608 | tf_op jit(solution)/shard_map/row_solve/pallas_call | solution.py:210
  16.4 32.5 %all_to_all.10.x_ref = f32[32,3,16,128]{3,2,1,0:T(8,128)S(1)} all-to-all(f32[32,3,16,128]{3,2,1,0:T(8,128)S(1)} %row_solve.1), channel_id=1, replica_groups=mesh['slab'=8,'pencil'=32] {'pencil'}, dimensions={0} | all-to-all | bytes 1572864 | tf_op jit(solution)/shard_map/all_to_all | solution.py:288
  48.9 0.0 copy-done
  48.9 0.0 copy-done.1
  48.9 2.2 %column_solve.1 = f32[32,3,16,128]{3,2,1,0:T(8,128)S(1)} custom-call(s32[1]{0:T(128)} %bitcast.here_ref, s32[16]{0:T(128)S(1)} %copy-done.1, f32[2,512,512]{2,1,0:T(8,128)S(1)} %copy-done, f32[32,3,16,128]{3,2,1,0:T(8,128)S(1)} %all_to_all.10.x_ref), custom_call_target="tpu_custom_call" | custom-call | flops 1207959552 | bytes 4194304 | tf_op jit(solution)/shard_map/column_solve/pallas_call | solution.py:255
  51.1 26.6 %all_to_all.11.x_ref = f32[32,3,16,128]{3,2,1,0:T(8,128)S(1)} all-to-all(f32[32,3,16,128]{3,2,1,0:T(8,128)S(1)} %column_solve.1), channel_id=1, replica_groups=mesh['slab'=8,'pencil'=32] {'pencil'}, dimensions={0} | all-to-all | bytes 1572864 | tf_op jit(solution)/shard_map/all_to_all | solution.py:288
  77.7 0.9 %place.1 = f32[12,16,1024]{2,1,0:T(8,128)} custom-call(f32[32,3,16,128]{3,2,1,0:T(8,128)S(1)} %all_to_all.11.x_ref), custom_call_target="tpu_custom_call" | custom-call | tf_op jit(solution)/shard_map/place/pallas_call | solution.py:277
Async XLA Ops:
  1.2 13.5 %collective-permute-start = (f32[16,1024]{1,0:T(8,128)S(1)}, f32[16,1024]{1,0:T(8,128)S(1)}, u32[]{:S(2)}, u32[]{:S(2)}) collective-permute-start(f32[16,1024]{1,0:T(8,128)S(1)} %get-tuple-element.23), channel_id=1, source_target_pairs={{0,32},{32,0},{64,96},{96,64},{128,160},{160,128},{192,224},{224,1... | collective-permute-start | bytes 196616 | tf_op jit(solution)/shard_map/ppermute | solution.py:296
  5.0 9.7 %collective-permute-start.1 = (f32[16,1024]{1,0:T(8,128)S(1)}, f32[16,1024]{1,0:T(8,128)S(1)}, u32[]{:S(2)}, u32[]{:S(2)}) collective-permute-start(f32[16,1024]{1,0:T(8,128)S(1)} %get-tuple-element.24), channel_id=1, source_target_pairs={{0,224},{32,64},{64,32},{96,128},{128,96},{160,192},{192,160},{224... | collective-permute-start | bytes 196616 | tf_op jit(solution)/shard_map/ppermute | solution.py:297
  7.3 7.3 %collective-permute-start.2 = (f32[12,1024]{1,0:T(8,128)S(1)}, f32[12,1024]{1,0:T(8,128)S(1)}, u32[]{:S(2)}, u32[]{:S(2)}) collective-permute-start(f32[12,1024]{1,0:T(8,128)S(1)} %get-tuple-element.25), channel_id=1, source_target_pairs={{1,2},{2,1},{3,4},{4,3},{5,6},{6,5},{7,8},{8,7},{9,10},{10,9},{11,... | collective-permute-start | bytes 147464 | tf_op jit(solution)/shard_map/ppermute | solution.py:298
  11.6 3.1 %collective-permute-start.3 = (f32[12,1024]{1,0:T(8,128)S(1)}, f32[12,1024]{1,0:T(8,128)S(1)}, u32[]{:S(2)}, u32[]{:S(2)}) collective-permute-start(f32[12,1024]{1,0:T(8,128)S(1)} %get-tuple-element.26), channel_id=1, source_target_pairs={{0,1},{1,0},{2,3},{3,2},{4,5},{5,4},{6,7},{7,6},{8,9},{9,8},{10,11... | collective-permute-start | bytes 147464 | tf_op jit(solution)/shard_map/ppermute | solution.py:299
  14.7 34.2 %copy-start = (f32[2,512,512]{2,1,0:T(8,128)S(1)}, f32[2,512,512]{2,1,0:T(8,128)}, u32[]{:S(2)}) copy-start(f32[2,512,512]{2,1,0:T(8,128)} %w_ref.1) | copy-start | bytes 6291460
  14.7 34.2 %copy-start.1 = (s32[16]{0:T(128)S(1)}, s32[16]{0:T(128)}, u32[]{:S(2)}) copy-start(s32[16]{0:T(128)} %seg_ref.1) | copy-start | bytes 196
